TPU v7x, 32 devices: a whole 2x2x4 slice. The times are simulated.
32 devices in a mesh: gx: 4 (over x, core), gy: 8 (over z, y).
Axes of the slice: x: 2, y: 2, z: 4, core: 2. Of those that a mesh axis runs over, the one named last changes fastest.
Arguments:
- atom_feat: bfloat16 [4, 8, 32, 64], P('gx', 'gy'), may hold values from -6 to 6
- bond_feat: bfloat16 [4, 8, 32, 1024], P('gx', 'gy'), may hold values from -6 to 6
- neighbours: int32 [4, 8, 32, 16], P('gx', 'gy'), may hold values from 0 to 1023, as said below
- bond_dirs: float32 [2, 4, 8, 512], P(None, 'gx', 'gy'), may hold values from -3.140625 to 3.140625
- bond_in_weight: bfloat16 [192, 128], replicated, may hold values from -0.4375 to 0.4375
- bond_mix_weight: bfloat16 [64, 64], replicated, may hold values from -0.75 to 0.75
- pair_weight: bfloat16 [64, 256], replicated, may hold values from -0.75 to 0.75
- angle_weight: bfloat16 [64, 128], replicated, may hold values from -0.75 to 0.75
- pair_hidden_weight: bfloat16 [64, 128], replicated, may hold values from -0.75 to 0.75
- pair_out_weight: bfloat16 [64, 64], replicated, may hold values from -0.1875 to 0.1875
- atom_in_weight: bfloat16 [128, 128], replicated, may hold values from -0.5 to 0.5
- atom_out_weight: bfloat16 [64, 64], replicated, may hold values from -0.75 to 0.75
Outputs:
- atom_out: bfloat16 [4, 8, 32, 64], P('gx', 'gy')
- bond_out: bfloat16 [4, 8, 32, 1024], P('gx', 'gy')
Inputs may be any that keep to these rules, and one draw needn't show every extreme that they name: Atom neighbours[i, p] lies in atom i's block or in one of the eight blocks next to it along gx and gy, wrapping round at the ends; atom neighbours[i, p] has atom i at slot 15 - p. Every block has the same numbers of bonds pointing into each of these nine blocks, at most 64, and exactly 64 into itself.
All inputs are finite; a program needn't handle non-finite values.
Results may differ from a plain program's by a relative error of at most 0.008.
Values may be sent and summed in bfloat16 or wider, within the bound.
No kernel may reach another device: no remote copies, remote signals or barrier semaphores. Data moves between devices by JAX's collectives and lax.ppermute only.
A program may use at most 64 MiB of HBM per device.

v0:
```python
import functools

import jax
import jax.numpy as jnp
from jax import lax
from jax.experimental import pallas as pl
from jax.experimental.pallas import tpu as pltpu
from jax.sharding import PartitionSpec as P

F32 = jnp.float32
BF16 = jnp.bfloat16
CAP = 64


def quotient(values, size):
    if size & (size - 1) == 0:
        return values >> (size.bit_length() - 1)
    return lax.div(values, jnp.int32(size))


def remainder(values, size):
    if size & (size - 1) == 0:
        return values & (size - 1)
    return lax.rem(values, jnp.int32(size))


def step_code(owner, home, extent, paired, receives):
    step = remainder(owner - home + 1 + extent, extent)
    if paired:
        ahead = jnp.where(remainder(home, 2) == 0, 0, 2)
    else:
        ahead = 0 if receives else 2
    return jnp.where(step == 1, 0, jnp.where(step == ahead, 1, 2))


def moves(extent, paired):
    if paired:
        near = [(i, i ^ 1) for i in range(extent)]
        return [(i, (((i + 1) ^ 1) - 1) % extent) for i in range(extent)], near
    up = [(i, (i + 1) % extent) for i in range(extent)]
    return up, [(j, i) for i, j in up]


def slot_at(position, slots):
    half = slots // 2
    return jnp.where(position < half, 2 * position, 2 * (position - half) + 1)


def bond_row(table):
    slots, atoms = table.shape
    per_group = 128 // atoms
    tiled = jnp.concatenate([table.astype(F32)] * per_group, axis=1)
    row = lax.broadcasted_iota(jnp.int32, tiled.shape, 0)
    position = quotient(lax.broadcasted_iota(jnp.int32, tiled.shape, 1), atoms)
    pieces = []
    for group in range(slots // per_group):
        chosen = row == slot_at(position + group * per_group, slots)
        pieces.append(jnp.sum(jnp.where(chosen, tiled, 0.0), axis=0, keepdims=True))
    return jnp.concatenate(pieces, axis=1).astype(jnp.int32)


def bond_codes(targets, atoms, extents, paired, receives):
    owner = quotient(targets, atoms)
    block = (quotient(owner, extents[1]), remainder(owner, extents[1]))
    return tuple(
        step_code(block[k], lax.axis_index(axis), extents[k], paired[k], receives)
        for k, axis in enumerate(("gx", "gy"))
    )


def left_lanes(shape):
    return lax.broadcasted_iota(jnp.int32, shape, 1) < shape[1] // 2


def swapped(rows):
    half = rows.shape[1] // 2
    return jnp.concatenate([rows[:, half:], rows[:, :half]], axis=1)


def blocks_of(bond_ref, pairs):
    width = bond_ref.shape[3] // pairs
    return [bond_ref[0, 0, :, k * width : (k + 1) * width] for k in range(pairs)]


def pack_kernel(
    extents,
    paired,
    targets_hbm,
    atom_hbm,
    bond_hbm,
    own_ref,
    one_ref,
    two_ref,
    targets_ref,
    atom_ref,
    bond_ref,
    sems,
):
    sources = ((targets_hbm, targets_ref), (bond_hbm, bond_ref), (atom_hbm, atom_ref))
    copies = [
        pltpu.make_async_copy(source, target, sems.at[k])
        for k, (source, target) in enumerate(sources)
    ]
    for copy in copies:
        copy.start()
    atoms, feature = atom_ref.shape[2], atom_ref.shape[3]
    slots = targets_ref.shape[0]
    bonds = slots * atoms
    lanes = 128
    groups = bonds // lanes
    copies[0].wait()
    code_x, code_y = bond_codes(bond_row(targets_ref[...]), atoms, extents, paired, False)
    code = 3 * code_x + code_y
    rows = lax.broadcasted_iota(jnp.int32, (16, lanes), 0)
    marks = [rows == code[:, g * lanes : (g + 1) * lanes] for g in range(groups)]
    stacked = jnp.concatenate([m.astype(F32) for m in marks], axis=0).astype(BF16)
    before = lax.broadcasted_iota(jnp.int32, (lanes, 2 * lanes), 0)
    after = lax.broadcasted_iota(jnp.int32, (lanes, 2 * lanes), 1)
    sums = jnp.where((before < after) | (after >= lanes), 1.0, 0.0).astype(BF16)
    counted = jnp.dot(stacked, sums, preferred_element_type=F32)
    place = []
    earlier = jnp.zeros((16, lanes), F32)
    for g in range(groups):
        part = counted[g * 16 : (g + 1) * 16]
        place.append(
            jnp.sum(jnp.where(marks[g], part[:, :lanes] + earlier, 0.0), axis=0, keepdims=True)
        )
        earlier = earlier + part[:, lanes:]
    place = jnp.concatenate(place, axis=1).astype(jnp.int32)
    half = CAP // 2
    right = quotient(place, half)
    wanted = 9 * half * right + place - half * right + half * code
    spot = lax.broadcasted_iota(jnp.int32, (9 * CAP, bonds), 0)
    chosen = jnp.where(spot == wanted, 1.0, 0.0).astype(BF16)
    copies[1].wait()
    blocks = blocks_of(bond_ref, slots // 2)
    values = [jnp.concatenate([x[:, :feature]] * 2, axis=1) for x in blocks]
    values += [jnp.concatenate([x[:, feature:]] * 2, axis=1) for x in blocks]
    packed = jnp.dot(chosen, jnp.concatenate(values, axis=0), preferred_element_type=F32)
    packed = jnp.where(
        left_lanes((9 * half, 2 * feature)), packed[: 9 * half], packed[9 * half :]
    ).astype(BF16)
    copies[2].wait()
    atom = atom_ref[0, 0]
    atom = jnp.concatenate([atom[: atoms // 2], atom[atoms // 2 :]], axis=1)
    for third, ref in enumerate((own_ref, one_ref, two_ref)):
        ref[: 3 * half] = packed[3 * half * third : 3 * half * (third + 1)]
        ref[3 * half :] = atom


def crossed(left, right):
    half = left.shape[1] // 2
    parts = [left[:, :half], right[:, :half], left[:, half:], right[:, half:]]
    return jnp.concatenate(parts, axis=1)


def two_blocks(weight):
    blank = jnp.zeros_like(weight)
    return jnp.concatenate([crossed(weight, blank), crossed(blank, weight)], axis=0)


def diagonal_blocks(weight):
    blank = jnp.zeros_like(weight)
    return jnp.concatenate(
        [jnp.concatenate([weight, blank], axis=1), jnp.concatenate([blank, weight], axis=1)],
        axis=0,
    )


def angular_kernel(atoms, dirs_ref, angle_ref, angular_ref):
    slots, pairs, _ = angular_ref.shape
    bonds = 2 * pairs
    degrees = angle_ref.shape[0]
    weight = (two_blocks(angle_ref[...].astype(F32)) * 0.5).astype(BF16)
    polar, azimuth = dirs_ref[0, 0], dirs_ref[1, 0]
    unit = jnp.concatenate(
        [
            jnp.sin(polar) * jnp.cos(azimuth),
            jnp.sin(polar) * jnp.sin(azimuth),
            jnp.cos(polar),
            jnp.zeros((5, bonds), F32),
        ],
        axis=0,
    )
    high = unit.astype(BF16).astype(F32)
    middle = (unit - high).astype(BF16).astype(F32)
    parts = jnp.concatenate([high, middle, unit - high - middle], axis=0).astype(BF16)
    bond = lax.broadcasted_iota(jnp.int32, (1, bonds), 1)
    source = remainder(bond, atoms) * slots + slot_at(quotient(bond, atoms), slots)
    spot = lax.broadcasted_iota(jnp.int32, (bonds, bonds), 0)
    chosen = jnp.where(spot == source, 1.0, 0.0).astype(BF16)
    unit = jnp.dot(parts, chosen, preferred_element_type=F32)
    unit = unit[0:8] + unit[8:16] + unit[16:24]
    even = [jnp.broadcast_to(unit[k : k + 1, :pairs], (8, pairs)) for k in range(3)]
    odd = [jnp.broadcast_to(unit[k : k + 1, pairs:], (8, pairs)) for k in range(3)]
    row = lax.broadcasted_iota(jnp.int32, (8, pairs), 0)

    def turned(vector, places):
        places = places % (pairs // atoms)
        if places == 0:
            return vector
        return [pltpu.roll(part, pairs - atoms * places, 1) for part in vector]

    def basis(first, second):
        cosine = first[0] * second[0] + first[1] * second[1] + first[2] * second[2]
        series = [jnp.ones_like(cosine), cosine]
        double = cosine + cosine
        for _ in range(7):
            series.append(double * series[-1] - series[-2])
        lower = series[7]
        upper = series[1]
        for index in range(1, 8):
            lower = jnp.where(row == index, series[7 - index], lower)
            upper = jnp.where(row == index, series[1 + index], upper)
        double = series[8] + series[8]
        blocks = [lower, upper]
        for _ in range(degrees // 8 - 1):
            blocks.append(double * blocks[-1] - blocks[-2])
        return blocks[1:]

    for diagonal in range(slots):
        places = diagonal // 2
        if diagonal % 2 == 0:
            blocks = basis(even, turned(even, places)) + basis(odd, turned(odd, places))
        else:
            blocks = basis(even, turned(odd, places)) + basis(odd, turned(even, places + 1))
        series = jnp.concatenate(blocks, axis=0).T.astype(BF16)
        angular_ref[diagonal] = jnp.dot(series, weight, preferred_element_type=F32)


def prepare_kernel(
    extents,
    paired,
    targets_ref,
    atom_ref,
    bond_ref,
    *refs,
):
    sources, results, held, sems = refs[:9], refs[9:21], refs[21:28], refs[28]
    chosen_ref, own_ref, near_ref, far_weight_ref, mix_weight_ref, pair_weight_ref = results[:6]
    hidden_weight_ref, out_weight_ref, atom_in_weight_ref, atom_out_weight_ref = results[6:10]
    bond_in_ref, bond_mix_ref, pair_ref, pair_hidden_ref, pair_out_ref = held[:5]
    atom_in_ref, atom_out_ref = held[5:]
    copies = [
        pltpu.make_async_copy(source, target, sems.at[k])
        for k, (source, target) in enumerate(zip(sources, held + results[10:]))
    ]
    for copy in copies:
        copy.start()
    atoms, feature = atom_ref.shape[2], atom_ref.shape[3]
    slots = targets_ref.shape[0]
    bonds = slots * atoms
    targets = bond_row(targets_ref[...])
    code_x, code_y = bond_codes(targets, atoms, extents, paired, True)
    code = 3 * code_y + code_x
    bond = lax.broadcasted_iota(jnp.int32, (1, bonds), 1)
    far_slot = slots - 1 - slot_at(quotient(bond, atoms), slots)
    far_atom = remainder(targets, atoms)
    far = (remainder(far_slot, 2) * (slots // 2) + quotient(far_slot, 2)) * atoms + far_atom
    base = (code * bonds).astype(F32)
    key = base + far.astype(F32)

    def column(values):
        return jnp.broadcast_to(values.astype(F32), (128, bonds)).T

    keys = column(key)
    place = []
    for group in range(bonds // 128):
        here = slice(group * 128, (group + 1) * 128)
        inside = (keys < key[:, here]) & (keys >= base[:, here])
        place.append(jnp.sum(jnp.where(inside, 1.0, 0.0), axis=0, keepdims=True))
    place = jnp.concatenate(place, axis=1).astype(jnp.int32)
    half, tall = CAP // 2, atoms // 2
    bond_spot = 9 * half * quotient(place, half) + half * code + remainder(place, half)
    atom_spot = 9 * CAP + 9 * tall * quotient(far_atom, tall) + tall * code
    atom_spot = column(atom_spot + remainder(far_atom, tall))
    bond_spot = column(bond_spot)
    total = 9 * CAP + 9 * atoms
    for start in range(0, total, 128):
        width = min(128, total - start)
        spot = lax.broadcasted_iota(jnp.int32, (bonds, 128), 1).astype(F32) + float(start)
        chosen = jnp.where((spot == bond_spot) | (spot == atom_spot), 1.0, 0.0).astype(BF16)
        chosen_ref[:, start : start + width] = chosen[:, :width]

    atom = atom_ref[0, 0]
    blocks = blocks_of(bond_ref, slots // 2)
    own = [jnp.concatenate([atom, x[:, :feature]], axis=1) for x in blocks]
    own += [jnp.concatenate([atom, x[:, feature:]], axis=1) for x in blocks]
    own = jnp.concatenate(own, axis=0)
    own_ref[...] = own

    for copy in copies:
        copy.wait()
    weight = bond_in_ref[...].astype(F32)
    source, other, bond_part = (weight[k * feature : (k + 1) * feature] for k in range(3))
    blank = jnp.zeros_like(source)
    near = [crossed(other, source), crossed(blank, bond_part)]
    near = (jnp.concatenate(near, axis=0) * 0.5).astype(BF16)
    near_ref[...] = jnp.dot(own, near, preferred_element_type=F32)
    away = [crossed(bond_part, blank), crossed(source, other)]
    far_weight_ref[...] = (jnp.concatenate(away, axis=0) * 0.5).astype(BF16)
    mix_weight_ref[...] = (diagonal_blocks(bond_mix_ref[...].astype(F32)) * 0.5).astype(BF16)
    weight = pair_ref[...].astype(F32) * 0.5
    pair_weight_ref[...] = jnp.concatenate(
        [two_blocks(weight[:, : 2 * feature]), two_blocks(weight[:, 2 * feature :])], axis=1
    ).astype(BF16)
    hidden_weight_ref[...] = (two_blocks(pair_hidden_ref[...].astype(F32)) * 0.25).astype(BF16)
    out_weight_ref[...] = (diagonal_blocks(pair_out_ref[...].astype(F32)) * 0.5).astype(BF16)
    weight = atom_in_ref[...].astype(F32) * 0.5
    atom_in_weight_ref[...] = crossed(weight, jnp.zeros_like(weight)).astype(BF16)
    weight = atom_out_ref[...].astype(F32) * 0.5
    blank = jnp.zeros_like(weight)
    weight = jnp.concatenate([weight, blank], axis=1)
    atom_out_weight_ref[...] = jnp.concatenate([weight, jnp.zeros_like(weight)], axis=0).astype(
        BF16
    )


def doubled_gate(values):
    half = values.shape[1] // 2
    first, second = values[:, :half], values[:, half:]
    return first * (1.0 + jnp.tanh(first)) * (1.0 + jnp.tanh(second))


def main_kernel(
    own_rows_ref,
    one_ref,
    two_ref,
    four_ref,
    three_ref,
    angular_ref,
    chosen_ref,
    own_ref,
    near_ref,
    far_weight_ref,
    mix_weight_ref,
    pair_weight_ref,
    hidden_weight_ref,
    out_weight_ref,
    atom_in_weight_ref,
    atom_out_weight_ref,
    atom_result_hbm,
    bond_result_hbm,
    atom_result_ref,
    bond_result_ref,
    first_ref,
    second_ref,
    pair_ref,
    total_ref,
    sems,
):
    slots, pairs, _ = angular_ref.shape
    bonds = 2 * pairs
    atoms = bonds // slots
    feature = own_ref.shape[1] // 2
    half = CAP // 2
    near_refs = (own_rows_ref, one_ref, two_ref)
    away_refs = (three_ref, four_ref)
    sent = [ref[:half] for ref in near_refs] + [ref[: 3 * half] for ref in away_refs]
    sent = jnp.concatenate(sent, axis=0)
    sent_atom = jnp.concatenate([ref[3 * half :] for ref in near_refs + away_refs], axis=0)
    blank = jnp.zeros((9 * half, feature), BF16)
    blank_atom = jnp.zeros((sent_atom.shape[0], feature), BF16)
    received = jnp.concatenate(
        [
            jnp.concatenate([sent[:, :feature], blank], axis=1),
            jnp.concatenate([sent[:, feature:], blank], axis=1),
            jnp.concatenate([blank_atom, sent_atom[:, :feature]], axis=1),
            jnp.concatenate([blank_atom, sent_atom[:, feature:]], axis=1),
        ],
        axis=0,
    )
    far = jnp.dot(chosen_ref[...], received, preferred_element_type=F32)
    incoming = near_ref[...] + jnp.dot(
        far.astype(BF16), far_weight_ref[...], preferred_element_type=F32
    )
    hidden = doubled_gate(incoming).astype(BF16)
    mixed = jnp.dot(hidden, mix_weight_ref[...], preferred_element_type=F32)
    old = jnp.where(left_lanes((bonds, 2 * feature)), far, own_ref[...].astype(F32))
    new = (old + mixed).astype(BF16).astype(F32)
    average = ((new + pltpu.roll(new, feature, 1)) * 0.5).astype(BF16).astype(F32)
    even, odd = average[:pairs], average[pairs:]
    left = left_lanes((pairs, 2 * feature))
    packed = jnp.where(left, even, odd)
    shifted = jnp.where(left, odd, jnp.concatenate([even[atoms:], even[:atoms]], axis=0))
    width = 4 * feature
    projected = jnp.dot(packed.astype(BF16), pair_weight_ref[...], preferred_element_type=F32)
    first_ref[...] = projected[:, :width]
    second = jnp.dot(shifted.astype(BF16), pair_weight_ref[:, width:], preferred_element_type=F32)
    for copy in range(2):
        second_ref[0, copy * pairs : (copy + 1) * pairs] = projected[:, width:]
        second_ref[1, copy * pairs : (copy + 1) * pairs] = second
    hidden_weight = hidden_weight_ref[...]
    height = pairs // 2
    steps = [(parity, start) for start in (0, height) for parity in (0, 1)]

    def first_gates(turn):
        for step, (parity, start) in enumerate(steps):
            offset = pl.multiple_of(start + turn * atoms, atoms)
            mixture = angular_ref[2 * turn + parity, pl.ds(start, height)] + (
                first_ref[pl.ds(start, height)] + second_ref[parity, pl.ds(offset, height)]
            )
            pair_ref[step] = doubled_gate(mixture).astype(BF16)

    def second_gates():
        gates = [
            doubled_gate(jnp.dot(pair_ref[k], hidden_weight, preferred_element_type=F32))
            for k in range(len(steps))
        ]
        for part, start in enumerate((0, height)):
            total_ref[pl.ds(start, height)] += gates[2 * part] + gates[2 * part + 1]

    def body(turn, carry):
        second_gates()
        first_gates(turn)
        return carry

    total_ref[...] = jnp.zeros_like(total_ref)
    first_gates(0)
    lax.fori_loop(1, slots // 2, body, 0)
    second_gates()
    pair_sum = total_ref[...].astype(BF16)
    bond_out = packed + jnp.dot(pair_sum, out_weight_ref[...], preferred_element_type=F32)
    bond_out = bond_out.astype(BF16)
    for k in range(slots // 2):
        bond_result_ref[0, 0, :, 2 * k * feature : 2 * (k + 1) * feature] = bond_out[
            k * atoms : (k + 1) * atoms
        ]
    bond_copy = pltpu.make_async_copy(bond_result_ref, bond_result_hbm, sems.at[0])
    bond_copy.start()
    pooled = jnp.zeros((atoms, 2 * feature), F32)
    for k in range(slots // 2):
        pooled = pooled + bond_out[k * atoms : (k + 1) * atoms].astype(F32)
    pooled = (pooled + pltpu.roll(pooled, feature, 1)) * (1.0 / slots)
    atom = own_ref[0:atoms].astype(F32)
    left = left_lanes((atoms, 2 * feature))
    joined = jnp.where(left, atom, pooled).astype(BF16)
    atom_hidden = doubled_gate(
        jnp.dot(joined, atom_in_weight_ref[...], preferred_element_type=F32)
    ).astype(BF16)
    atom_new = atom + jnp.dot(atom_hidden, atom_out_weight_ref[...], preferred_element_type=F32)
    atom_result_ref[0, 0] = atom_new[:, :feature].astype(BF16)
    atom_copy = pltpu.make_async_copy(atom_result_ref, atom_result_hbm, sems.at[1])
    atom_copy.start()
    bond_copy.wait()
    atom_copy.wait()


def per_device(
    atom_feat,
    bond_feat,
    neighbours,
    bond_dirs,
    bond_in_weight,
    bond_mix_weight,
    pair_weight,
    angle_weight,
    pair_hidden_weight,
    pair_out_weight,
    atom_in_weight,
    atom_out_weight,
):
    atoms, feature = atom_feat.shape[2], atom_feat.shape[3]
    slots = neighbours.shape[3]
    bonds = atoms * slots
    pairs = bonds // 2
    half = CAP // 2
    extents = (lax.axis_size("gx"), lax.axis_size("gy"))
    paired = (extents[0] % 2 == 0, False)
    targets = neighbours[0, 0].T
    hbm = pl.BlockSpec(memory_space=pltpu.HBM)
    vmem = pl.BlockSpec(memory_space=pltpu.VMEM)
    params = pltpu.CompilerParams(vmem_limit_bytes=32 * 2**20)

    def shaped(shape, dtype):
        return jax.ShapeDtypeStruct(shape, dtype)

    def in_hbm(arrays):
        return tuple(pltpu.with_memory_space_constraint(x, pltpu.HBM) for x in arrays)

    payload = shaped((3 * half + atoms // 2, 2 * feature), BF16)
    inputs = (targets, atom_feat, bond_feat)
    own, one, two, *held = pl.pallas_call(
        functools.partial(pack_kernel, extents, paired),
        out_shape=(payload,) * 3 + tuple(shaped(x.shape, x.dtype) for x in inputs),
        in_specs=[hbm] * 3,
        out_specs=(vmem,) * 6,
        scratch_shapes=[pltpu.SemaphoreType.DMA((3,))],
        compiler_params=params,
        name="pack",
    )(*in_hbm(inputs))
    first, second = moves(extents[0], paired[0])
    one = lax.ppermute(one, "gx", first)
    two = lax.ppermute(two, "gx", second)
    weights = (bond_in_weight, bond_mix_weight, pair_weight, pair_hidden_weight)
    weights += (pair_out_weight, atom_in_weight, atom_out_weight)
    *prepared, bond_dirs, angle_weight = pl.pallas_call(
        functools.partial(prepare_kernel, extents, paired),
        out_shape=(
            shaped((bonds, 9 * CAP + 9 * atoms), BF16),
            shaped((bonds, 2 * feature), BF16),
            shaped((bonds, 4 * feature), F32),
            shaped((2 * feature, 4 * feature), BF16),
            shaped((2 * feature, 2 * feature), BF16),
            shaped((2 * feature, 8 * feature), BF16),
            shaped((2 * feature, 4 * feature), BF16),
            shaped((2 * feature, 2 * feature), BF16),
            shaped((2 * feature, 4 * feature), BF16),
            shaped((2 * feature, 2 * feature), BF16),
            shaped(bond_dirs.shape, F32),
            shaped(angle_weight.shape, BF16),
        ),
        in_specs=[vmem] * 3 + [hbm] * 9,
        out_specs=(vmem,) * 12,
        scratch_shapes=[pltpu.VMEM(x.shape, BF16) for x in weights]
        + [pltpu.SemaphoreType.DMA((9,))],
        compiler_params=params,
        cost_estimate=pl.CostEstimate(flops=64 * 2**20, bytes_accessed=2**21, transcendentals=0),
        name="prepare",
    )(*held, *in_hbm(weights + (bond_dirs, angle_weight)))
    own, one, two, prepared = lax.optimization_barrier((own, one, two, prepared))
    first, second = moves(extents[1], paired[1])

    def forwarded(block):
        parts = [x[block * half : (block + 1) * half] for x in (own, one, two)]
        return jnp.concatenate(parts + [x[3 * half :] for x in (own, one, two)], axis=0)

    three = lax.ppermute(forwarded(1), "gy", first)
    four = lax.ppermute(forwarded(2), "gy", second)
    angular = pl.pallas_call(
        functools.partial(angular_kernel, atoms),
        out_shape=shaped((slots, pairs, 4 * feature), F32),
        in_specs=[vmem, vmem],
        out_specs=vmem,
        compiler_params=params,
        cost_estimate=pl.CostEstimate(
            flops=256 * 2**20, bytes_accessed=2**22, transcendentals=4096
        ),
        name="angular",
    )(bond_dirs, angle_weight)
    return pl.pallas_call(
        main_kernel,
        out_shape=(shaped(atom_feat.shape, BF16), shaped(bond_feat.shape, BF16)),
        in_specs=[vmem] * 16,
        out_specs=(hbm, hbm),
        scratch_shapes=[
            pltpu.VMEM(atom_feat.shape, BF16),
            pltpu.VMEM(bond_feat.shape, BF16),
            pltpu.VMEM((pairs, 4 * feature), F32),
            pltpu.VMEM((2, 2 * pairs, 4 * feature), F32),
            pltpu.VMEM((4, pairs // 2, 2 * feature), BF16),
            pltpu.VMEM((pairs, 2 * feature), F32),
            pltpu.SemaphoreType.DMA((2,)),
        ],
        compiler_params=params,
        cost_estimate=pl.CostEstimate(
            flops=400 * 2**20, bytes_accessed=2**22, transcendentals=2**21
        ),
        name="main",
    )(own, one, two, four, three, angular, *prepared)


def solution(mesh):
    placed = (
        P("gx", "gy", None, None),
        P("gx", "gy", None, None),
        P("gx", "gy", None, None),
        P(None, "gx", "gy", None),
        P(),
        P(),
        P(),
        P(),
        P(),
        P(),
        P(),
        P(),
    )
    return jax.shard_map(
        per_device,
        mesh=mesh,
        in_specs=placed,
        out_specs=(P("gx", "gy", None, None), P("gx", "gy", None, None)),
        check_vma=False,
    )
```

profile of v0, /device:TPU:0, one launch (start us, length us, event | category | flops | bytes accessed | tf_op | source)
XLA Modules:
  0.0 18.4 jit_solution(15495879621187072358)
XLA Ops:
  0.6 1.6 %pack.1 = (bf16[112,128]{1,0:T(8,128)(2,1)S(1)}, bf16[112,128]{1,0:T(8,128)(2,1)S(1)}, bf16[112,128]{1,0:T(8,128)(2,1)S(1)}, s32[16,32]{1,0:T(8,128)S(1)}, bf16[...) custom-call(s32[16,32]{1,0:T(8,128)} %bitcast.3, bf16[1,1,32,64]{3,2,1,0:T(8,128)(2,1)} %atom_hbm.1, ...), custom_call_target="tpu_custom_call" | custom-call | tf_op jit(solution)/shard_map/pack/pallas_call | solution.py:483
  2.2 2.4 %collective-permute-start = (bf16[112,128]{1,0:T(8,128)(2,1)S(1)}, bf16[112,128]{1,0:T(8,128)(2,1)S(1)}, u32[]{:S(2)}, u32[]{:S(2)}) collective-permute-start(bf16[112,128]{1,0:T(8,128)(2,1)S(1)} %get-tuple-element.34), channel_id=1, source_target_pairs={{0,24},{8,16},{16,8},{24,0},{1,25},{9,17},{17,9},{25,1},{2,26},{10... | collective-permute-start | bytes 86024 | tf_op jit(solution)/shard_map/ppermute | solution.py:493
  4.7 0.7 %collective-permute-start.1 = (bf16[112,128]{1,0:T(8,128)(2,1)S(1)}, bf16[112,128]{1,0:T(8,128)(2,1)S(1)}, u32[]{:S(2)}, u32[]{:S(2)}) collective-permute-start(bf16[112,128]{1,0:T(8,128)(2,1)S(1)} %get-tuple-element.35), channel_id=1, source_target_pairs={{0,8},{8,0},{16,24},{24,16},{1,9},{9,1},{17,25},{25,17},{2,10},{10... | collective-permute-start | bytes 86024 | tf_op jit(solution)/shard_map/ppermute | solution.py:494
  5.3 1.9 %prepare.1 = (bf16[512,864]{1,0:T(8,128)(2,1)S(1)}, bf16[512,128]{1,0:T(8,128)(2,1)S(1)}, f32[512,256]{1,0:T(8,128)S(1)}, bf16[128,256]{1,0:T(8,128)(2,1)S(1)}, ...) custom-call(s32[16,32]{1,0:T(8,128)S(1)} %get-tuple-element.36.targe, ...), custom_call_target="tpu_custom_call" | custom-call | flops 67108864 | bytes 2097152 | tf_op jit(solution)/shard_map/prepare/pallas_call | solution.py:497
  7.2 0.0 collective-permute-done.one_ref
  7.2 0.0 collective-permute-done.1.two_ref
  7.3 1.6 %collective-permute-start.3 = (bf16[144,128]{1,0:T(8,128)(2,1)S(1)}, bf16[144,128]{1,0:T(8,128)(2,1)S(1)}, u32[]{:S(2)}, u32[]{:S(2)}) collective-permute-start(bf16[144,128]{1,0:T(8,128)(2,1)S(1)} %get-tuple-element.64), channel_id=1, source_target_pairs={{0,1},{1,2},{2,3},{3,4},{4,5},{5,6},{6,7},{7,0},{8,9},{9,10},{10,1... | collective-permute-start | bytes 110600 | tf_op jit(solution)/shard_map/ppermute | solution.py:528
  8.9 3.2 %collective-permute-start.2 = (bf16[144,128]{1,0:T(8,128)(2,1)S(1)}, bf16[144,128]{1,0:T(8,128)(2,1)S(1)}, u32[]{:S(2)}, u32[]{:S(2)}) collective-permute-start(bf16[144,128]{1,0:T(8,128)(2,1)S(1)} %get-tuple-element.65), channel_id=1, source_target_pairs={{1,0},{2,1},{3,2},{4,3},{5,4},{6,5},{7,6},{0,7},{9,8},{10,9},{11,1... | collective-permute-start | bytes 110600 | tf_op jit(solution)/shard_map/ppermute | solution.py:529
  12.1 1.3 %angular.1.angular_ref = f32[16,256,256]{2,1,0:T(8,128)S(1)} custom-call(f32[2,1,1,512]{3,2,1,0:T(1,128)S(1)} %get-tuple-element.52.dirs_ref, bf16[64,128]{1,0:T(8,128)(2,1)S(1)} %get-tuple-element.53.angle_ref), custom_call_target="tpu_custom_call" | custom-call | flops 268435456 | bytes 4194304 | tf_op jit(solution)/shard_map/angular/pallas_call | solution.py:530
  13.4 0.7 %collective-permute-done.3.three_ref = bf16[144,128]{1,0:T(8,128)(2,1)S(1)} collective-permute-done((bf16[144,128]{1,0:T(8,128)(2,1)S(1)}, bf16[144,128]{1,0:T(8,128)(2,1)S(1)}, u32[]{:S(2)}, u32[]{:S(2)}) %collective-permute-start.3) | collective-permute-done | bytes 36896 | tf_op jit(solution)/shard_map/ppermute | solution.py:528
  14.0 0.0 collective-permute-done.2.four_ref
  14.0 4.3 %main.1 = (bf16[1,1,32,64]{3,2,1,0:T(8,128)(2,1)}, bf16[1,1,32,1024]{3,2,1,0:T(8,128)(2,1)}) custom-call(bf16[112,128]{1,0:T(8,128)(2,1)S(1)} %get-tuple-element.49.own_rows_ref, bf16[112,128]{1,0:T(8,128)(2,1)S(1)} %collective-permute-done.one_ref, bf16[112,128]{1,0:T(8,128)(2,1)S(1)} %collective-permute-done.1.two_ref, ...), custom_call_target="tpu_custom_call" | custom-call | flops 419430400 | bytes 4194304 | tf_op jit(solution)/shard_map/main/pallas_call | solution.py:541
  (6 shorter events, 0.1 us)
Async XLA Ops:
  2.2 5.0 %collective-permute-start = (bf16[112,128]{1,0:T(8,128)(2,1)S(1)}, bf16[112,128]{1,0:T(8,128)(2,1)S(1)}, u32[]{:S(2)}, u32[]{:S(2)}) collective-permute-start(bf16[112,128]{1,0:T(8,128)(2,1)S(1)} %get-tuple-element.34), channel_id=1, source_target_pairs={{0,24},{8,16},{16,8},{24,0},{1,25},{9,17},{17,9},{25,1},{2,26},{10... | collective-permute-start | bytes 86024 | tf_op jit(solution)/shard_map/ppermute | solution.py:493
  4.7 2.6 %collective-permute-start.1 = (bf16[112,128]{1,0:T(8,128)(2,1)S(1)}, bf16[112,128]{1,0:T(8,128)(2,1)S(1)}, u32[]{:S(2)}, u32[]{:S(2)}) collective-permute-start(bf16[112,128]{1,0:T(8,128)(2,1)S(1)} %get-tuple-element.35), channel_id=1, source_target_pairs={{0,8},{8,0},{16,24},{24,16},{1,9},{9,1},{17,25},{25,17},{2,10},{10... | collective-permute-start | bytes 86024 | tf_op jit(solution)/shard_map/ppermute | solution.py:494
  7.3 6.7 %collective-permute-start.3 = (bf16[144,128]{1,0:T(8,128)(2,1)S(1)}, bf16[144,128]{1,0:T(8,128)(2,1)S(1)}, u32[]{:S(2)}, u32[]{:S(2)}) collective-permute-start(bf16[144,128]{1,0:T(8,128)(2,1)S(1)} %get-tuple-element.64), channel_id=1, source_target_pairs={{0,1},{1,2},{2,3},{3,4},{4,5},{5,6},{6,7},{7,0},{8,9},{9,10},{10,1... | collective-permute-start | bytes 110600 | tf_op jit(solution)/shard_map/ppermute | solution.py:528
  8.9 5.1 %collective-permute-start.2 = (bf16[144,128]{1,0:T(8,128)(2,1)S(1)}, bf16[144,128]{1,0:T(8,128)(2,1)S(1)}, u32[]{:S(2)}, u32[]{:S(2)}) collective-permute-start(bf16[144,128]{1,0:T(8,128)(2,1)S(1)} %get-tuple-element.65), channel_id=1, source_target_pairs={{1,0},{2,1},{3,2},{4,3},{5,4},{6,5},{7,6},{0,7},{9,8},{10,9},{11,1... | collective-permute-start | bytes 110600 | tf_op jit(solution)/shard_map/ppermute | solution.py:529
where the time goes:
time: 18.6 us; the launch traced here: 18.4 us
  Pallas kernels  9.04 us (49%)
  starting transfers between devices  7.89 us (42%)
  between operations  0.7 us (4%)
  waiting for transfers between devices  0.68 us (4%)
    pallas_call x1, Pallas kernels, per_device(): pl.pallas_call(main_kernel, out_shape=(shaped(atom_feat.shape, BF16), sha...  4.33 us
    ppermute x1, starting transfers between devices, per_device(): four = lax.ppermute(forwarded(2), 'gy', second)  3.18 us
    ppermute x1, starting transfers between devices, per_device(): one = lax.ppermute(one, 'gx', first)  2.44 us
    pallas_call x1, Pallas kernels, per_device(): pl.pallas_call(functools.partial(prepare_kernel, extents, paired), out_sh...  1.88 us
    ppermute x1, starting transfers between devices, per_device(): three = lax.ppermute(forwarded(1), 'gy', first)  1.6 us
    pallas_call x1, Pallas kernels, per_device(): pl.pallas_call(functools.partial(pack_kernel, extents, paired), out_shape...  1.57 us
    pallas_call x1, Pallas kernels, per_device(): pl.pallas_call(functools.partial(angular_kernel, atoms), out_shape=shaped...  1.26 us
    ppermute x1, starting transfers between devices, per_device(): two = lax.ppermute(two, 'gx', second)  0.68 us
  transfers between devices with their start and end apart: 4, of which 1 were waited for; matrix products, arithmetic and copies ran while one was open for 0% of the time, Pallas kernels for 17%

commit v1 on v0

--- a/solution.py
+++ b/solution.py
@@ -322,36 +322,25 @@
     return first * (1.0 + jnp.tanh(first)) * (1.0 + jnp.tanh(second))
 
 
-def main_kernel(
+def bond_kernel(
     own_rows_ref,
     one_ref,
     two_ref,
     four_ref,
     three_ref,
-    angular_ref,
     chosen_ref,
     own_ref,
     near_ref,
     far_weight_ref,
     mix_weight_ref,
     pair_weight_ref,
-    hidden_weight_ref,
-    out_weight_ref,
-    atom_in_weight_ref,
-    atom_out_weight_ref,
-    atom_result_hbm,
-    bond_result_hbm,
-    atom_result_ref,
-    bond_result_ref,
+    packed_ref,
     first_ref,
     second_ref,
-    pair_ref,
-    total_ref,
-    sems,
 ):
-    slots, pairs, _ = angular_ref.shape
-    bonds = 2 * pairs
-    atoms = bonds // slots
+    bonds = own_ref.shape[0]
+    pairs = bonds // 2
+    atoms = 2 * (own_rows_ref.shape[0] - 3 * CAP // 2)
     feature = own_ref.shape[1] // 2
     half = CAP // 2
     near_refs = (own_rows_ref, one_ref, two_ref)
@@ -385,65 +374,66 @@
     shifted = jnp.where(left, odd, jnp.concatenate([even[atoms:], even[:atoms]], axis=0))
     width = 4 * feature
     projected = jnp.dot(packed.astype(BF16), pair_weight_ref[...], preferred_element_type=F32)
+    packed_ref[...] = packed
     first_ref[...] = projected[:, :width]
-    second = jnp.dot(shifted.astype(BF16), pair_weight_ref[:, width:], preferred_element_type=F32)
-    for copy in range(2):
-        second_ref[0, copy * pairs : (copy + 1) * pairs] = projected[:, width:]
-        second_ref[1, copy * pairs : (copy + 1) * pairs] = second
+    second_ref[0] = projected[:, width:]
+    second_ref[1] = jnp.dot(
+        shifted.astype(BF16), pair_weight_ref[:, width:], preferred_element_type=F32
+    )
+
+
+def pair_kernel(
+    angular_ref,
+    packed_ref,
+    first_ref,
+    second_ref,
+    hidden_weight_ref,
+    out_weight_ref,
+    bond_result_ref,
+):
+    slots, pairs, _ = angular_ref.shape
+    atoms = 2 * pairs // slots
+    width = packed_ref.shape[1]
     hidden_weight = hidden_weight_ref[...]
     height = pairs // 2
-    steps = [(parity, start) for start in (0, height) for parity in (0, 1)]
-
-    def first_gates(turn):
-        for step, (parity, start) in enumerate(steps):
-            offset = pl.multiple_of(start + turn * atoms, atoms)
-            mixture = angular_ref[2 * turn + parity, pl.ds(start, height)] + (
-                first_ref[pl.ds(start, height)] + second_ref[parity, pl.ds(offset, height)]
+    for start in range(0, pairs, height):
+        total = jnp.zeros((height, width), F32)
+        for diagonal in range(slots):
+            offset = start + diagonal // 2 * atoms
+            pieces = [
+                second_ref[diagonal % 2, pl.ds((offset + k) % pairs, atoms)]
+                for k in range(0, height, atoms)
+            ]
+            mixture = angular_ref[diagonal, pl.ds(start, height)] + (
+                first_ref[pl.ds(start, height)] + jnp.concatenate(pieces, axis=0)
             )
-            pair_ref[step] = doubled_gate(mixture).astype(BF16)
-
-    def second_gates():
-        gates = [
-            doubled_gate(jnp.dot(pair_ref[k], hidden_weight, preferred_element_type=F32))
-            for k in range(len(steps))
-        ]
-        for part, start in enumerate((0, height)):
-            total_ref[pl.ds(start, height)] += gates[2 * part] + gates[2 * part + 1]
-
-    def body(turn, carry):
-        second_gates()
-        first_gates(turn)
-        return carry
-
-    total_ref[...] = jnp.zeros_like(total_ref)
-    first_gates(0)
-    lax.fori_loop(1, slots // 2, body, 0)
-    second_gates()
-    pair_sum = total_ref[...].astype(BF16)
-    bond_out = packed + jnp.dot(pair_sum, out_weight_ref[...], preferred_element_type=F32)
-    bond_out = bond_out.astype(BF16)
-    for k in range(slots // 2):
-        bond_result_ref[0, 0, :, 2 * k * feature : 2 * (k + 1) * feature] = bond_out[
-            k * atoms : (k + 1) * atoms
-        ]
-    bond_copy = pltpu.make_async_copy(bond_result_ref, bond_result_hbm, sems.at[0])
-    bond_copy.start()
+            pair = doubled_gate(mixture).astype(BF16)
+            total = total + doubled_gate(
+                jnp.dot(pair, hidden_weight, preferred_element_type=F32)
+            )
+        bond_out = packed_ref[pl.ds(start, height)] + jnp.dot(
+            total.astype(BF16), out_weight_ref[...], preferred_element_type=F32
+        )
+        bond_out = bond_out.astype(BF16)
+        for k in range(height // atoms):
+            place = (start // atoms + k) * width
+            bond_result_ref[0, 0, :, place : place + width] = bond_out[k * atoms : (k + 1) * atoms]
+
+
+def atom_kernel(bond_ref, own_ref, atom_in_weight_ref, atom_out_weight_ref, atom_result_ref):
+    atoms, feature = atom_result_ref.shape[2], atom_result_ref.shape[3]
+    slots = bond_ref.shape[3] // feature
     pooled = jnp.zeros((atoms, 2 * feature), F32)
-    for k in range(slots // 2):
-        pooled = pooled + bond_out[k * atoms : (k + 1) * atoms].astype(F32)
+    for block in blocks_of(bond_ref, slots // 2):
+        pooled = pooled + block.astype(F32)
     pooled = (pooled + pltpu.roll(pooled, feature, 1)) * (1.0 / slots)
     atom = own_ref[0:atoms].astype(F32)
-    left = left_lanes((atoms, 2 * feature))
-    joined = jnp.where(left, atom, pooled).astype(BF16)
+    joined = jnp.where(left_lanes((atoms, 2 * feature)), atom, pooled).astype(BF16)
     atom_hidden = doubled_gate(
         jnp.dot(joined, atom_in_weight_ref[...], preferred_element_type=F32)
     ).astype(BF16)
     atom_new = atom + jnp.dot(atom_hidden, atom_out_weight_ref[...], preferred_element_type=F32)
     atom_result_ref[0, 0] = atom_new[:, :feature].astype(BF16)
-    atom_copy = pltpu.make_async_copy(atom_result_ref, atom_result_hbm, sems.at[1])
-    atom_copy.start()
-    bond_copy.wait()
-    atom_copy.wait()
 
 
 def per_device(
@@ -538,26 +528,37 @@
         ),
         name="angular",
     )(bond_dirs, angle_weight)
-    return pl.pallas_call(
-        main_kernel,
-        out_shape=(shaped(atom_feat.shape, BF16), shaped(bond_feat.shape, BF16)),
-        in_specs=[vmem] * 16,
-        out_specs=(hbm, hbm),
-        scratch_shapes=[
-            pltpu.VMEM(atom_feat.shape, BF16),
-            pltpu.VMEM(bond_feat.shape, BF16),
-            pltpu.VMEM((pairs, 4 * feature), F32),
-            pltpu.VMEM((2, 2 * pairs, 4 * feature), F32),
-            pltpu.VMEM((4, pairs // 2, 2 * feature), BF16),
-            pltpu.VMEM((pairs, 2 * feature), F32),
-            pltpu.SemaphoreType.DMA((2,)),
-        ],
+    chosen, own_rows, near, far_weight, mix_weight, pair_weight, *others = prepared
+    hidden_weight, out_weight, atom_in_weight, atom_out_weight = others
+    packed, projected, turned = pl.pallas_call(
+        bond_kernel,
+        out_shape=(
+            shaped((pairs, 2 * feature), F32),
+            shaped((pairs, 4 * feature), F32),
+            shaped((2, pairs, 4 * feature), F32),
+        ),
+        in_specs=[vmem] * 11,
+        out_specs=(vmem,) * 3,
         compiler_params=params,
-        cost_estimate=pl.CostEstimate(
-            flops=400 * 2**20, bytes_accessed=2**22, transcendentals=2**21
-        ),
-        name="main",
-    )(own, one, two, four, three, angular, *prepared)
+        name="bonds",
+    )(own, one, two, four, three, chosen, own_rows, near, far_weight, mix_weight, pair_weight)
+    bond_out = pl.pallas_call(
+        pair_kernel,
+        out_shape=shaped(bond_feat.shape, BF16),
+        in_specs=[vmem] * 6,
+        out_specs=vmem,
+        compiler_params=params,
+        name="pairs",
+    )(angular, packed, projected, turned, hidden_weight, out_weight)
+    atom_out = pl.pallas_call(
+        atom_kernel,
+        out_shape=shaped(atom_feat.shape, BF16),
+        in_specs=[vmem] * 4,
+        out_specs=vmem,
+        compiler_params=params,
+        name="atoms",
+    )(bond_out, own_rows, atom_in_weight, atom_out_weight)
+    return atom_out, bond_out
 
 
 def solution(mesh):

time: 18.6 us -> 19.6 us (1.054)
  local copies, waits for them, and re-layouts: 0.05 us -> 0.89 us
    unnamed x5 -> x7, local copies, waits for them, and re-layouts: 0.04 us -> 0.88 us
    pallas_call x1 -> x3, Pallas kernels: 4.33 us -> 4.37 us  [the longest x1 2.18 us: per_device(): pl.pallas_call(pair_kernel, out_shape=shaped(bond_feat.shape, BF16), in_s...]
  transfers between devices with their start and end apart: 4 -> 4, of which waited for: 1 -> 1; matrix products, arithmetic and copies ran while one was open for 0% -> 0% of each run, Pallas kernels for 17% -> 16%
where the time goes in v1:
time: 19.6 us; the launch traced here: 19.2 us
  Pallas kernels  9.08 us (46%)
  starting transfers between devices  7.89 us (40%)
  local copies, waits for them, and re-layouts  0.89 us (5%)
  between operations  0.7 us (4%)
  waiting for transfers between devices  0.68 us (3%)
    ppermute x1, starting transfers between devices, per_device(): four = lax.ppermute(forwarded(2), 'gy', second)  3.18 us
    ppermute x1, starting transfers between devices, per_device(): one = lax.ppermute(one, 'gx', first)  2.44 us
    pallas_call x1, Pallas kernels, per_device(): pl.pallas_call(pair_kernel, out_shape=shaped(bond_feat.shape, BF16), in_s...  2.18 us
    pallas_call x1, Pallas kernels, per_device(): pl.pallas_call(functools.partial(prepare_kernel, extents, paired), out_sh...  1.88 us
    ppermute x1, starting transfers between devices, per_device(): three = lax.ppermute(forwarded(1), 'gy', first)  1.6 us
    pallas_call x1, Pallas kernels, per_device(): pl.pallas_call(functools.partial(pack_kernel, extents, paired), out_shape...  1.57 us
    pallas_call x1, Pallas kernels, per_device(): pl.pallas_call(bond_kernel, out_shape=(shaped((pairs, 2 * feature), F32),...  1.27 us
    pallas_call x1, Pallas kernels, per_device(): pl.pallas_call(functools.partial(angular_kernel, atoms), out_shape=shaped...  1.26 us
  transfers between devices with their start and end apart: 4, of which 1 were waited for; matrix products, arithmetic and copies ran while one was open for 0% of the time, Pallas kernels for 16%

profile of v1, /device:TPU:0, one launch (start us, length us, event | category | flops | bytes accessed | tf_op | source)
XLA Modules:
  0.0 19.2 jit_solution(15803890326046174274)
XLA Ops:
  0.6 1.6 %pack.1 = (bf16[112,128]{1,0:T(8,128)(2,1)S(1)}, bf16[112,128]{1,0:T(8,128)(2,1)S(1)}, bf16[112,128]{1,0:T(8,128)(2,1)S(1)}, s32[16,32]{1,0:T(8,128)S(1)}, bf16[...) custom-call(s32[16,32]{1,0:T(8,128)} %bitcast.3, bf16[1,1,32,64]{3,2,1,0:T(8,128)(2,1)} %atom_hbm.1, ...), custom_call_target="tpu_custom_call" | custom-call | tf_op jit(solution)/shard_map/pack/pallas_call | solution.py:473
  2.2 2.4 %collective-permute-start = (bf16[112,128]{1,0:T(8,128)(2,1)S(1)}, bf16[112,128]{1,0:T(8,128)(2,1)S(1)}, u32[]{:S(2)}, u32[]{:S(2)}) collective-permute-start(bf16[112,128]{1,0:T(8,128)(2,1)S(1)} %get-tuple-element.42), channel_id=1, source_target_pairs={{0,24},{8,16},{16,8},{24,0},{1,25},{9,17},{17,9},{25,1},{2,26},{10... | collective-permute-start | bytes 86024 | tf_op jit(solution)/shard_map/ppermute | solution.py:483
  4.7 0.7 %collective-permute-start.1 = (bf16[112,128]{1,0:T(8,128)(2,1)S(1)}, bf16[112,128]{1,0:T(8,128)(2,1)S(1)}, u32[]{:S(2)}, u32[]{:S(2)}) collective-permute-start(bf16[112,128]{1,0:T(8,128)(2,1)S(1)} %get-tuple-element.43), channel_id=1, source_target_pairs={{0,8},{8,0},{16,24},{24,16},{1,9},{9,1},{17,25},{25,17},{2,10},{10... | collective-permute-start | bytes 86024 | tf_op jit(solution)/shard_map/ppermute | solution.py:484
  5.3 1.9 %prepare.1 = (bf16[512,864]{1,0:T(8,128)(2,1)S(1)}, bf16[512,128]{1,0:T(8,128)(2,1)S(1)}, f32[512,256]{1,0:T(8,128)S(1)}, bf16[128,256]{1,0:T(8,128)(2,1)S(1)}, ...) custom-call(s32[16,32]{1,0:T(8,128)S(1)} %get-tuple-element.36.targe, ...), custom_call_target="tpu_custom_call" | custom-call | flops 67108864 | bytes 2097152 | tf_op jit(solution)/shard_map/prepare/pallas_call | solution.py:487
  7.2 0.0 collective-permute-done.one_ref
  7.2 0.0 collective-permute-done.1.two_ref
  7.3 1.6 %collective-permute-start.3 = (bf16[144,128]{1,0:T(8,128)(2,1)S(1)}, bf16[144,128]{1,0:T(8,128)(2,1)S(1)}, u32[]{:S(2)}, u32[]{:S(2)}) collective-permute-start(bf16[144,128]{1,0:T(8,128)(2,1)S(1)} %get-tuple-element.70), channel_id=1, source_target_pairs={{0,1},{1,2},{2,3},{3,4},{4,5},{5,6},{6,7},{7,0},{8,9},{9,10},{10,1... | collective-permute-start | bytes 110600 | tf_op jit(solution)/shard_map/ppermute | solution.py:518
  8.9 3.2 %collective-permute-start.2 = (bf16[144,128]{1,0:T(8,128)(2,1)S(1)}, bf16[144,128]{1,0:T(8,128)(2,1)S(1)}, u32[]{:S(2)}, u32[]{:S(2)}) collective-permute-start(bf16[144,128]{1,0:T(8,128)(2,1)S(1)} %get-tuple-element.71), channel_id=1, source_target_pairs={{1,0},{2,1},{3,2},{4,3},{5,4},{6,5},{7,6},{0,7},{9,8},{10,9},{11,1... | collective-permute-start | bytes 110600 | tf_op jit(solution)/shard_map/ppermute | solution.py:519
  12.1 1.3 %angular.1.angular_ref = f32[16,256,256]{2,1,0:T(8,128)S(1)} custom-call(f32[2,1,1,512]{3,2,1,0:T(1,128)S(1)} %get-tuple-element.39.dirs_ref, bf16[64,128]{1,0:T(8,128)(2,1)S(1)} %get-tuple-element.40.angle_ref), custom_call_target="tpu_custom_call" | custom-call | flops 268435456 | bytes 4194304 | tf_op jit(solution)/shard_map/angular/pallas_call | solution.py:520
  13.4 0.7 %collective-permute-done.3.three_ref = bf16[144,128]{1,0:T(8,128)(2,1)S(1)} collective-permute-done((bf16[144,128]{1,0:T(8,128)(2,1)S(1)}, bf16[144,128]{1,0:T(8,128)(2,1)S(1)}, u32[]{:S(2)}, u32[]{:S(2)}) %collective-permute-start.3) | collective-permute-done | bytes 36896 | tf_op jit(solution)/shard_map/ppermute | solution.py:518
  14.0 0.0 collective-permute-done.2.four_ref
  14.0 1.3 %bonds.1 = (f32[256,128]{1,0:T(8,128)S(1)}, f32[256,256]{1,0:T(8,128)S(1)}, f32[2,256,256]{2,1,0:T(8,128)S(1)}) custom-call(bf16[112,128]{1,0:T(8,128)(2,1)S(1)} %get-tuple-element.54.own_rows_ref, bf16[112,128]{1,0:T(8,128)(2,1)S(1)} %collective-permute-done.one_ref, bf16[112,128]{1,0:T(8,128)(2,1)S(1)} %collective-permute-done.1.two_ref, ...), custom_call_target="tpu_custom_call" | custom-call | tf_op jit(solution)/shard_map/bonds/pallas_call | solution.py:533
  15.3 2.2 %pairs.1.bond_ref = bf16[1,1,32,1024]{3,2,1,0:T(8,128)(2,1)} custom-call(f32[16,256,256]{2,1,0:T(8,128)S(1)} %angular.1.angular_ref, f32[256,128]{1,0:T(8,128)S(1)} %get-tuple-element.63.packed_ref, f32[256,256]{1,0:T(8,128)S(1)} %get-tuple-element.64.first_ref, f32[2,256,256]{2,1,0:T(8,128)S(1)} %get-tuple-element.65.second_ref, ...), custom_call_target="tpu_custom_call" | custom-call | tf_op jit(solution)/shard_map/pairs/pallas_call | solution.py:545
  17.5 0.0 copy-start
  17.5 0.8 %copy-done = bf16[1,1,32,1024]{3,2,1,0:T(8,128)(2,1)S(1)} copy-done((bf16[1,1,32,1024]{3,2,1,0:T(8,128)(2,1)S(1)}, bf16[1,1,32,1024]{3,2,1,0:T(8,128)(2,1)}, u32[]{:S(2)}) %copy-start) | copy-done | bytes 65560
  18.3 0.9 %atoms.1 = bf16[1,1,32,64]{3,2,1,0:T(8,128)(2,1)} custom-call(bf16[1,1,32,1024]{3,2,1,0:T(8,128)(2,1)S(1)} %copy-done, bf16[512,128]{1,0:T(8,128)(2,1)S(1)} %get-tuple-element.58.own_ref, bf16[128,256]{1,0:T(8,128)(2,1)S(1)} %get-tuple-element.68.atom_in_weight_ref, bf16[128,128]{1,0:T(8,128)(2,1)S(1)} %get-tuple-element.69.atom_out_weight_ref), custom_call_target="tpu_custom_call" | custom-call | tf_op jit(solution)/shard_map/atoms/pallas_call | solution.py:553
  (6 shorter events, 0.1 us)
Async XLA Ops:
  2.2 5.0 %collective-permute-start = (bf16[112,128]{1,0:T(8,128)(2,1)S(1)}, bf16[112,128]{1,0:T(8,128)(2,1)S(1)}, u32[]{:S(2)}, u32[]{:S(2)}) collective-permute-start(bf16[112,128]{1,0:T(8,128)(2,1)S(1)} %get-tuple-element.42), channel_id=1, source_target_pairs={{0,24},{8,16},{16,8},{24,0},{1,25},{9,17},{17,9},{25,1},{2,26},{10... | collective-permute-start | bytes 86024 | tf_op jit(solution)/shard_map/ppermute | solution.py:483
  4.7 2.6 %collective-permute-start.1 = (bf16[112,128]{1,0:T(8,128)(2,1)S(1)}, bf16[112,128]{1,0:T(8,128)(2,1)S(1)}, u32[]{:S(2)}, u32[]{:S(2)}) collective-permute-start(bf16[112,128]{1,0:T(8,128)(2,1)S(1)} %get-tuple-element.43), channel_id=1, source_target_pairs={{0,8},{8,0},{16,24},{24,16},{1,9},{9,1},{17,25},{25,17},{2,10},{10... | collective-permute-start | bytes 86024 | tf_op jit(solution)/shard_map/ppermute | solution.py:484
  7.3 6.7 %collective-permute-start.3 = (bf16[144,128]{1,0:T(8,128)(2,1)S(1)}, bf16[144,128]{1,0:T(8,128)(2,1)S(1)}, u32[]{:S(2)}, u32[]{:S(2)}) collective-permute-start(bf16[144,128]{1,0:T(8,128)(2,1)S(1)} %get-tuple-element.70), channel_id=1, source_target_pairs={{0,1},{1,2},{2,3},{3,4},{4,5},{5,6},{6,7},{7,0},{8,9},{9,10},{10,1... | collective-permute-start | bytes 110600 | tf_op jit(solution)/shard_map/ppermute | solution.py:518
  8.9 5.1 %collective-permute-start.2 = (bf16[144,128]{1,0:T(8,128)(2,1)S(1)}, bf16[144,128]{1,0:T(8,128)(2,1)S(1)}, u32[]{:S(2)}, u32[]{:S(2)}) collective-permute-start(bf16[144,128]{1,0:T(8,128)(2,1)S(1)} %get-tuple-element.71), channel_id=1, source_target_pairs={{1,0},{2,1},{3,2},{4,3},{5,4},{6,5},{7,6},{0,7},{9,8},{10,9},{11,1... | collective-permute-start | bytes 110600 | tf_op jit(solution)/shard_map/ppermute | solution.py:519
  17.5 0.8 %copy-start = (bf16[1,1,32,1024]{3,2,1,0:T(8,128)(2,1)S(1)}, bf16[1,1,32,1024]{3,2,1,0:T(8,128)(2,1)}, u32[]{:S(2)}) copy-start(bf16[1,1,32,1024]{3,2,1,0:T(8,128)(2,1)} %pairs.1.bond_ref) | copy-start | bytes 196612

commit v2 on v0

--- a/solution.py
+++ b/solution.py
@@ -134,12 +134,9 @@
     chosen = jnp.where(spot == wanted, 1.0, 0.0).astype(BF16)
     copies[1].wait()
     blocks = blocks_of(bond_ref, slots // 2)
-    values = [jnp.concatenate([x[:, :feature]] * 2, axis=1) for x in blocks]
-    values += [jnp.concatenate([x[:, feature:]] * 2, axis=1) for x in blocks]
+    values = [x[:, :feature] for x in blocks] + [x[:, feature:] for x in blocks]
     packed = jnp.dot(chosen, jnp.concatenate(values, axis=0), preferred_element_type=F32)
-    packed = jnp.where(
-        left_lanes((9 * half, 2 * feature)), packed[: 9 * half], packed[9 * half :]
-    ).astype(BF16)
+    packed = jnp.concatenate([packed[: 9 * half], packed[9 * half :]], axis=1).astype(BF16)
     copies[2].wait()
     atom = atom_ref[0, 0]
     atom = jnp.concatenate([atom[: atoms // 2], atom[atoms // 2 :]], axis=1)
@@ -236,14 +233,15 @@
     bond_ref,
     *refs,
 ):
-    sources, results, held, sems = refs[:9], refs[9:21], refs[21:28], refs[28]
-    chosen_ref, own_ref, near_ref, far_weight_ref, mix_weight_ref, pair_weight_ref = results[:6]
-    hidden_weight_ref, out_weight_ref, atom_in_weight_ref, atom_out_weight_ref = results[6:10]
+    sources, results, held, sems = refs[:9], refs[9:22], refs[22:29], refs[29]
+    chosen_ref, right_ref, own_ref, near_ref = results[:4]
+    far_weight_ref, mix_weight_ref, pair_weight_ref, hidden_weight_ref = results[4:8]
+    out_weight_ref, atom_in_weight_ref, atom_out_weight_ref = results[8:11]
     bond_in_ref, bond_mix_ref, pair_ref, pair_hidden_ref, pair_out_ref = held[:5]
     atom_in_ref, atom_out_ref = held[5:]
     copies = [
         pltpu.make_async_copy(source, target, sems.at[k])
-        for k, (source, target) in enumerate(zip(sources, held + results[10:]))
+        for k, (source, target) in enumerate(zip(sources, held + results[11:]))
     ]
     for copy in copies:
         copy.start()
@@ -271,11 +269,11 @@
         place.append(jnp.sum(jnp.where(inside, 1.0, 0.0), axis=0, keepdims=True))
     place = jnp.concatenate(place, axis=1).astype(jnp.int32)
     half, tall = CAP // 2, atoms // 2
-    bond_spot = 9 * half * quotient(place, half) + half * code + remainder(place, half)
-    atom_spot = 9 * CAP + 9 * tall * quotient(far_atom, tall) + tall * code
-    atom_spot = column(atom_spot + remainder(far_atom, tall))
-    bond_spot = column(bond_spot)
-    total = 9 * CAP + 9 * atoms
+    bond_spot = column(half * code + remainder(place, half))
+    atom_spot = column(9 * half + tall * code + remainder(far_atom, tall))
+    right = (column(quotient(place, half)), column(quotient(far_atom, tall)))
+    right_ref[...] = jnp.where(left_lanes((bonds, 128)), right[0], right[1])
+    total = 9 * half + 9 * tall
     for start in range(0, total, 128):
         width = min(128, total - start)
         spot = lax.broadcasted_iota(jnp.int32, (bonds, 128), 1).astype(F32) + float(start)
@@ -330,6 +328,7 @@
     three_ref,
     angular_ref,
     chosen_ref,
+    right_ref,
     own_ref,
     near_ref,
     far_weight_ref,
@@ -345,105 +344,98 @@
     bond_result_ref,
     first_ref,
     second_ref,
-    pair_ref,
-    total_ref,
     sems,
 ):
     slots, pairs, _ = angular_ref.shape
     bonds = 2 * pairs
     atoms = bonds // slots
     feature = own_ref.shape[1] // 2
+    width = 2 * feature
     half = CAP // 2
     near_refs = (own_rows_ref, one_ref, two_ref)
     away_refs = (three_ref, four_ref)
     sent = [ref[:half] for ref in near_refs] + [ref[: 3 * half] for ref in away_refs]
     sent = jnp.concatenate(sent, axis=0)
     sent_atom = jnp.concatenate([ref[3 * half :] for ref in near_refs + away_refs], axis=0)
-    blank = jnp.zeros((9 * half, feature), BF16)
+    blank = jnp.zeros((sent.shape[0], feature), BF16)
     blank_atom = jnp.zeros((sent_atom.shape[0], feature), BF16)
     received = jnp.concatenate(
         [
-            jnp.concatenate([sent[:, :feature], blank], axis=1),
-            jnp.concatenate([sent[:, feature:], blank], axis=1),
-            jnp.concatenate([blank_atom, sent_atom[:, :feature]], axis=1),
-            jnp.concatenate([blank_atom, sent_atom[:, feature:]], axis=1),
+            jnp.concatenate([sent[:, :feature], blank, sent[:, feature:], blank], axis=1),
+            jnp.concatenate(
+                [blank_atom, sent_atom[:, :feature], blank_atom, sent_atom[:, feature:]], axis=1
+            ),
         ],
         axis=0,
     )
     far = jnp.dot(chosen_ref[...], received, preferred_element_type=F32)
+    far = jnp.where(right_ref[...] > 0.0, far[:, width:], far[:, :width])
     incoming = near_ref[...] + jnp.dot(
         far.astype(BF16), far_weight_ref[...], preferred_element_type=F32
     )
     hidden = doubled_gate(incoming).astype(BF16)
     mixed = jnp.dot(hidden, mix_weight_ref[...], preferred_element_type=F32)
-    old = jnp.where(left_lanes((bonds, 2 * feature)), far, own_ref[...].astype(F32))
+    old = jnp.where(left_lanes((bonds, width)), far, own_ref[...].astype(F32))
     new = (old + mixed).astype(BF16).astype(F32)
     average = ((new + pltpu.roll(new, feature, 1)) * 0.5).astype(BF16).astype(F32)
     even, odd = average[:pairs], average[pairs:]
-    left = left_lanes((pairs, 2 * feature))
+    left = left_lanes((pairs, width))
     packed = jnp.where(left, even, odd)
     shifted = jnp.where(left, odd, jnp.concatenate([even[atoms:], even[:atoms]], axis=0))
-    width = 4 * feature
     projected = jnp.dot(packed.astype(BF16), pair_weight_ref[...], preferred_element_type=F32)
-    first_ref[...] = projected[:, :width]
-    second = jnp.dot(shifted.astype(BF16), pair_weight_ref[:, width:], preferred_element_type=F32)
-    for copy in range(2):
-        second_ref[0, copy * pairs : (copy + 1) * pairs] = projected[:, width:]
-        second_ref[1, copy * pairs : (copy + 1) * pairs] = second
+    first_ref[...] = projected[:, : 2 * width]
+    second_ref[0] = projected[:, 2 * width :]
+    second_ref[1] = jnp.dot(
+        shifted.astype(BF16), pair_weight_ref[:, 2 * width :], preferred_element_type=F32
+    )
     hidden_weight = hidden_weight_ref[...]
     height = pairs // 2
-    steps = [(parity, start) for start in (0, height) for parity in (0, 1)]
-
-    def first_gates(turn):
-        for step, (parity, start) in enumerate(steps):
-            offset = pl.multiple_of(start + turn * atoms, atoms)
-            mixture = angular_ref[2 * turn + parity, pl.ds(start, height)] + (
-                first_ref[pl.ds(start, height)] + second_ref[parity, pl.ds(offset, height)]
+    pooled = jnp.zeros((atoms, width), F32)
+    copies = []
+    for part, start in enumerate(range(0, pairs, height)):
+        total = jnp.zeros((height, width), F32)
+        for diagonal in range(slots):
+            offset = start + diagonal // 2 * atoms
+            pieces = [
+                second_ref[diagonal % 2, pl.ds((offset + k) % pairs, atoms)]
+                for k in range(0, height, atoms)
+            ]
+            mixture = angular_ref[diagonal, pl.ds(start, height)] + (
+                first_ref[pl.ds(start, height)] + jnp.concatenate(pieces, axis=0)
             )
-            pair_ref[step] = doubled_gate(mixture).astype(BF16)
-
-    def second_gates():
-        gates = [
-            doubled_gate(jnp.dot(pair_ref[k], hidden_weight, preferred_element_type=F32))
-            for k in range(len(steps))
-        ]
-        for part, start in enumerate((0, height)):
-            total_ref[pl.ds(start, height)] += gates[2 * part] + gates[2 * part + 1]
-
-    def body(turn, carry):
-        second_gates()
-        first_gates(turn)
-        return carry
-
-    total_ref[...] = jnp.zeros_like(total_ref)
-    first_gates(0)
-    lax.fori_loop(1, slots // 2, body, 0)
-    second_gates()
-    pair_sum = total_ref[...].astype(BF16)
-    bond_out = packed + jnp.dot(pair_sum, out_weight_ref[...], preferred_element_type=F32)
-    bond_out = bond_out.astype(BF16)
-    for k in range(slots // 2):
-        bond_result_ref[0, 0, :, 2 * k * feature : 2 * (k + 1) * feature] = bond_out[
-            k * atoms : (k + 1) * atoms
-        ]
-    bond_copy = pltpu.make_async_copy(bond_result_ref, bond_result_hbm, sems.at[0])
-    bond_copy.start()
-    pooled = jnp.zeros((atoms, 2 * feature), F32)
-    for k in range(slots // 2):
-        pooled = pooled + bond_out[k * atoms : (k + 1) * atoms].astype(F32)
+            pair = doubled_gate(mixture.astype(BF16))
+            second = jnp.dot(pair, hidden_weight, preferred_element_type=F32)
+            total = total + doubled_gate(second.astype(BF16)).astype(F32)
+        bond_out = packed[start : start + height] + jnp.dot(
+            total.astype(BF16), out_weight_ref[...], preferred_element_type=F32
+        )
+        bond_out = bond_out.astype(BF16)
+        for k in range(height // atoms):
+            place = (start // atoms + k) * width
+            rows = bond_out[k * atoms : (k + 1) * atoms]
+            bond_result_ref[0, 0, :, place : place + width] = rows
+            pooled = pooled + rows.astype(F32)
+        columns = pl.ds(start // atoms * width, height // atoms * width)
+        copies.append(
+            pltpu.make_async_copy(
+                bond_result_ref.at[0, 0, :, columns],
+                bond_result_hbm.at[0, 0, :, columns],
+                sems.at[part],
+            )
+        )
+        copies[-1].start()
     pooled = (pooled + pltpu.roll(pooled, feature, 1)) * (1.0 / slots)
     atom = own_ref[0:atoms].astype(F32)
-    left = left_lanes((atoms, 2 * feature))
-    joined = jnp.where(left, atom, pooled).astype(BF16)
+    joined = jnp.where(left_lanes((atoms, width)), atom, pooled).astype(BF16)
     atom_hidden = doubled_gate(
         jnp.dot(joined, atom_in_weight_ref[...], preferred_element_type=F32)
     ).astype(BF16)
     atom_new = atom + jnp.dot(atom_hidden, atom_out_weight_ref[...], preferred_element_type=F32)
     atom_result_ref[0, 0] = atom_new[:, :feature].astype(BF16)
-    atom_copy = pltpu.make_async_copy(atom_result_ref, atom_result_hbm, sems.at[1])
-    atom_copy.start()
-    bond_copy.wait()
-    atom_copy.wait()
+    copies.append(pltpu.make_async_copy(atom_result_ref, atom_result_hbm, sems.at[2]))
+    copies[-1].start()
+    for copy in copies:
+        copy.wait()
 
 
 def per_device(
@@ -497,7 +489,8 @@
     *prepared, bond_dirs, angle_weight = pl.pallas_call(
         functools.partial(prepare_kernel, extents, paired),
         out_shape=(
-            shaped((bonds, 9 * CAP + 9 * atoms), BF16),
+            shaped((bonds, 9 * half + 9 * atoms // 2), BF16),
+            shaped((bonds, 2 * feature), F32),
             shaped((bonds, 2 * feature), BF16),
             shaped((bonds, 4 * feature), F32),
             shaped((2 * feature, 4 * feature), BF16),
@@ -511,7 +504,7 @@
             shaped(angle_weight.shape, BF16),
         ),
         in_specs=[vmem] * 3 + [hbm] * 9,
-        out_specs=(vmem,) * 12,
+        out_specs=(vmem,) * 13,
         scratch_shapes=[pltpu.VMEM(x.shape, BF16) for x in weights]
         + [pltpu.SemaphoreType.DMA((9,))],
         compiler_params=params,
@@ -541,21 +534,16 @@
     return pl.pallas_call(
         main_kernel,
         out_shape=(shaped(atom_feat.shape, BF16), shaped(bond_feat.shape, BF16)),
-        in_specs=[vmem] * 16,
+        in_specs=[vmem] * 17,
         out_specs=(hbm, hbm),
         scratch_shapes=[
             pltpu.VMEM(atom_feat.shape, BF16),
             pltpu.VMEM(bond_feat.shape, BF16),
             pltpu.VMEM((pairs, 4 * feature), F32),
-            pltpu.VMEM((2, 2 * pairs, 4 * feature), F32),
-            pltpu.VMEM((4, pairs // 2, 2 * feature), BF16),
-            pltpu.VMEM((pairs, 2 * feature), F32),
-            pltpu.SemaphoreType.DMA((2,)),
+            pltpu.VMEM((2, pairs, 4 * feature), F32),
+            pltpu.SemaphoreType.DMA((3,)),
         ],
         compiler_params=params,
-        cost_estimate=pl.CostEstimate(
-            flops=400 * 2**20, bytes_accessed=2**22, transcendentals=2**21
-        ),
         name="main",
     )(own, one, two, four, three, angular, *prepared)
 

time: 18.6 us -> 17.7 us (0.952)
  Pallas kernels: 9.04 us -> 8.13 us
    pallas_call x1, Pallas kernels: 4.33 us -> 3.42 us  [per_device(): pl.pallas_call(main_kernel, out_shape=(shaped(atom_feat.shape, BF16), sha...]
  transfers between devices with their start and end apart: 4 -> 4, of which waited for: 1 -> 1; matrix products, arithmetic and copies ran while one was open for 0% -> 0% of each run, Pallas kernels for 17% -> 18%
where the time goes in v2:
time: 17.7 us; the launch traced here: 17.5 us
  Pallas kernels  8.13 us (46%)
  starting transfers between devices  7.89 us (45%)
  between operations  0.7 us (4%)
  waiting for transfers between devices  0.68 us (4%)
    pallas_call x1, Pallas kernels, per_device(): pl.pallas_call(main_kernel, out_shape=(shaped(atom_feat.shape, BF16), sha...  3.42 us
    ppermute x1, starting transfers between devices, per_device(): four = lax.ppermute(forwarded(2), 'gy', second)  3.15 us
    ppermute x1, starting transfers between devices, per_device(): one = lax.ppermute(one, 'gx', first)  2.44 us
    pallas_call x1, Pallas kernels, per_device(): pl.pallas_call(functools.partial(prepare_kernel, extents, paired), out_sh...  1.85 us
    ppermute x1, starting transfers between devices, per_device(): three = lax.ppermute(forwarded(1), 'gy', first)  1.63 us
    pallas_call x1, Pallas kernels, per_device(): pl.pallas_call(functools.partial(pack_kernel, extents, paired), out_shape...  1.61 us
    pallas_call x1, Pallas kernels, per_device(): pl.pallas_call(functools.partial(angular_kernel, atoms), out_shape=shaped...  1.26 us
    ppermute x1, starting transfers between devices, per_device(): two = lax.ppermute(two, 'gx', second)  0.68 us
  transfers between devices with their start and end apart: 4, of which 1 were waited for; matrix products, arithmetic and copies ran while one was open for 0% of the time, Pallas kernels for 18%

profile of v2, /device:TPU:0, one launch (start us, length us, event | category | flops | bytes accessed | tf_op | source)
XLA Modules:
  0.0 17.5 jit_solution(14425722880307966815)
XLA Ops:
  0.6 1.6 %pack.1 = (bf16[112,128]{1,0:T(8,128)(2,1)S(1)}, bf16[112,128]{1,0:T(8,128)(2,1)S(1)}, bf16[112,128]{1,0:T(8,128)(2,1)S(1)}, s32[16,32]{1,0:T(8,128)S(1)}, bf16[...) custom-call(s32[16,32]{1,0:T(8,128)} %bitcast.3, bf16[1,1,32,64]{3,2,1,0:T(8,128)(2,1)} %atom_hbm.1, ...), custom_call_target="tpu_custom_call" | custom-call | tf_op jit(solution)/shard_map/pack/pallas_call | solution.py:475
  2.2 2.4 %collective-permute-start = (bf16[112,128]{1,0:T(8,128)(2,1)S(1)}, bf16[112,128]{1,0:T(8,128)(2,1)S(1)}, u32[]{:S(2)}, u32[]{:S(2)}) collective-permute-start(bf16[112,128]{1,0:T(8,128)(2,1)S(1)} %get-tuple-element.36), channel_id=1, source_target_pairs={{0,24},{8,16},{16,8},{24,0},{1,25},{9,17},{17,9},{25,1},{2,26},{10... | collective-permute-start | bytes 86024 | tf_op jit(solution)/shard_map/ppermute | solution.py:485
  4.7 0.7 %collective-permute-start.1 = (bf16[112,128]{1,0:T(8,128)(2,1)S(1)}, bf16[112,128]{1,0:T(8,128)(2,1)S(1)}, u32[]{:S(2)}, u32[]{:S(2)}) collective-permute-start(bf16[112,128]{1,0:T(8,128)(2,1)S(1)} %get-tuple-element.37), channel_id=1, source_target_pairs={{0,8},{8,0},{16,24},{24,16},{1,9},{9,1},{17,25},{25,17},{2,10},{10... | collective-permute-start | bytes 86024 | tf_op jit(solution)/shard_map/ppermute | solution.py:486
  5.4 1.8 %prepare.1 = (bf16[512,432]{1,0:T(8,128)(2,1)S(1)}, f32[512,128]{1,0:T(8,128)S(1)}, bf16[512,128]{1,0:T(8,128)(2,1)S(1)}, f32[512,256]{1,0:T(8,128)S(1)}, bf16[1...) custom-call(s32[16,32]{1,0:T(8,128)S(1)} %get-tuple-element.38.targe, ...), custom_call_target="tpu_custom_call" | custom-call | flops 67108864 | bytes 2097152 | tf_op jit(solution)/shard_map/prepare/pallas_call | solution.py:489
  7.2 0.0 collective-permute-done.one_ref
  7.2 0.0 collective-permute-done.1.two_ref
  7.3 1.6 %collective-permute-start.3 = (bf16[144,128]{1,0:T(8,128)(2,1)S(1)}, bf16[144,128]{1,0:T(8,128)(2,1)S(1)}, u32[]{:S(2)}, u32[]{:S(2)}) collective-permute-start(bf16[144,128]{1,0:T(8,128)(2,1)S(1)} %get-tuple-element.68), channel_id=1, source_target_pairs={{0,1},{1,2},{2,3},{3,4},{4,5},{5,6},{6,7},{7,0},{8,9},{9,10},{10,1... | collective-permute-start | bytes 110600 | tf_op jit(solution)/shard_map/ppermute | solution.py:521
  9.0 3.1 %collective-permute-start.2 = (bf16[144,128]{1,0:T(8,128)(2,1)S(1)}, bf16[144,128]{1,0:T(8,128)(2,1)S(1)}, u32[]{:S(2)}, u32[]{:S(2)}) collective-permute-start(bf16[144,128]{1,0:T(8,128)(2,1)S(1)} %get-tuple-element.69), channel_id=1, source_target_pairs={{1,0},{2,1},{3,2},{4,3},{5,4},{6,5},{7,6},{0,7},{9,8},{10,9},{11,1... | collective-permute-start | bytes 110600 | tf_op jit(solution)/shard_map/ppermute | solution.py:522
  12.1 1.3 %angular.1.angular_ref = f32[16,256,256]{2,1,0:T(8,128)S(1)} custom-call(f32[2,1,1,512]{3,2,1,0:T(1,128)S(1)} %get-tuple-element.55.dirs_ref, bf16[64,128]{1,0:T(8,128)(2,1)S(1)} %get-tuple-element.56.angle_ref), custom_call_target="tpu_custom_call" | custom-call | flops 268435456 | bytes 4194304 | tf_op jit(solution)/shard_map/angular/pallas_call | solution.py:523
  13.4 0.7 %collective-permute-done.3.three_ref = bf16[144,128]{1,0:T(8,128)(2,1)S(1)} collective-permute-done((bf16[144,128]{1,0:T(8,128)(2,1)S(1)}, bf16[144,128]{1,0:T(8,128)(2,1)S(1)}, u32[]{:S(2)}, u32[]{:S(2)}) %collective-permute-start.3) | collective-permute-done | bytes 36896 | tf_op jit(solution)/shard_map/ppermute | solution.py:521
  14.0 0.0 collective-permute-done.2.four_ref
  14.0 3.4 %main.1 = (bf16[1,1,32,64]{3,2,1,0:T(8,128)(2,1)}, bf16[1,1,32,1024]{3,2,1,0:T(8,128)(2,1)}) custom-call(bf16[112,128]{1,0:T(8,128)(2,1)S(1)} %get-tuple-element.52.own_rows_ref, bf16[112,128]{1,0:T(8,128)(2,1)S(1)} %collective-permute-done.one_ref, bf16[112,128]{1,0:T(8,128)(2,1)S(1)} %collective-permute-done.1.two_ref, ...), custom_call_target="tpu_custom_call" | custom-call | tf_op jit(solution)/shard_map/main/pallas_call | solution.py:534
  (6 shorter events, 0.1 us)
Async XLA Ops:
  2.2 5.0 %collective-permute-start = (bf16[112,128]{1,0:T(8,128)(2,1)S(1)}, bf16[112,128]{1,0:T(8,128)(2,1)S(1)}, u32[]{:S(2)}, u32[]{:S(2)}) collective-permute-start(bf16[112,128]{1,0:T(8,128)(2,1)S(1)} %get-tuple-element.36), channel_id=1, source_target_pairs={{0,24},{8,16},{16,8},{24,0},{1,25},{9,17},{17,9},{25,1},{2,26},{10... | collective-permute-start | bytes 86024 | tf_op jit(solution)/shard_map/ppermute | solution.py:485
  4.7 2.5 %collective-permute-start.1 = (bf16[112,128]{1,0:T(8,128)(2,1)S(1)}, bf16[112,128]{1,0:T(8,128)(2,1)S(1)}, u32[]{:S(2)}, u32[]{:S(2)}) collective-permute-start(bf16[112,128]{1,0:T(8,128)(2,1)S(1)} %get-tuple-element.37), channel_id=1, source_target_pairs={{0,8},{8,0},{16,24},{24,16},{1,9},{9,1},{17,25},{25,17},{2,10},{10... | collective-permute-start | bytes 86024 | tf_op jit(solution)/shard_map/ppermute | solution.py:486
  7.3 6.7 %collective-permute-start.3 = (bf16[144,128]{1,0:T(8,128)(2,1)S(1)}, bf16[144,128]{1,0:T(8,128)(2,1)S(1)}, u32[]{:S(2)}, u32[]{:S(2)}) collective-permute-start(bf16[144,128]{1,0:T(8,128)(2,1)S(1)} %get-tuple-element.68), channel_id=1, source_target_pairs={{0,1},{1,2},{2,3},{3,4},{4,5},{5,6},{6,7},{7,0},{8,9},{9,10},{10,1... | collective-permute-start | bytes 110600 | tf_op jit(solution)/shard_map/ppermute | solution.py:521
  9.0 5.1 %collective-permute-start.2 = (bf16[144,128]{1,0:T(8,128)(2,1)S(1)}, bf16[144,128]{1,0:T(8,128)(2,1)S(1)}, u32[]{:S(2)}, u32[]{:S(2)}) collective-permute-start(bf16[144,128]{1,0:T(8,128)(2,1)S(1)} %get-tuple-element.69), channel_id=1, source_target_pairs={{1,0},{2,1},{3,2},{4,3},{5,4},{6,5},{7,6},{0,7},{9,8},{10,9},{11,1... | collective-permute-start | bytes 110600 | tf_op jit(solution)/shard_map/ppermute | solution.py:522

commit v3 on v2

--- a/solution.py
+++ b/solution.py
@@ -344,6 +344,7 @@
     bond_result_ref,
     first_ref,
     second_ref,
+    pair_ref,
     sems,
 ):
     slots, pairs, _ = angular_ref.shape
@@ -388,42 +389,44 @@
     second_ref[1] = jnp.dot(
         shifted.astype(BF16), pair_weight_ref[:, 2 * width :], preferred_element_type=F32
     )
-    hidden_weight = hidden_weight_ref[...]
-    height = pairs // 2
+    group = 4
+
+    def first_gates(base):
+        for start in range(0, pairs, atoms):
+            here = first_ref[pl.ds(start, atoms)]
+            for diagonal in range(base, base + group):
+                there = (start + diagonal // 2 * atoms) % pairs
+                mixture = angular_ref[diagonal, pl.ds(start, atoms)] + (
+                    here + second_ref[diagonal % 2, pl.ds(there, atoms)]
+                )
+                pair_ref[pl.ds(diagonal * pairs + start, atoms)] = doubled_gate(mixture).astype(
+                    BF16
+                )
+
+    total = jnp.zeros((pairs, width), F32)
+    first_gates(0)
+    for base in range(0, slots, group):
+        second = jnp.dot(
+            pair_ref[pl.ds(base * pairs, group * pairs)],
+            hidden_weight_ref[...],
+            preferred_element_type=F32,
+        )
+        if base + group < slots:
+            first_gates(base + group)
+        gates = doubled_gate(second)
+        for k in range(group):
+            total = total + gates[k * pairs : (k + 1) * pairs]
+    bond_out = packed + jnp.dot(
+        total.astype(BF16), out_weight_ref[...], preferred_element_type=F32
+    )
+    bond_out = bond_out.astype(BF16)
     pooled = jnp.zeros((atoms, width), F32)
-    copies = []
-    for part, start in enumerate(range(0, pairs, height)):
-        total = jnp.zeros((height, width), F32)
-        for diagonal in range(slots):
-            offset = start + diagonal // 2 * atoms
-            pieces = [
-                second_ref[diagonal % 2, pl.ds((offset + k) % pairs, atoms)]
-                for k in range(0, height, atoms)
-            ]
-            mixture = angular_ref[diagonal, pl.ds(start, height)] + (
-                first_ref[pl.ds(start, height)] + jnp.concatenate(pieces, axis=0)
-            )
-            pair = doubled_gate(mixture.astype(BF16))
-            second = jnp.dot(pair, hidden_weight, preferred_element_type=F32)
-            total = total + doubled_gate(second.astype(BF16)).astype(F32)
-        bond_out = packed[start : start + height] + jnp.dot(
-            total.astype(BF16), out_weight_ref[...], preferred_element_type=F32
-        )
-        bond_out = bond_out.astype(BF16)
-        for k in range(height // atoms):
-            place = (start // atoms + k) * width
-            rows = bond_out[k * atoms : (k + 1) * atoms]
-            bond_result_ref[0, 0, :, place : place + width] = rows
-            pooled = pooled + rows.astype(F32)
-        columns = pl.ds(start // atoms * width, height // atoms * width)
-        copies.append(
-            pltpu.make_async_copy(
-                bond_result_ref.at[0, 0, :, columns],
-                bond_result_hbm.at[0, 0, :, columns],
-                sems.at[part],
-            )
-        )
-        copies[-1].start()
+    for k in range(slots // 2):
+        rows = bond_out[k * atoms : (k + 1) * atoms]
+        bond_result_ref[0, 0, :, k * width : (k + 1) * width] = rows
+        pooled = pooled + rows.astype(F32)
+    copies = [pltpu.make_async_copy(bond_result_ref, bond_result_hbm, sems.at[0])]
+    copies[0].start()
     pooled = (pooled + pltpu.roll(pooled, feature, 1)) * (1.0 / slots)
     atom = own_ref[0:atoms].astype(F32)
     joined = jnp.where(left_lanes((atoms, width)), atom, pooled).astype(BF16)
@@ -432,7 +435,7 @@
     ).astype(BF16)
     atom_new = atom + jnp.dot(atom_hidden, atom_out_weight_ref[...], preferred_element_type=F32)
     atom_result_ref[0, 0] = atom_new[:, :feature].astype(BF16)
-    copies.append(pltpu.make_async_copy(atom_result_ref, atom_result_hbm, sems.at[2]))
+    copies.append(pltpu.make_async_copy(atom_result_ref, atom_result_hbm, sems.at[1]))
     copies[-1].start()
     for copy in copies:
         copy.wait()
@@ -541,7 +544,8 @@
             pltpu.VMEM(bond_feat.shape, BF16),
             pltpu.VMEM((pairs, 4 * feature), F32),
             pltpu.VMEM((2, pairs, 4 * feature), F32),
-            pltpu.SemaphoreType.DMA((3,)),
+            pltpu.VMEM((slots * pairs, 2 * feature), BF16),
+            pltpu.SemaphoreType.DMA((2,)),
         ],
         compiler_params=params,
         name="main",

time: 17.7 us -> 17.7 us (level)
  no operation moved by 1% of the time
where the time goes in v3:
time: 17.7 us; the launch traced here: 17.4 us
  Pallas kernels  8.09 us (46%)
  starting transfers between devices  7.89 us (45%)
  between operations  0.7 us (4%)
  waiting for transfers between devices  0.68 us (4%)
    pallas_call x1, Pallas kernels, per_device(): pl.pallas_call(main_kernel, out_shape=(shaped(atom_feat.shape, BF16), sha...  3.37 us
    ppermute x1, starting transfers between devices, per_device(): four = lax.ppermute(forwarded(2), 'gy', second)  3.15 us
    ppermute x1, starting transfers between devices, per_device(): one = lax.ppermute(one, 'gx', first)  2.44 us
    pallas_call x1, Pallas kernels, per_device(): pl.pallas_call(functools.partial(prepare_kernel, extents, paired), out_sh...  1.85 us
    ppermute x1, starting transfers between devices, per_device(): three = lax.ppermute(forwarded(1), 'gy', first)  1.63 us
    pallas_call x1, Pallas kernels, per_device(): pl.pallas_call(functools.partial(pack_kernel, extents, paired), out_shape...  1.61 us
    pallas_call x1, Pallas kernels, per_device(): pl.pallas_call(functools.partial(angular_kernel, atoms), out_shape=shaped...  1.26 us
    ppermute x1, starting transfers between devices, per_device(): two = lax.ppermute(two, 'gx', second)  0.68 us
  transfers between devices with their start and end apart: 4, of which 1 were waited for; matrix products, arithmetic and copies ran while one was open for 0% of the time, Pallas kernels for 18%

profile of v3, /device:TPU:0, one launch (start us, length us, event | category | flops | bytes accessed | tf_op | source)
XLA Modules:
  0.0 17.4 jit_solution(15466460821744993277)
XLA Ops:
  0.6 1.6 %pack.1 = (bf16[112,128]{1,0:T(8,128)(2,1)S(1)}, bf16[112,128]{1,0:T(8,128)(2,1)S(1)}, bf16[112,128]{1,0:T(8,128)(2,1)S(1)}, s32[16,32]{1,0:T(8,128)S(1)}, bf16[...) custom-call(s32[16,32]{1,0:T(8,128)} %bitcast.3, bf16[1,1,32,64]{3,2,1,0:T(8,128)(2,1)} %atom_hbm.1, ...), custom_call_target="tpu_custom_call" | custom-call | tf_op jit(solution)/shard_map/pack/pallas_call | solution.py:478
  2.2 2.4 %collective-permute-start = (bf16[112,128]{1,0:T(8,128)(2,1)S(1)}, bf16[112,128]{1,0:T(8,128)(2,1)S(1)}, u32[]{:S(2)}, u32[]{:S(2)}) collective-permute-start(bf16[112,128]{1,0:T(8,128)(2,1)S(1)} %get-tuple-element.36), channel_id=1, source_target_pairs={{0,24},{8,16},{16,8},{24,0},{1,25},{9,17},{17,9},{25,1},{2,26},{10... | collective-permute-start | bytes 86024 | tf_op jit(solution)/shard_map/ppermute | solution.py:488
  4.7 0.7 %collective-permute-start.1 = (bf16[112,128]{1,0:T(8,128)(2,1)S(1)}, bf16[112,128]{1,0:T(8,128)(2,1)S(1)}, u32[]{:S(2)}, u32[]{:S(2)}) collective-permute-start(bf16[112,128]{1,0:T(8,128)(2,1)S(1)} %get-tuple-element.37), channel_id=1, source_target_pairs={{0,8},{8,0},{16,24},{24,16},{1,9},{9,1},{17,25},{25,17},{2,10},{10... | collective-permute-start | bytes 86024 | tf_op jit(solution)/shard_map/ppermute | solution.py:489
  5.4 1.8 %prepare.1 = (bf16[512,432]{1,0:T(8,128)(2,1)S(1)}, f32[512,128]{1,0:T(8,128)S(1)}, bf16[512,128]{1,0:T(8,128)(2,1)S(1)}, f32[512,256]{1,0:T(8,128)S(1)}, bf16[1...) custom-call(s32[16,32]{1,0:T(8,128)S(1)} %get-tuple-element.38.targe, ...), custom_call_target="tpu_custom_call" | custom-call | flops 67108864 | bytes 2097152 | tf_op jit(solution)/shard_map/prepare/pallas_call | solution.py:492
  7.2 0.0 collective-permute-done.one_ref
  7.2 0.0 collective-permute-done.1.two_ref
  7.3 1.6 %collective-permute-start.3 = (bf16[144,128]{1,0:T(8,128)(2,1)S(1)}, bf16[144,128]{1,0:T(8,128)(2,1)S(1)}, u32[]{:S(2)}, u32[]{:S(2)}) collective-permute-start(bf16[144,128]{1,0:T(8,128)(2,1)S(1)} %get-tuple-element.68), channel_id=1, source_target_pairs={{0,1},{1,2},{2,3},{3,4},{4,5},{5,6},{6,7},{7,0},{8,9},{9,10},{10,1... | collective-permute-start | bytes 110600 | tf_op jit(solution)/shard_map/ppermute | solution.py:524
  9.0 3.1 %collective-permute-start.2 = (bf16[144,128]{1,0:T(8,128)(2,1)S(1)}, bf16[144,128]{1,0:T(8,128)(2,1)S(1)}, u32[]{:S(2)}, u32[]{:S(2)}) collective-permute-start(bf16[144,128]{1,0:T(8,128)(2,1)S(1)} %get-tuple-element.69), channel_id=1, source_target_pairs={{1,0},{2,1},{3,2},{4,3},{5,4},{6,5},{7,6},{0,7},{9,8},{10,9},{11,1... | collective-permute-start | bytes 110600 | tf_op jit(solution)/shard_map/ppermute | solution.py:525
  12.1 1.3 %angular.1.angular_ref = f32[16,256,256]{2,1,0:T(8,128)S(1)} custom-call(f32[2,1,1,512]{3,2,1,0:T(1,128)S(1)} %get-tuple-element.55.dirs_ref, bf16[64,128]{1,0:T(8,128)(2,1)S(1)} %get-tuple-element.56.angle_ref), custom_call_target="tpu_custom_call" | custom-call | flops 268435456 | bytes 4194304 | tf_op jit(solution)/shard_map/angular/pallas_call | solution.py:526
  13.4 0.7 %collective-permute-done.3.three_ref = bf16[144,128]{1,0:T(8,128)(2,1)S(1)} collective-permute-done((bf16[144,128]{1,0:T(8,128)(2,1)S(1)}, bf16[144,128]{1,0:T(8,128)(2,1)S(1)}, u32[]{:S(2)}, u32[]{:S(2)}) %collective-permute-start.3) | collective-permute-done | bytes 36896 | tf_op jit(solution)/shard_map/ppermute | solution.py:524
  14.0 0.0 collective-permute-done.2.four_ref
  14.0 3.4 %main.1 = (bf16[1,1,32,64]{3,2,1,0:T(8,128)(2,1)}, bf16[1,1,32,1024]{3,2,1,0:T(8,128)(2,1)}) custom-call(bf16[112,128]{1,0:T(8,128)(2,1)S(1)} %get-tuple-element.52.own_rows_ref, bf16[112,128]{1,0:T(8,128)(2,1)S(1)} %collective-permute-done.one_ref, bf16[112,128]{1,0:T(8,128)(2,1)S(1)} %collective-permute-done.1.two_ref, ...), custom_call_target="tpu_custom_call" | custom-call | tf_op jit(solution)/shard_map/main/pallas_call | solution.py:537
  (6 shorter events, 0.1 us)
Async XLA Ops:
  2.2 5.0 %collective-permute-start = (bf16[112,128]{1,0:T(8,128)(2,1)S(1)}, bf16[112,128]{1,0:T(8,128)(2,1)S(1)}, u32[]{:S(2)}, u32[]{:S(2)}) collective-permute-start(bf16[112,128]{1,0:T(8,128)(2,1)S(1)} %get-tuple-element.36), channel_id=1, source_target_pairs={{0,24},{8,16},{16,8},{24,0},{1,25},{9,17},{17,9},{25,1},{2,26},{10... | collective-permute-start | bytes 86024 | tf_op jit(solution)/shard_map/ppermute | solution.py:488
  4.7 2.5 %collective-permute-start.1 = (bf16[112,128]{1,0:T(8,128)(2,1)S(1)}, bf16[112,128]{1,0:T(8,128)(2,1)S(1)}, u32[]{:S(2)}, u32[]{:S(2)}) collective-permute-start(bf16[112,128]{1,0:T(8,128)(2,1)S(1)} %get-tuple-element.37), channel_id=1, source_target_pairs={{0,8},{8,0},{16,24},{24,16},{1,9},{9,1},{17,25},{25,17},{2,10},{10... | collective-permute-start | bytes 86024 | tf_op jit(solution)/shard_map/ppermute | solution.py:489
  7.3 6.7 %collective-permute-start.3 = (bf16[144,128]{1,0:T(8,128)(2,1)S(1)}, bf16[144,128]{1,0:T(8,128)(2,1)S(1)}, u32[]{:S(2)}, u32[]{:S(2)}) collective-permute-start(bf16[144,128]{1,0:T(8,128)(2,1)S(1)} %get-tuple-element.68), channel_id=1, source_target_pairs={{0,1},{1,2},{2,3},{3,4},{4,5},{5,6},{6,7},{7,0},{8,9},{9,10},{10,1... | collective-permute-start | bytes 110600 | tf_op jit(solution)/shard_map/ppermute | solution.py:524
  9.0 5.1 %collective-permute-start.2 = (bf16[144,128]{1,0:T(8,128)(2,1)S(1)}, bf16[144,128]{1,0:T(8,128)(2,1)S(1)}, u32[]{:S(2)}, u32[]{:S(2)}) collective-permute-start(bf16[144,128]{1,0:T(8,128)(2,1)S(1)} %get-tuple-element.69), channel_id=1, source_target_pairs={{1,0},{2,1},{3,2},{4,3},{5,4},{6,5},{7,6},{0,7},{9,8},{10,9},{11,1... | collective-permute-start | bytes 110600 | tf_op jit(solution)/shard_map/ppermute | solution.py:525

commit v4 on v3

--- a/solution.py
+++ b/solution.py
@@ -399,8 +399,8 @@
                 mixture = angular_ref[diagonal, pl.ds(start, atoms)] + (
                     here + second_ref[diagonal % 2, pl.ds(there, atoms)]
                 )
-                pair_ref[pl.ds(diagonal * pairs + start, atoms)] = doubled_gate(mixture).astype(
-                    BF16
+                pair_ref[pl.ds(diagonal * pairs + start, atoms)] = doubled_gate(
+                    mixture.astype(BF16)
                 )
 
     total = jnp.zeros((pairs, width), F32)
@@ -413,9 +413,9 @@
         )
         if base + group < slots:
             first_gates(base + group)
-        gates = doubled_gate(second)
+        gates = doubled_gate(second.astype(BF16))
         for k in range(group):
-            total = total + gates[k * pairs : (k + 1) * pairs]
+            total = total + gates[k * pairs : (k + 1) * pairs].astype(F32)
     bond_out = packed + jnp.dot(
         total.astype(BF16), out_weight_ref[...], preferred_element_type=F32
     )

time: 17.7 us -> 17.7 us (level)
  no operation moved by 1% of the time
where the time goes in v4:
time: 17.7 us; the launch traced here: 17.4 us
  Pallas kernels  8.1 us (46%)
  starting transfers between devices  7.89 us (45%)
  between operations  0.7 us (4%)
  waiting for transfers between devices  0.68 us (4%)
    pallas_call x1, Pallas kernels, per_device(): pl.pallas_call(main_kernel, out_shape=(shaped(atom_feat.shape, BF16), sha...  3.38 us
    ppermute x1, starting transfers between devices, per_device(): four = lax.ppermute(forwarded(2), 'gy', second)  3.15 us
    ppermute x1, starting transfers between devices, per_device(): one = lax.ppermute(one, 'gx', first)  2.44 us
    pallas_call x1, Pallas kernels, per_device(): pl.pallas_call(functools.partial(prepare_kernel, extents, paired), out_sh...  1.85 us
    ppermute x1, starting transfers between devices, per_device(): three = lax.ppermute(forwarded(1), 'gy', first)  1.63 us
    pallas_call x1, Pallas kernels, per_device(): pl.pallas_call(functools.partial(pack_kernel, extents, paired), out_shape...  1.61 us
    pallas_call x1, Pallas kernels, per_device(): pl.pallas_call(functools.partial(angular_kernel, atoms), out_shape=shaped...  1.26 us
    ppermute x1, starting transfers between devices, per_device(): two = lax.ppermute(two, 'gx', second)  0.68 us
  transfers between devices with their start and end apart: 4, of which 1 were waited for; matrix products, arithmetic and copies ran while one was open for 0% of the time, Pallas kernels for 18%

profile of v4, /device:TPU:0, one launch (start us, length us, event | category | flops | bytes accessed | tf_op | source)
XLA Modules:
  0.0 17.4 jit_solution(10760696746732314955)
XLA Ops:
  0.6 1.6 %pack.1 = (bf16[112,128]{1,0:T(8,128)(2,1)S(1)}, bf16[112,128]{1,0:T(8,128)(2,1)S(1)}, bf16[112,128]{1,0:T(8,128)(2,1)S(1)}, s32[16,32]{1,0:T(8,128)S(1)}, bf16[...) custom-call(s32[16,32]{1,0:T(8,128)} %bitcast.3, bf16[1,1,32,64]{3,2,1,0:T(8,128)(2,1)} %atom_hbm.1, ...), custom_call_target="tpu_custom_call" | custom-call | tf_op jit(solution)/shard_map/pack/pallas_call | solution.py:478
  2.2 2.4 %collective-permute-start = (bf16[112,128]{1,0:T(8,128)(2,1)S(1)}, bf16[112,128]{1,0:T(8,128)(2,1)S(1)}, u32[]{:S(2)}, u32[]{:S(2)}) collective-permute-start(bf16[112,128]{1,0:T(8,128)(2,1)S(1)} %get-tuple-element.36), channel_id=1, source_target_pairs={{0,24},{8,16},{16,8},{24,0},{1,25},{9,17},{17,9},{25,1},{2,26},{10... | collective-permute-start | bytes 86024 | tf_op jit(solution)/shard_map/ppermute | solution.py:488
  4.7 0.7 %collective-permute-start.1 = (bf16[112,128]{1,0:T(8,128)(2,1)S(1)}, bf16[112,128]{1,0:T(8,128)(2,1)S(1)}, u32[]{:S(2)}, u32[]{:S(2)}) collective-permute-start(bf16[112,128]{1,0:T(8,128)(2,1)S(1)} %get-tuple-element.37), channel_id=1, source_target_pairs={{0,8},{8,0},{16,24},{24,16},{1,9},{9,1},{17,25},{25,17},{2,10},{10... | collective-permute-start | bytes 86024 | tf_op jit(solution)/shard_map/ppermute | solution.py:489
  5.4 1.8 %prepare.1 = (bf16[512,432]{1,0:T(8,128)(2,1)S(1)}, f32[512,128]{1,0:T(8,128)S(1)}, bf16[512,128]{1,0:T(8,128)(2,1)S(1)}, f32[512,256]{1,0:T(8,128)S(1)}, bf16[1...) custom-call(s32[16,32]{1,0:T(8,128)S(1)} %get-tuple-element.38.targe, ...), custom_call_target="tpu_custom_call" | custom-call | flops 67108864 | bytes 2097152 | tf_op jit(solution)/shard_map/prepare/pallas_call | solution.py:492
  7.2 0.0 collective-permute-done.one_ref
  7.2 0.0 collective-permute-done.1.two_ref
  7.3 1.6 %collective-permute-start.3 = (bf16[144,128]{1,0:T(8,128)(2,1)S(1)}, bf16[144,128]{1,0:T(8,128)(2,1)S(1)}, u32[]{:S(2)}, u32[]{:S(2)}) collective-permute-start(bf16[144,128]{1,0:T(8,128)(2,1)S(1)} %get-tuple-element.68), channel_id=1, source_target_pairs={{0,1},{1,2},{2,3},{3,4},{4,5},{5,6},{6,7},{7,0},{8,9},{9,10},{10,1... | collective-permute-start | bytes 110600 | tf_op jit(solution)/shard_map/ppermute | solution.py:524
  9.0 3.1 %collective-permute-start.2 = (bf16[144,128]{1,0:T(8,128)(2,1)S(1)}, bf16[144,128]{1,0:T(8,128)(2,1)S(1)}, u32[]{:S(2)}, u32[]{:S(2)}) collective-permute-start(bf16[144,128]{1,0:T(8,128)(2,1)S(1)} %get-tuple-element.69), channel_id=1, source_target_pairs={{1,0},{2,1},{3,2},{4,3},{5,4},{6,5},{7,6},{0,7},{9,8},{10,9},{11,1... | collective-permute-start | bytes 110600 | tf_op jit(solution)/shard_map/ppermute | solution.py:525
  12.1 1.3 %angular.1.angular_ref = f32[16,256,256]{2,1,0:T(8,128)S(1)} custom-call(f32[2,1,1,512]{3,2,1,0:T(1,128)S(1)} %get-tuple-element.55.dirs_ref, bf16[64,128]{1,0:T(8,128)(2,1)S(1)} %get-tuple-element.56.angle_ref), custom_call_target="tpu_custom_call" | custom-call | flops 268435456 | bytes 4194304 | tf_op jit(solution)/shard_map/angular/pallas_call | solution.py:526
  13.4 0.7 %collective-permute-done.3.three_ref = bf16[144,128]{1,0:T(8,128)(2,1)S(1)} collective-permute-done((bf16[144,128]{1,0:T(8,128)(2,1)S(1)}, bf16[144,128]{1,0:T(8,128)(2,1)S(1)}, u32[]{:S(2)}, u32[]{:S(2)}) %collective-permute-start.3) | collective-permute-done | bytes 36896 | tf_op jit(solution)/shard_map/ppermute | solution.py:524
  14.0 0.0 collective-permute-done.2.four_ref
  14.0 3.4 %main.1 = (bf16[1,1,32,64]{3,2,1,0:T(8,128)(2,1)}, bf16[1,1,32,1024]{3,2,1,0:T(8,128)(2,1)}) custom-call(bf16[112,128]{1,0:T(8,128)(2,1)S(1)} %get-tuple-element.52.own_rows_ref, bf16[112,128]{1,0:T(8,128)(2,1)S(1)} %collective-permute-done.one_ref, bf16[112,128]{1,0:T(8,128)(2,1)S(1)} %collective-permute-done.1.two_ref, ...), custom_call_target="tpu_custom_call" | custom-call | tf_op jit(solution)/shard_map/main/pallas_call | solution.py:537
  (6 shorter events, 0.1 us)
Async XLA Ops:
  2.2 5.0 %collective-permute-start = (bf16[112,128]{1,0:T(8,128)(2,1)S(1)}, bf16[112,128]{1,0:T(8,128)(2,1)S(1)}, u32[]{:S(2)}, u32[]{:S(2)}) collective-permute-start(bf16[112,128]{1,0:T(8,128)(2,1)S(1)} %get-tuple-element.36), channel_id=1, source_target_pairs={{0,24},{8,16},{16,8},{24,0},{1,25},{9,17},{17,9},{25,1},{2,26},{10... | collective-permute-start | bytes 86024 | tf_op jit(solution)/shard_map/ppermute | solution.py:488
  4.7 2.5 %collective-permute-start.1 = (bf16[112,128]{1,0:T(8,128)(2,1)S(1)}, bf16[112,128]{1,0:T(8,128)(2,1)S(1)}, u32[]{:S(2)}, u32[]{:S(2)}) collective-permute-start(bf16[112,128]{1,0:T(8,128)(2,1)S(1)} %get-tuple-element.37), channel_id=1, source_target_pairs={{0,8},{8,0},{16,24},{24,16},{1,9},{9,1},{17,25},{25,17},{2,10},{10... | collective-permute-start | bytes 86024 | tf_op jit(solution)/shard_map/ppermute | solution.py:489
  7.3 6.7 %collective-permute-start.3 = (bf16[144,128]{1,0:T(8,128)(2,1)S(1)}, bf16[144,128]{1,0:T(8,128)(2,1)S(1)}, u32[]{:S(2)}, u32[]{:S(2)}) collective-permute-start(bf16[144,128]{1,0:T(8,128)(2,1)S(1)} %get-tuple-element.68), channel_id=1, source_target_pairs={{0,1},{1,2},{2,3},{3,4},{4,5},{5,6},{6,7},{7,0},{8,9},{9,10},{10,1... | collective-permute-start | bytes 110600 | tf_op jit(solution)/shard_map/ppermute | solution.py:524
  9.0 5.1 %collective-permute-start.2 = (bf16[144,128]{1,0:T(8,128)(2,1)S(1)}, bf16[144,128]{1,0:T(8,128)(2,1)S(1)}, u32[]{:S(2)}, u32[]{:S(2)}) collective-permute-start(bf16[144,128]{1,0:T(8,128)(2,1)S(1)} %get-tuple-element.69), channel_id=1, source_target_pairs={{1,0},{2,1},{3,2},{4,3},{5,4},{6,5},{7,6},{0,7},{9,8},{10,9},{11,1... | collective-permute-start | bytes 110600 | tf_op jit(solution)/shard_map/ppermute | solution.py:525

commit v5 on v3

--- a/solution.py
+++ b/solution.py
@@ -234,9 +234,9 @@
     *refs,
 ):
     sources, results, held, sems = refs[:9], refs[9:22], refs[22:29], refs[29]
-    chosen_ref, right_ref, own_ref, near_ref = results[:4]
-    far_weight_ref, mix_weight_ref, pair_weight_ref, hidden_weight_ref = results[4:8]
-    out_weight_ref, atom_in_weight_ref, atom_out_weight_ref = results[8:11]
+    chosen_ref, right_ref, own_ref = results[:3]
+    bond_weight_ref, mix_weight_ref, pair_weight_ref, hidden_weight_ref = results[3:7]
+    out_weight_ref, atom_in_weight_ref, sum_weight_ref, atom_out_weight_ref = results[7:11]
     bond_in_ref, bond_mix_ref, pair_ref, pair_hidden_ref, pair_out_ref = held[:5]
     atom_in_ref, atom_out_ref = held[5:]
     copies = [
@@ -292,11 +292,9 @@
     weight = bond_in_ref[...].astype(F32)
     source, other, bond_part = (weight[k * feature : (k + 1) * feature] for k in range(3))
     blank = jnp.zeros_like(source)
+    away = [crossed(bond_part, blank), crossed(source, other)]
     near = [crossed(other, source), crossed(blank, bond_part)]
-    near = (jnp.concatenate(near, axis=0) * 0.5).astype(BF16)
-    near_ref[...] = jnp.dot(own, near, preferred_element_type=F32)
-    away = [crossed(bond_part, blank), crossed(source, other)]
-    far_weight_ref[...] = (jnp.concatenate(away, axis=0) * 0.5).astype(BF16)
+    bond_weight_ref[...] = (jnp.concatenate(away + near, axis=0) * 0.5).astype(BF16)
     mix_weight_ref[...] = (diagonal_blocks(bond_mix_ref[...].astype(F32)) * 0.5).astype(BF16)
     weight = pair_ref[...].astype(F32) * 0.5
     pair_weight_ref[...] = jnp.concatenate(
@@ -305,7 +303,15 @@
     hidden_weight_ref[...] = (two_blocks(pair_hidden_ref[...].astype(F32)) * 0.25).astype(BF16)
     out_weight_ref[...] = (diagonal_blocks(pair_out_ref[...].astype(F32)) * 0.5).astype(BF16)
     weight = atom_in_ref[...].astype(F32) * 0.5
-    atom_in_weight_ref[...] = crossed(weight, jnp.zeros_like(weight)).astype(BF16)
+    weight = crossed(weight, jnp.zeros_like(weight))
+    mean = weight[feature:] * (1.0 / slots)
+    atom_in_weight_ref[...] = jnp.concatenate([weight[:feature], mean, mean], axis=0).astype(BF16)
+    folded = jnp.dot(
+        pair_out_ref[...], (mean * 0.5).astype(BF16), preferred_element_type=F32
+    )
+    high = folded.astype(BF16)
+    low = (folded - high.astype(F32)).astype(BF16)
+    sum_weight_ref[...] = jnp.concatenate([high, high, low, low], axis=0)
     weight = atom_out_ref[...].astype(F32) * 0.5
     blank = jnp.zeros_like(weight)
     weight = jnp.concatenate([weight, blank], axis=1)
@@ -330,13 +336,13 @@
     chosen_ref,
     right_ref,
     own_ref,
-    near_ref,
-    far_weight_ref,
+    bond_weight_ref,
     mix_weight_ref,
     pair_weight_ref,
     hidden_weight_ref,
     out_weight_ref,
     atom_in_weight_ref,
+    sum_weight_ref,
     atom_out_weight_ref,
     atom_result_hbm,
     bond_result_hbm,
@@ -371,12 +377,15 @@
     )
     far = jnp.dot(chosen_ref[...], received, preferred_element_type=F32)
     far = jnp.where(right_ref[...] > 0.0, far[:, width:], far[:, :width])
-    incoming = near_ref[...] + jnp.dot(
-        far.astype(BF16), far_weight_ref[...], preferred_element_type=F32
+    own = own_ref[...]
+    incoming = jnp.dot(
+        jnp.concatenate([far.astype(BF16), own], axis=1),
+        bond_weight_ref[...],
+        preferred_element_type=F32,
     )
     hidden = doubled_gate(incoming).astype(BF16)
     mixed = jnp.dot(hidden, mix_weight_ref[...], preferred_element_type=F32)
-    old = jnp.where(left_lanes((bonds, width)), far, own_ref[...].astype(F32))
+    old = jnp.where(left_lanes((bonds, width)), far, own.astype(F32))
     new = (old + mixed).astype(BF16).astype(F32)
     average = ((new + pltpu.roll(new, feature, 1)) * 0.5).astype(BF16).astype(F32)
     even, odd = average[:pairs], average[pairs:]
@@ -389,7 +398,7 @@
     second_ref[1] = jnp.dot(
         shifted.astype(BF16), pair_weight_ref[:, 2 * width :], preferred_element_type=F32
     )
-    group = 4
+    group = 2
 
     def first_gates(base):
         for start in range(0, pairs, atoms):
@@ -403,16 +412,28 @@
                     BF16
                 )
 
+    def summed(rows):
+        parts = [rows[k * atoms : (k + 1) * atoms] for k in range(slots // 2)]
+        while len(parts) > 1:
+            parts = [x + y for x, y in zip(parts[::2], parts[1::2])]
+        return parts[0]
+
+    atom = own[0:atoms]
+    atom_incoming = jnp.dot(
+        jnp.concatenate([atom[:, :feature], summed(packed).astype(BF16)], axis=1),
+        atom_in_weight_ref[...],
+        preferred_element_type=F32,
+    )
     total = jnp.zeros((pairs, width), F32)
     first_gates(0)
     for base in range(0, slots, group):
+        if base + group < slots:
+            first_gates(base + group)
         second = jnp.dot(
             pair_ref[pl.ds(base * pairs, group * pairs)],
             hidden_weight_ref[...],
             preferred_element_type=F32,
         )
-        if base + group < slots:
-            first_gates(base + group)
         gates = doubled_gate(second)
         for k in range(group):
             total = total + gates[k * pairs : (k + 1) * pairs]
@@ -420,20 +441,20 @@
         total.astype(BF16), out_weight_ref[...], preferred_element_type=F32
     )
     bond_out = bond_out.astype(BF16)
-    pooled = jnp.zeros((atoms, width), F32)
     for k in range(slots // 2):
-        rows = bond_out[k * atoms : (k + 1) * atoms]
-        bond_result_ref[0, 0, :, k * width : (k + 1) * width] = rows
-        pooled = pooled + rows.astype(F32)
+        bond_result_ref[0, 0, :, k * width : (k + 1) * width] = bond_out[
+            k * atoms : (k + 1) * atoms
+        ]
     copies = [pltpu.make_async_copy(bond_result_ref, bond_result_hbm, sems.at[0])]
     copies[0].start()
-    pooled = (pooled + pltpu.roll(pooled, feature, 1)) * (1.0 / slots)
-    atom = own_ref[0:atoms].astype(F32)
-    joined = jnp.where(left_lanes((atoms, width)), atom, pooled).astype(BF16)
-    atom_hidden = doubled_gate(
-        jnp.dot(joined, atom_in_weight_ref[...], preferred_element_type=F32)
-    ).astype(BF16)
-    atom_new = atom + jnp.dot(atom_hidden, atom_out_weight_ref[...], preferred_element_type=F32)
+    sums = summed(total).astype(BF16)
+    atom_incoming = atom_incoming + jnp.dot(
+        jnp.concatenate([sums, sums], axis=1), sum_weight_ref[...], preferred_element_type=F32
+    )
+    atom_hidden = doubled_gate(atom_incoming).astype(BF16)
+    atom_new = atom.astype(F32) + jnp.dot(
+        atom_hidden, atom_out_weight_ref[...], preferred_element_type=F32
+    )
     atom_result_ref[0, 0] = atom_new[:, :feature].astype(BF16)
     copies.append(pltpu.make_async_copy(atom_result_ref, atom_result_hbm, sems.at[1]))
     copies[-1].start()
@@ -495,13 +516,13 @@
             shaped((bonds, 9 * half + 9 * atoms // 2), BF16),
             shaped((bonds, 2 * feature), F32),
             shaped((bonds, 2 * feature), BF16),
-            shaped((bonds, 4 * feature), F32),
-            shaped((2 * feature, 4 * feature), BF16),
+            shaped((4 * feature, 4 * feature), BF16),
             shaped((2 * feature, 2 * feature), BF16),
             shaped((2 * feature, 8 * feature), BF16),
             shaped((2 * feature, 4 * feature), BF16),
             shaped((2 * feature, 2 * feature), BF16),
-            shaped((2 * feature, 4 * feature), BF16),
+            shaped((3 * feature, 4 * feature), BF16),
+            shaped((4 * feature, 4 * feature), BF16),
             shaped((2 * feature, 2 * feature), BF16),
             shaped(bond_dirs.shape, F32),
             shaped(angle_weight.shape, BF16),

time: 17.7 us -> 17.5 us (0.989)
  Pallas kernels: 8.09 us -> 7.91 us
where the time goes in v5:
time: 17.5 us; the launch traced here: 17.2 us
  starting transfers between devices  7.94 us (45%)
  Pallas kernels  7.91 us (45%)
  between operations  0.7 us (4%)
  waiting for transfers between devices  0.64 us (4%)
    pallas_call x1, Pallas kernels, per_device(): pl.pallas_call(main_kernel, out_shape=(shaped(atom_feat.shape, BF16), sha...  3.28 us
    ppermute x1, starting transfers between devices, per_device(): four = lax.ppermute(forwarded(2), 'gy', second)  3.11 us
    ppermute x1, starting transfers between devices, per_device(): one = lax.ppermute(one, 'gx', first)  2.44 us
    pallas_call x1, Pallas kernels, per_device(): pl.pallas_call(functools.partial(prepare_kernel, extents, paired), out_sh...  1.77 us
    ppermute x1, starting transfers between devices, per_device(): three = lax.ppermute(forwarded(1), 'gy', first)  1.71 us
    pallas_call x1, Pallas kernels, per_device(): pl.pallas_call(functools.partial(pack_kernel, extents, paired), out_shape...  1.61 us
    pallas_call x1, Pallas kernels, per_device(): pl.pallas_call(functools.partial(angular_kernel, atoms), out_shape=shaped...  1.26 us
    ppermute x1, starting transfers between devices, per_device(): two = lax.ppermute(two, 'gx', second)  0.68 us
  transfers between devices with their start and end apart: 4, of which 1 were waited for; matrix products, arithmetic and copies ran while one was open for 0% of the time, Pallas kernels for 18%

profile of v5, /device:TPU:0, one launch (start us, length us, event | category | flops | bytes accessed | tf_op | source)
XLA Modules:
  0.0 17.2 jit_solution(953635263691663569)
XLA Ops:
  0.6 1.6 %pack.1 = (bf16[112,128]{1,0:T(8,128)(2,1)S(1)}, bf16[112,128]{1,0:T(8,128)(2,1)S(1)}, bf16[112,128]{1,0:T(8,128)(2,1)S(1)}, s32[16,32]{1,0:T(8,128)S(1)}, bf16[...) custom-call(s32[16,32]{1,0:T(8,128)} %bitcast.3, bf16[1,1,32,64]{3,2,1,0:T(8,128)(2,1)} %atom_hbm.1, ...), custom_call_target="tpu_custom_call" | custom-call | tf_op jit(solution)/shard_map/pack/pallas_call | solution.py:499
  2.2 2.4 %collective-permute-start = (bf16[112,128]{1,0:T(8,128)(2,1)S(1)}, bf16[112,128]{1,0:T(8,128)(2,1)S(1)}, u32[]{:S(2)}, u32[]{:S(2)}) collective-permute-start(bf16[112,128]{1,0:T(8,128)(2,1)S(1)} %get-tuple-element.36), channel_id=1, source_target_pairs={{0,24},{8,16},{16,8},{24,0},{1,25},{9,17},{17,9},{25,1},{2,26},{10... | collective-permute-start | bytes 86024 | tf_op jit(solution)/shard_map/ppermute | solution.py:509
  4.7 0.7 %collective-permute-start.1 = (bf16[112,128]{1,0:T(8,128)(2,1)S(1)}, bf16[112,128]{1,0:T(8,128)(2,1)S(1)}, u32[]{:S(2)}, u32[]{:S(2)}) collective-permute-start(bf16[112,128]{1,0:T(8,128)(2,1)S(1)} %get-tuple-element.37), channel_id=1, source_target_pairs={{0,8},{8,0},{16,24},{24,16},{1,9},{9,1},{17,25},{25,17},{2,10},{10... | collective-permute-start | bytes 86024 | tf_op jit(solution)/shard_map/ppermute | solution.py:510
  5.4 1.8 %prepare.1 = (bf16[512,432]{1,0:T(8,128)(2,1)S(1)}, f32[512,128]{1,0:T(8,128)S(1)}, bf16[512,128]{1,0:T(8,128)(2,1)S(1)}, bf16[256,256]{1,0:T(8,128)(2,1)S(1)}, ...) custom-call(s32[16,32]{1,0:T(8,128)S(1)} %get-tuple-element.38.targe, ...), custom_call_target="tpu_custom_call" | custom-call | flops 67108864 | bytes 2097152 | tf_op jit(solution)/shard_map/prepare/pallas_call | solution.py:513
  7.1 0.0 collective-permute-done.one_ref
  7.2 0.0 collective-permute-done.1.two_ref
  7.2 1.7 %collective-permute-start.3 = (bf16[144,128]{1,0:T(8,128)(2,1)S(1)}, bf16[144,128]{1,0:T(8,128)(2,1)S(1)}, u32[]{:S(2)}, u32[]{:S(2)}) collective-permute-start(bf16[144,128]{1,0:T(8,128)(2,1)S(1)} %get-tuple-element.68), channel_id=1, source_target_pairs={{0,1},{1,2},{2,3},{3,4},{4,5},{5,6},{6,7},{7,0},{8,9},{9,10},{10,1... | collective-permute-start | bytes 110600 | tf_op jit(solution)/shard_map/ppermute | solution.py:545
  9.0 3.1 %collective-permute-start.2 = (bf16[144,128]{1,0:T(8,128)(2,1)S(1)}, bf16[144,128]{1,0:T(8,128)(2,1)S(1)}, u32[]{:S(2)}, u32[]{:S(2)}) collective-permute-start(bf16[144,128]{1,0:T(8,128)(2,1)S(1)} %get-tuple-element.69), channel_id=1, source_target_pairs={{1,0},{2,1},{3,2},{4,3},{5,4},{6,5},{7,6},{0,7},{9,8},{10,9},{11,1... | collective-permute-start | bytes 110600 | tf_op jit(solution)/shard_map/ppermute | solution.py:546
  12.1 1.3 %angular.1.angular_ref = f32[16,256,256]{2,1,0:T(8,128)S(1)} custom-call(f32[2,1,1,512]{3,2,1,0:T(1,128)S(1)} %get-tuple-element.55.dirs_ref, bf16[64,128]{1,0:T(8,128)(2,1)S(1)} %get-tuple-element.56.angle_ref), custom_call_target="tpu_custom_call" | custom-call | flops 268435456 | bytes 4194304 | tf_op jit(solution)/shard_map/angular/pallas_call | solution.py:547
  13.3 0.6 %collective-permute-done.3.three_ref = bf16[144,128]{1,0:T(8,128)(2,1)S(1)} collective-permute-done((bf16[144,128]{1,0:T(8,128)(2,1)S(1)}, bf16[144,128]{1,0:T(8,128)(2,1)S(1)}, u32[]{:S(2)}, u32[]{:S(2)}) %collective-permute-start.3) | collective-permute-done | bytes 36896 | tf_op jit(solution)/shard_map/ppermute | solution.py:545
  14.0 0.0 collective-permute-done.2.four_ref
  14.0 3.3 %main.1 = (bf16[1,1,32,64]{3,2,1,0:T(8,128)(2,1)}, bf16[1,1,32,1024]{3,2,1,0:T(8,128)(2,1)}) custom-call(bf16[112,128]{1,0:T(8,128)(2,1)S(1)} %get-tuple-element.52.own_rows_ref, bf16[112,128]{1,0:T(8,128)(2,1)S(1)} %collective-permute-done.one_ref, bf16[112,128]{1,0:T(8,128)(2,1)S(1)} %collective-permute-done.1.two_ref, ...), custom_call_target="tpu_custom_call" | custom-call | tf_op jit(solution)/shard_map/main/pallas_call | solution.py:558
  (6 shorter events, 0.1 us)
Async XLA Ops:
  2.2 4.9 %collective-permute-start = (bf16[112,128]{1,0:T(8,128)(2,1)S(1)}, bf16[112,128]{1,0:T(8,128)(2,1)S(1)}, u32[]{:S(2)}, u32[]{:S(2)}) collective-permute-start(bf16[112,128]{1,0:T(8,128)(2,1)S(1)} %get-tuple-element.36), channel_id=1, source_target_pairs={{0,24},{8,16},{16,8},{24,0},{1,25},{9,17},{17,9},{25,1},{2,26},{10... | collective-permute-start | bytes 86024 | tf_op jit(solution)/shard_map/ppermute | solution.py:509
  4.7 2.5 %collective-permute-start.1 = (bf16[112,128]{1,0:T(8,128)(2,1)S(1)}, bf16[112,128]{1,0:T(8,128)(2,1)S(1)}, u32[]{:S(2)}, u32[]{:S(2)}) collective-permute-start(bf16[112,128]{1,0:T(8,128)(2,1)S(1)} %get-tuple-element.37), channel_id=1, source_target_pairs={{0,8},{8,0},{16,24},{24,16},{1,9},{9,1},{17,25},{25,17},{2,10},{10... | collective-permute-start | bytes 86024 | tf_op jit(solution)/shard_map/ppermute | solution.py:510
  7.2 6.7 %collective-permute-start.3 = (bf16[144,128]{1,0:T(8,128)(2,1)S(1)}, bf16[144,128]{1,0:T(8,128)(2,1)S(1)}, u32[]{:S(2)}, u32[]{:S(2)}) collective-permute-start(bf16[144,128]{1,0:T(8,128)(2,1)S(1)} %get-tuple-element.68), channel_id=1, source_target_pairs={{0,1},{1,2},{2,3},{3,4},{4,5},{5,6},{6,7},{7,0},{8,9},{9,10},{10,1... | collective-permute-start | bytes 110600 | tf_op jit(solution)/shard_map/ppermute | solution.py:545
  9.0 5.0 %collective-permute-start.2 = (bf16[144,128]{1,0:T(8,128)(2,1)S(1)}, bf16[144,128]{1,0:T(8,128)(2,1)S(1)}, u32[]{:S(2)}, u32[]{:S(2)}) collective-permute-start(bf16[144,128]{1,0:T(8,128)(2,1)S(1)} %get-tuple-element.69), channel_id=1, source_target_pairs={{1,0},{2,1},{3,2},{4,3},{5,4},{6,5},{7,6},{0,7},{9,8},{10,9},{11,1... | collective-permute-start | bytes 110600 | tf_op jit(solution)/shard_map/ppermute | solution.py:546

commit v6 on v5

--- a/solution.py
+++ b/solution.py
@@ -88,9 +88,9 @@
     targets_hbm,
     atom_hbm,
     bond_hbm,
-    own_ref,
-    one_ref,
-    two_ref,
+    up_ref,
+    down_ref,
+    spot_ref,
     targets_ref,
     atom_ref,
     bond_ref,
@@ -110,7 +110,7 @@
     groups = bonds // lanes
     copies[0].wait()
     code_x, code_y = bond_codes(bond_row(targets_ref[...]), atoms, extents, paired, False)
-    code = 3 * code_x + code_y
+    code = 3 * code_y + code_x
     rows = lax.broadcasted_iota(jnp.int32, (16, lanes), 0)
     marks = [rows == code[:, g * lanes : (g + 1) * lanes] for g in range(groups)]
     stacked = jnp.concatenate([m.astype(F32) for m in marks], axis=0).astype(BF16)
@@ -129,20 +129,31 @@
     place = jnp.concatenate(place, axis=1).astype(jnp.int32)
     half = CAP // 2
     right = quotient(place, half)
-    wanted = 9 * half * right + place - half * right + half * code
-    spot = lax.broadcasted_iota(jnp.int32, (9 * CAP, bonds), 0)
+    spot = place - half * right + half * code
+    spot_ref[...] = jnp.where(code < 3, spot + 3 * half * right, -1)
+    wanted = jnp.where(code < 3, -1, spot - 3 * half + 6 * half * right)
+    copies[1].wait()
+    copies[2].wait()
+    packed = packed_rows(wanted, bond_ref, slots, 6 * half)
+    for k, ref in enumerate((up_ref, down_ref)):
+        ref[: 3 * half] = packed[3 * half * k : 3 * half * (k + 1)]
+        ref[3 * half :] = atom_rows(atom_ref)
+
+
+def packed_rows(wanted, bond_ref, slots, count):
+    spot = lax.broadcasted_iota(jnp.int32, (2 * count, wanted.shape[1]), 0)
     chosen = jnp.where(spot == wanted, 1.0, 0.0).astype(BF16)
-    copies[1].wait()
     blocks = blocks_of(bond_ref, slots // 2)
+    feature = blocks[0].shape[1] // 2
     values = [x[:, :feature] for x in blocks] + [x[:, feature:] for x in blocks]
     packed = jnp.dot(chosen, jnp.concatenate(values, axis=0), preferred_element_type=F32)
-    packed = jnp.concatenate([packed[: 9 * half], packed[9 * half :]], axis=1).astype(BF16)
-    copies[2].wait()
+    return jnp.concatenate([packed[:count], packed[count:]], axis=1).astype(BF16)
+
+
+def atom_rows(atom_ref):
     atom = atom_ref[0, 0]
-    atom = jnp.concatenate([atom[: atoms // 2], atom[atoms // 2 :]], axis=1)
-    for third, ref in enumerate((own_ref, one_ref, two_ref)):
-        ref[: 3 * half] = packed[3 * half * third : 3 * half * (third + 1)]
-        ref[3 * half :] = atom
+    half = atom.shape[0] // 2
+    return jnp.concatenate([atom[:half], atom[half:]], axis=1)
 
 
 def crossed(left, right):
@@ -228,29 +239,32 @@
 def prepare_kernel(
     extents,
     paired,
+    spot_ref,
     targets_ref,
     atom_ref,
     bond_ref,
     *refs,
 ):
-    sources, results, held, sems = refs[:9], refs[9:22], refs[22:29], refs[29]
-    chosen_ref, right_ref, own_ref = results[:3]
-    bond_weight_ref, mix_weight_ref, pair_weight_ref, hidden_weight_ref = results[3:7]
-    out_weight_ref, atom_in_weight_ref, sum_weight_ref, atom_out_weight_ref = results[7:11]
+    sources, results, held, sems = refs[:9], refs[9:23], refs[23:30], refs[30]
+    near_ref, chosen_ref, right_ref, own_ref = results[:4]
+    bond_weight_ref, mix_weight_ref, pair_weight_ref, hidden_weight_ref = results[4:8]
+    out_weight_ref, atom_in_weight_ref, sum_weight_ref, atom_out_weight_ref = results[8:12]
     bond_in_ref, bond_mix_ref, pair_ref, pair_hidden_ref, pair_out_ref = held[:5]
     atom_in_ref, atom_out_ref = held[5:]
     copies = [
         pltpu.make_async_copy(source, target, sems.at[k])
-        for k, (source, target) in enumerate(zip(sources, held + results[11:]))
+        for k, (source, target) in enumerate(zip(sources, held + results[12:]))
     ]
     for copy in copies:
         copy.start()
     atoms, feature = atom_ref.shape[2], atom_ref.shape[3]
     slots = targets_ref.shape[0]
     bonds = slots * atoms
+    near_ref[: 3 * CAP // 2] = packed_rows(spot_ref[...], bond_ref, slots, 3 * CAP // 2)
+    near_ref[3 * CAP // 2 :] = atom_rows(atom_ref)
     targets = bond_row(targets_ref[...])
     code_x, code_y = bond_codes(targets, atoms, extents, paired, True)
-    code = 3 * code_y + code_x
+    code = 3 * code_x + code_y
     bond = lax.broadcasted_iota(jnp.int32, (1, bonds), 1)
     far_slot = slots - 1 - slot_at(quotient(bond, atoms), slots)
     far_atom = remainder(targets, atoms)
@@ -327,11 +341,11 @@
 
 
 def main_kernel(
-    own_rows_ref,
+    near_ref,
+    up_ref,
+    down_ref,
+    two_ref,
     one_ref,
-    two_ref,
-    four_ref,
-    three_ref,
     angular_ref,
     chosen_ref,
     right_ref,
@@ -359,8 +373,8 @@
     feature = own_ref.shape[1] // 2
     width = 2 * feature
     half = CAP // 2
-    near_refs = (own_rows_ref, one_ref, two_ref)
-    away_refs = (three_ref, four_ref)
+    near_refs = (near_ref, up_ref, down_ref)
+    away_refs = (one_ref, two_ref)
     sent = [ref[:half] for ref in near_refs] + [ref[: 3 * half] for ref in away_refs]
     sent = jnp.concatenate(sent, axis=0)
     sent_atom = jnp.concatenate([ref[3 * half :] for ref in near_refs + away_refs], axis=0)
@@ -496,23 +510,25 @@
 
     payload = shaped((3 * half + atoms // 2, 2 * feature), BF16)
     inputs = (targets, atom_feat, bond_feat)
-    own, one, two, *held = pl.pallas_call(
+    up, down, *held = pl.pallas_call(
         functools.partial(pack_kernel, extents, paired),
-        out_shape=(payload,) * 3 + tuple(shaped(x.shape, x.dtype) for x in inputs),
+        out_shape=(payload, payload, shaped((1, bonds), jnp.int32))
+        + tuple(shaped(x.shape, x.dtype) for x in inputs),
         in_specs=[hbm] * 3,
         out_specs=(vmem,) * 6,
         scratch_shapes=[pltpu.SemaphoreType.DMA((3,))],
         compiler_params=params,
         name="pack",
     )(*in_hbm(inputs))
-    first, second = moves(extents[0], paired[0])
-    one = lax.ppermute(one, "gx", first)
-    two = lax.ppermute(two, "gx", second)
+    first, second = moves(extents[1], paired[1])
+    up = lax.ppermute(up, "gy", first)
+    down = lax.ppermute(down, "gy", second)
     weights = (bond_in_weight, bond_mix_weight, pair_weight, pair_hidden_weight)
     weights += (pair_out_weight, atom_in_weight, atom_out_weight)
-    *prepared, bond_dirs, angle_weight = pl.pallas_call(
+    near, *prepared, bond_dirs, angle_weight = pl.pallas_call(
         functools.partial(prepare_kernel, extents, paired),
         out_shape=(
+            payload,
             shaped((bonds, 9 * half + 9 * atoms // 2), BF16),
             shaped((bonds, 2 * feature), F32),
             shaped((bonds, 2 * feature), BF16),
@@ -527,23 +543,23 @@
             shaped(bond_dirs.shape, F32),
             shaped(angle_weight.shape, BF16),
         ),
-        in_specs=[vmem] * 3 + [hbm] * 9,
-        out_specs=(vmem,) * 13,
+        in_specs=[vmem] * 4 + [hbm] * 9,
+        out_specs=(vmem,) * 14,
         scratch_shapes=[pltpu.VMEM(x.shape, BF16) for x in weights]
         + [pltpu.SemaphoreType.DMA((9,))],
         compiler_params=params,
         cost_estimate=pl.CostEstimate(flops=64 * 2**20, bytes_accessed=2**21, transcendentals=0),
         name="prepare",
     )(*held, *in_hbm(weights + (bond_dirs, angle_weight)))
-    own, one, two, prepared = lax.optimization_barrier((own, one, two, prepared))
-    first, second = moves(extents[1], paired[1])
+    near, up, down, prepared = lax.optimization_barrier((near, up, down, prepared))
+    first, second = moves(extents[0], paired[0])
 
     def forwarded(block):
-        parts = [x[block * half : (block + 1) * half] for x in (own, one, two)]
-        return jnp.concatenate(parts + [x[3 * half :] for x in (own, one, two)], axis=0)
-
-    three = lax.ppermute(forwarded(1), "gy", first)
-    four = lax.ppermute(forwarded(2), "gy", second)
+        parts = [x[block * half : (block + 1) * half] for x in (near, up, down)]
+        return jnp.concatenate(parts + [x[3 * half :] for x in (near, up, down)], axis=0)
+
+    one = lax.ppermute(forwarded(1), "gx", first)
+    two = lax.ppermute(forwarded(2), "gx", second)
     angular = pl.pallas_call(
         functools.partial(angular_kernel, atoms),
         out_shape=shaped((slots, pairs, 4 * feature), F32),
@@ -570,7 +586,7 @@
         ],
         compiler_params=params,
         name="main",
-    )(own, one, two, four, three, angular, *prepared)
+    )(near, up, down, two, one, angular, *prepared)
 
 
 def solution(mesh):

time: 17.5 us -> 17.2 us (0.983)
  Pallas kernels: 7.91 us -> 7.68 us
    pallas_call x1, Pallas kernels: 1.61 us -> 1.36 us  [per_device(): pl.pallas_call(functools.partial(pack_kernel, extents, paired), out_shape...]
where the time goes in v6:
time: 17.2 us; the launch traced here: 17 us
  starting transfers between devices  7.91 us (46%)
  Pallas kernels  7.68 us (45%)
  between operations  0.7 us (4%)
  waiting for transfers between devices  0.64 us (4%)
    pallas_call x1, Pallas kernels, per_device(): pl.pallas_call(main_kernel, out_shape=(shaped(atom_feat.shape, BF16), sha...  3.28 us
    ppermute x1, starting transfers between devices, per_device(): down = lax.ppermute(down, 'gy', second)  3.1 us
    ppermute x1, starting transfers between devices, per_device(): up = lax.ppermute(up, 'gy', first)  3.02 us
    pallas_call x1, Pallas kernels, per_device(): pl.pallas_call(functools.partial(prepare_kernel, extents, paired), out_sh...  1.79 us
    pallas_call x1, Pallas kernels, per_device(): pl.pallas_call(functools.partial(pack_kernel, extents, paired), out_shape...  1.36 us
    pallas_call x1, Pallas kernels, per_device(): pl.pallas_call(functools.partial(angular_kernel, atoms), out_shape=shaped...  1.26 us
    ppermute x1, starting transfers between devices, per_device(): two = lax.ppermute(forwarded(2), 'gx', second)  1.07 us
    ppermute x1, starting transfers between devices, per_device(): one = lax.ppermute(forwarded(1), 'gx', first)  0.72 us
  transfers between devices with their start and end apart: 4, of which 1 were waited for; matrix products, arithmetic and copies ran while one was open for 0% of the time, Pallas kernels for 18%

profile of v6, /device:TPU:0, one launch (start us, length us, event | category | flops | bytes accessed | tf_op | source)
XLA Modules:
  0.0 17.0 jit_solution(10359077627432009421)
XLA Ops:
  0.6 1.4 %pack.1 = (bf16[112,128]{1,0:T(8,128)(2,1)S(1)}, bf16[112,128]{1,0:T(8,128)(2,1)S(1)}, s32[1,512]{1,0:T(1,128)S(1)}, s32[16,32]{1,0:T(8,128)S(1)}, bf16[1,1,32,6...) custom-call(s32[16,32]{1,0:T(8,128)} %bitcast.3, bf16[1,1,32,64]{3,2,1,0:T(8,128)(2,1)} %atom_hbm.1, ...), custom_call_target="tpu_custom_call" | custom-call | tf_op jit(solution)/shard_map/pack/pallas_call | solution.py:513
  2.0 3.0 %collective-permute-start = (bf16[112,128]{1,0:T(8,128)(2,1)S(1)}, bf16[112,128]{1,0:T(8,128)(2,1)S(1)}, u32[]{:S(2)}, u32[]{:S(2)}) collective-permute-start(bf16[112,128]{1,0:T(8,128)(2,1)S(1)} %get-tuple-element.41), channel_id=1, source_target_pairs={{0,1},{1,2},{2,3},{3,4},{4,5},{5,6},{6,7},{7,0},{8,9},{9,10},{10,1... | collective-permute-start | bytes 86024 | tf_op jit(solution)/shard_map/ppermute | solution.py:524
  5.0 3.1 %collective-permute-start.1 = (bf16[112,128]{1,0:T(8,128)(2,1)S(1)}, bf16[112,128]{1,0:T(8,128)(2,1)S(1)}, u32[]{:S(2)}, u32[]{:S(2)}) collective-permute-start(bf16[112,128]{1,0:T(8,128)(2,1)S(1)} %get-tuple-element.42), channel_id=1, source_target_pairs={{1,0},{2,1},{3,2},{4,3},{5,4},{6,5},{7,6},{0,7},{9,8},{10,9},{11,1... | collective-permute-start | bytes 86024 | tf_op jit(solution)/shard_map/ppermute | solution.py:525
  8.1 1.8 %prepare.1 = (bf16[112,128]{1,0:T(8,128)(2,1)S(1)}, bf16[512,432]{1,0:T(8,128)(2,1)S(1)}, f32[512,128]{1,0:T(8,128)S(1)}, bf16[512,128]{1,0:T(8,128)(2,1)S(1)}, ...) custom-call(s32[1,512]{1,0:T(1,128)S(1)} %get-tuple-element.36.spot_, ...), custom_call_target="tpu_custom_call" | custom-call | flops 67108864 | bytes 2097152 | tf_op jit(solution)/shard_map/prepare/pallas_call | solution.py:528
  9.9 0.0 collective-permute-done.up_ref
  9.9 0.0 collective-permute-done.1.down_ref
  10.0 0.7 %collective-permute-start.3 = (bf16[144,128]{1,0:T(8,128)(2,1)S(1)}, bf16[144,128]{1,0:T(8,128)(2,1)S(1)}, u32[]{:S(2)}, u32[]{:S(2)}) collective-permute-start(bf16[144,128]{1,0:T(8,128)(2,1)S(1)} %get-tuple-element.70), channel_id=1, source_target_pairs={{0,24},{8,16},{16,8},{24,0},{1,25},{9,17},{17,9},{25,1},{2,26},{10... | collective-permute-start | bytes 110600 | tf_op jit(solution)/shard_map/ppermute | solution.py:561
  10.7 1.1 %collective-permute-start.2 = (bf16[144,128]{1,0:T(8,128)(2,1)S(1)}, bf16[144,128]{1,0:T(8,128)(2,1)S(1)}, u32[]{:S(2)}, u32[]{:S(2)}) collective-permute-start(bf16[144,128]{1,0:T(8,128)(2,1)S(1)} %get-tuple-element.71), channel_id=1, source_target_pairs={{0,8},{8,0},{16,24},{24,16},{1,9},{9,1},{17,25},{25,17},{2,10},{10... | collective-permute-start | bytes 110600 | tf_op jit(solution)/shard_map/ppermute | solution.py:562
  11.8 1.3 %angular.1.angular_ref = f32[16,256,256]{2,1,0:T(8,128)S(1)} custom-call(f32[2,1,1,512]{3,2,1,0:T(1,128)S(1)} %get-tuple-element.57.dirs_ref, bf16[64,128]{1,0:T(8,128)(2,1)S(1)} %get-tuple-element.58.angle_ref), custom_call_target="tpu_custom_call" | custom-call | flops 268435456 | bytes 4194304 | tf_op jit(solution)/shard_map/angular/pallas_call | solution.py:563
  13.1 0.6 %collective-permute-done.3.one_ref = bf16[144,128]{1,0:T(8,128)(2,1)S(1)} collective-permute-done((bf16[144,128]{1,0:T(8,128)(2,1)S(1)}, bf16[144,128]{1,0:T(8,128)(2,1)S(1)}, u32[]{:S(2)}, u32[]{:S(2)}) %collective-permute-start.3) | collective-permute-done | bytes 36896 | tf_op jit(solution)/shard_map/ppermute | solution.py:561
  13.7 0.0 collective-permute-done.2.two_ref
  13.7 3.3 %main.1 = (bf16[1,1,32,64]{3,2,1,0:T(8,128)(2,1)}, bf16[1,1,32,1024]{3,2,1,0:T(8,128)(2,1)}) custom-call(bf16[112,128]{1,0:T(8,128)(2,1)S(1)} %get-tuple-element.54.near_ref, bf16[112,128]{1,0:T(8,128)(2,1)S(1)} %collective-permute-done.up_ref, bf16[112,128]{1,0:T(8,128)(2,1)S(1)} %collective-permute-done.1.down_ref, ...), custom_call_target="tpu_custom_call" | custom-call | tf_op jit(solution)/shard_map/main/pallas_call | solution.py:574
  (6 shorter events, 0.1 us)
Async XLA Ops:
  2.0 7.9 %collective-permute-start = (bf16[112,128]{1,0:T(8,128)(2,1)S(1)}, bf16[112,128]{1,0:T(8,128)(2,1)S(1)}, u32[]{:S(2)}, u32[]{:S(2)}) collective-permute-start(bf16[112,128]{1,0:T(8,128)(2,1)S(1)} %get-tuple-element.41), channel_id=1, source_target_pairs={{0,1},{1,2},{2,3},{3,4},{4,5},{5,6},{6,7},{7,0},{8,9},{9,10},{10,1... | collective-permute-start | bytes 86024 | tf_op jit(solution)/shard_map/ppermute | solution.py:524
  5.0 4.9 %collective-permute-start.1 = (bf16[112,128]{1,0:T(8,128)(2,1)S(1)}, bf16[112,128]{1,0:T(8,128)(2,1)S(1)}, u32[]{:S(2)}, u32[]{:S(2)}) collective-permute-start(bf16[112,128]{1,0:T(8,128)(2,1)S(1)} %get-tuple-element.42), channel_id=1, source_target_pairs={{1,0},{2,1},{3,2},{4,3},{5,4},{6,5},{7,6},{0,7},{9,8},{10,9},{11,1... | collective-permute-start | bytes 86024 | tf_op jit(solution)/shard_map/ppermute | solution.py:525
  10.0 3.7 %collective-permute-start.3 = (bf16[144,128]{1,0:T(8,128)(2,1)S(1)}, bf16[144,128]{1,0:T(8,128)(2,1)S(1)}, u32[]{:S(2)}, u32[]{:S(2)}) collective-permute-start(bf16[144,128]{1,0:T(8,128)(2,1)S(1)} %get-tuple-element.70), channel_id=1, source_target_pairs={{0,24},{8,16},{16,8},{24,0},{1,25},{9,17},{17,9},{25,1},{2,26},{10... | collective-permute-start | bytes 110600 | tf_op jit(solution)/shard_map/ppermute | solution.py:561
  10.7 3.0 %collective-permute-start.2 = (bf16[144,128]{1,0:T(8,128)(2,1)S(1)}, bf16[144,128]{1,0:T(8,128)(2,1)S(1)}, u32[]{:S(2)}, u32[]{:S(2)}) collective-permute-start(bf16[144,128]{1,0:T(8,128)(2,1)S(1)} %get-tuple-element.71), channel_id=1, source_target_pairs={{0,8},{8,0},{16,24},{24,16},{1,9},{9,1},{17,25},{25,17},{2,10},{10... | collective-permute-start | bytes 110600 | tf_op jit(solution)/shard_map/ppermute | solution.py:562

commit v7 on v6

--- a/solution.py
+++ b/solution.py
@@ -175,7 +175,14 @@
     )
 
 
-def angular_kernel(atoms, dirs_ref, angle_ref, angular_ref):
+def angular_kernel(atoms, dirs_ref, angle_ref, *refs):
+    sources, angular_ref, results, held, sems = refs[:7], refs[7], refs[8:16], refs[16:23], refs[23]
+    copies = [
+        pltpu.make_async_copy(source, target, sems.at[k])
+        for k, (source, target) in enumerate(zip(sources, held))
+    ]
+    for copy in copies:
+        copy.start()
     slots, pairs, _ = angular_ref.shape
     bonds = 2 * pairs
     degrees = angle_ref.shape[0]
@@ -234,6 +241,48 @@
             blocks = basis(even, turned(odd, places)) + basis(odd, turned(even, places + 1))
         series = jnp.concatenate(blocks, axis=0).T.astype(BF16)
         angular_ref[diagonal] = jnp.dot(series, weight, preferred_element_type=F32)
+    for copy in copies:
+        copy.wait()
+    prepare_weights(slots, held, results)
+
+
+def prepare_weights(slots, held, results):
+    bond_in_ref, bond_mix_ref, pair_ref, pair_hidden_ref, pair_out_ref, atom_in_ref = held[:6]
+    atom_out_ref = held[6]
+    bond_weight_ref, mix_weight_ref, pair_weight_ref, hidden_weight_ref = results[:4]
+    out_weight_ref, atom_in_weight_ref, sum_weight_ref, atom_out_weight_ref = results[4:]
+    feature = bond_mix_ref.shape[0]
+    weight = bond_in_ref[...].astype(F32)
+    source, other, bond_part = (weight[k * feature : (k + 1) * feature] for k in range(3))
+    blank = jnp.zeros_like(source)
+    away = [crossed(bond_part, blank), crossed(source, other)]
+    near = [crossed(other, source), crossed(blank, bond_part)]
+    bond_weight_ref[...] = (jnp.concatenate(away + near, axis=0) * 0.5).astype(BF16)
+    mix_weight_ref[...] = (diagonal_blocks(bond_mix_ref[...].astype(F32)) * 0.5).astype(BF16)
+    old = pair_ref[...].astype(F32) * 0.25
+    hidden = jnp.dot(bond_mix_ref[...], pair_ref[...], preferred_element_type=F32) * 0.125
+    weight = jnp.concatenate([hidden, hidden, old, old], axis=0).astype(BF16)
+    pair_weight_ref[...] = jnp.concatenate(
+        [two_blocks(weight[:, : 2 * feature]), two_blocks(weight[:, 2 * feature :])], axis=1
+    )
+    hidden_weight_ref[...] = (two_blocks(pair_hidden_ref[...].astype(F32)) * 0.25).astype(BF16)
+    out_weight_ref[...] = (diagonal_blocks(pair_out_ref[...].astype(F32)) * 0.5).astype(BF16)
+    weight = atom_in_ref[...].astype(F32) * 0.5
+    weight = crossed(weight, jnp.zeros_like(weight))
+    mean = weight[feature:] * (1.0 / slots)
+    atom_in_weight_ref[...] = jnp.concatenate([weight[:feature], mean, mean], axis=0).astype(BF16)
+    folded = jnp.dot(
+        pair_out_ref[...], (mean * 0.5).astype(BF16), preferred_element_type=F32
+    )
+    high = folded.astype(BF16)
+    low = (folded - high.astype(F32)).astype(BF16)
+    sum_weight_ref[...] = jnp.concatenate([high, high, low, low], axis=0)
+    weight = atom_out_ref[...].astype(F32) * 0.5
+    blank = jnp.zeros_like(weight)
+    weight = jnp.concatenate([weight, blank], axis=1)
+    atom_out_weight_ref[...] = jnp.concatenate([weight, jnp.zeros_like(weight)], axis=0).astype(
+        BF16
+    )
 
 
 def prepare_kernel(
@@ -243,17 +292,19 @@
     targets_ref,
     atom_ref,
     bond_ref,
-    *refs,
+    dirs_hbm,
+    angle_hbm,
+    near_ref,
+    chosen_ref,
+    right_ref,
+    own_ref,
+    dirs_ref,
+    angle_ref,
+    sems,
 ):
-    sources, results, held, sems = refs[:9], refs[9:23], refs[23:30], refs[30]
-    near_ref, chosen_ref, right_ref, own_ref = results[:4]
-    bond_weight_ref, mix_weight_ref, pair_weight_ref, hidden_weight_ref = results[4:8]
-    out_weight_ref, atom_in_weight_ref, sum_weight_ref, atom_out_weight_ref = results[8:12]
-    bond_in_ref, bond_mix_ref, pair_ref, pair_hidden_ref, pair_out_ref = held[:5]
-    atom_in_ref, atom_out_ref = held[5:]
     copies = [
         pltpu.make_async_copy(source, target, sems.at[k])
-        for k, (source, target) in enumerate(zip(sources, held + results[12:]))
+        for k, (source, target) in enumerate(((dirs_hbm, dirs_ref), (angle_hbm, angle_ref)))
     ]
     for copy in copies:
         copy.start()
@@ -300,38 +351,8 @@
     own += [jnp.concatenate([atom, x[:, feature:]], axis=1) for x in blocks]
     own = jnp.concatenate(own, axis=0)
     own_ref[...] = own
-
     for copy in copies:
         copy.wait()
-    weight = bond_in_ref[...].astype(F32)
-    source, other, bond_part = (weight[k * feature : (k + 1) * feature] for k in range(3))
-    blank = jnp.zeros_like(source)
-    away = [crossed(bond_part, blank), crossed(source, other)]
-    near = [crossed(other, source), crossed(blank, bond_part)]
-    bond_weight_ref[...] = (jnp.concatenate(away + near, axis=0) * 0.5).astype(BF16)
-    mix_weight_ref[...] = (diagonal_blocks(bond_mix_ref[...].astype(F32)) * 0.5).astype(BF16)
-    weight = pair_ref[...].astype(F32) * 0.5
-    pair_weight_ref[...] = jnp.concatenate(
-        [two_blocks(weight[:, : 2 * feature]), two_blocks(weight[:, 2 * feature :])], axis=1
-    ).astype(BF16)
-    hidden_weight_ref[...] = (two_blocks(pair_hidden_ref[...].astype(F32)) * 0.25).astype(BF16)
-    out_weight_ref[...] = (diagonal_blocks(pair_out_ref[...].astype(F32)) * 0.5).astype(BF16)
-    weight = atom_in_ref[...].astype(F32) * 0.5
-    weight = crossed(weight, jnp.zeros_like(weight))
-    mean = weight[feature:] * (1.0 / slots)
-    atom_in_weight_ref[...] = jnp.concatenate([weight[:feature], mean, mean], axis=0).astype(BF16)
-    folded = jnp.dot(
-        pair_out_ref[...], (mean * 0.5).astype(BF16), preferred_element_type=F32
-    )
-    high = folded.astype(BF16)
-    low = (folded - high.astype(F32)).astype(BF16)
-    sum_weight_ref[...] = jnp.concatenate([high, high, low, low], axis=0)
-    weight = atom_out_ref[...].astype(F32) * 0.5
-    blank = jnp.zeros_like(weight)
-    weight = jnp.concatenate([weight, blank], axis=1)
-    atom_out_weight_ref[...] = jnp.concatenate([weight, jnp.zeros_like(weight)], axis=0).astype(
-        BF16
-    )
 
 
 def doubled_gate(values):
@@ -398,20 +419,24 @@
         preferred_element_type=F32,
     )
     hidden = doubled_gate(incoming).astype(BF16)
+    old = jnp.where(left_lanes((bonds, width)), far, own.astype(F32))
+    both = jnp.concatenate([hidden, old.astype(BF16)], axis=1)
+    even, odd = both[:pairs], both[pairs:]
+    projected = jnp.dot(
+        jnp.concatenate([even, odd], axis=1), pair_weight_ref[...], preferred_element_type=F32
+    )
+    first_ref[...] = projected[:, : 2 * width]
+    second_ref[0] = projected[:, 2 * width :]
+    shifted = jnp.concatenate([even[atoms:], even[:atoms]], axis=0)
+    second_ref[1] = jnp.dot(
+        jnp.concatenate([odd, shifted], axis=1),
+        pair_weight_ref[:, 2 * width :],
+        preferred_element_type=F32,
+    )
     mixed = jnp.dot(hidden, mix_weight_ref[...], preferred_element_type=F32)
-    old = jnp.where(left_lanes((bonds, width)), far, own.astype(F32))
     new = (old + mixed).astype(BF16).astype(F32)
     average = ((new + pltpu.roll(new, feature, 1)) * 0.5).astype(BF16).astype(F32)
-    even, odd = average[:pairs], average[pairs:]
-    left = left_lanes((pairs, width))
-    packed = jnp.where(left, even, odd)
-    shifted = jnp.where(left, odd, jnp.concatenate([even[atoms:], even[:atoms]], axis=0))
-    projected = jnp.dot(packed.astype(BF16), pair_weight_ref[...], preferred_element_type=F32)
-    first_ref[...] = projected[:, : 2 * width]
-    second_ref[0] = projected[:, 2 * width :]
-    second_ref[1] = jnp.dot(
-        shifted.astype(BF16), pair_weight_ref[:, 2 * width :], preferred_element_type=F32
-    )
+    packed = jnp.where(left_lanes((pairs, width)), average[:pairs], average[pairs:])
     group = 2
 
     def first_gates(base):
@@ -532,45 +557,48 @@
             shaped((bonds, 9 * half + 9 * atoms // 2), BF16),
             shaped((bonds, 2 * feature), F32),
             shaped((bonds, 2 * feature), BF16),
+            shaped(bond_dirs.shape, F32),
+            shaped(angle_weight.shape, BF16),
+        ),
+        in_specs=[vmem] * 4 + [hbm] * 2,
+        out_specs=(vmem,) * 6,
+        scratch_shapes=[pltpu.SemaphoreType.DMA((2,))],
+        compiler_params=params,
+        cost_estimate=pl.CostEstimate(flops=64 * 2**20, bytes_accessed=2**21, transcendentals=0),
+        name="prepare",
+    )(*held, *in_hbm((bond_dirs, angle_weight)))
+    near, up, down, prepared = lax.optimization_barrier((near, up, down, prepared))
+    first, second = moves(extents[0], paired[0])
+
+    def forwarded(block):
+        parts = [x[block * half : (block + 1) * half] for x in (near, up, down)]
+        return jnp.concatenate(parts + [x[3 * half :] for x in (near, up, down)], axis=0)
+
+    one = lax.ppermute(forwarded(1), "gx", first)
+    two = lax.ppermute(forwarded(2), "gx", second)
+    angular, *made = pl.pallas_call(
+        functools.partial(angular_kernel, atoms),
+        out_shape=(
+            shaped((slots, pairs, 4 * feature), F32),
             shaped((4 * feature, 4 * feature), BF16),
             shaped((2 * feature, 2 * feature), BF16),
-            shaped((2 * feature, 8 * feature), BF16),
+            shaped((8 * feature, 8 * feature), BF16),
             shaped((2 * feature, 4 * feature), BF16),
             shaped((2 * feature, 2 * feature), BF16),
             shaped((3 * feature, 4 * feature), BF16),
             shaped((4 * feature, 4 * feature), BF16),
             shaped((2 * feature, 2 * feature), BF16),
-            shaped(bond_dirs.shape, F32),
-            shaped(angle_weight.shape, BF16),
         ),
-        in_specs=[vmem] * 4 + [hbm] * 9,
-        out_specs=(vmem,) * 14,
+        in_specs=[vmem] * 2 + [hbm] * 7,
+        out_specs=(vmem,) * 9,
         scratch_shapes=[pltpu.VMEM(x.shape, BF16) for x in weights]
-        + [pltpu.SemaphoreType.DMA((9,))],
-        compiler_params=params,
-        cost_estimate=pl.CostEstimate(flops=64 * 2**20, bytes_accessed=2**21, transcendentals=0),
-        name="prepare",
-    )(*held, *in_hbm(weights + (bond_dirs, angle_weight)))
-    near, up, down, prepared = lax.optimization_barrier((near, up, down, prepared))
-    first, second = moves(extents[0], paired[0])
-
-    def forwarded(block):
-        parts = [x[block * half : (block + 1) * half] for x in (near, up, down)]
-        return jnp.concatenate(parts + [x[3 * half :] for x in (near, up, down)], axis=0)
-
-    one = lax.ppermute(forwarded(1), "gx", first)
-    two = lax.ppermute(forwarded(2), "gx", second)
-    angular = pl.pallas_call(
-        functools.partial(angular_kernel, atoms),
-        out_shape=shaped((slots, pairs, 4 * feature), F32),
-        in_specs=[vmem, vmem],
-        out_specs=vmem,
+        + [pltpu.SemaphoreType.DMA((7,))],
         compiler_params=params,
         cost_estimate=pl.CostEstimate(
             flops=256 * 2**20, bytes_accessed=2**22, transcendentals=4096
         ),
         name="angular",
-    )(bond_dirs, angle_weight)
+    )(bond_dirs, angle_weight, *in_hbm(weights))
     return pl.pallas_call(
         main_kernel,
         out_shape=(shaped(atom_feat.shape, BF16), shaped(bond_feat.shape, BF16)),
@@ -586,7 +614,7 @@
         ],
         compiler_params=params,
         name="main",
-    )(near, up, down, two, one, angular, *prepared)
+    )(near, up, down, two, one, angular, *prepared, *made)
 
 
 def solution(mesh):

time: 17.2 us -> 17.1 us (level)
  Pallas kernels: 7.68 us -> 7.07 us
  waiting for transfers between devices: 0.64 us -> 1.03 us
    pallas_call x1, Pallas kernels: 1.79 us -> 0.87 us  [per_device(): pl.pallas_call(functools.partial(prepare_kernel, extents, paired), out_sh...]
    ppermute x1, waiting for transfers between devices: 0.01 us -> 0.91 us  [per_device(): up = lax.ppermute(up, 'gy', first)]
    ppermute x1, starting transfers between devices: 1.07 us -> 1.6 us  [per_device(): two = lax.ppermute(forwarded(2), 'gx', second)]
    ppermute x1, waiting for transfers between devices: 0.63 us -> 0.12 us  [per_device(): one = lax.ppermute(forwarded(1), 'gx', first)]
    ppermute x1, starting transfers between devices: 0.72 us -> 0.23 us  [per_device(): one = lax.ppermute(forwarded(1), 'gx', first)]
    pallas_call x1, Pallas kernels: 1.26 us -> 1.68 us  [per_device(): pl.pallas_call(functools.partial(angular_kernel, atoms), out_shape=(shape...]
  transfers between devices with their start and end apart: 4 -> 4, of which waited for: 1 -> 2; matrix products, arithmetic and copies ran while one was open for 0% -> 0% of each run, Pallas kernels for 18% -> 15%
where the time goes in v7:
time: 17.1 us; the launch traced here: 16.8 us
  starting transfers between devices  7.95 us (46%)
  Pallas kernels  7.07 us (41%)
  waiting for transfers between devices  1.03 us (6%)
  between operations  0.67 us (4%)
    pallas_call x1, Pallas kernels, per_device(): pl.pallas_call(main_kernel, out_shape=(shaped(atom_feat.shape, BF16), sha...  3.16 us
    ppermute x1, starting transfers between devices, per_device(): down = lax.ppermute(down, 'gy', second)  3.1 us
    ppermute x1, starting transfers between devices, per_device(): up = lax.ppermute(up, 'gy', first)  3.02 us
    pallas_call x1, Pallas kernels, per_device(): pl.pallas_call(functools.partial(angular_kernel, atoms), out_shape=(shape...  1.68 us
    ppermute x1, starting transfers between devices, per_device(): two = lax.ppermute(forwarded(2), 'gx', second)  1.6 us
    pallas_call x1, Pallas kernels, per_device(): pl.pallas_call(functools.partial(pack_kernel, extents, paired), out_shape...  1.36 us
    ppermute x1, waiting for transfers between devices, per_device(): up = lax.ppermute(up, 'gy', first)  0.91 us
    pallas_call x1, Pallas kernels, per_device(): pl.pallas_call(functools.partial(prepare_kernel, extents, paired), out_sh...  0.87 us
  transfers between devices with their start and end apart: 4, of which 2 were waited for; matrix products, arithmetic and copies ran while one was open for 0% of the time, Pallas kernels for 15%

profile of v7, /device:TPU:0, one launch (start us, length us, event | category | flops | bytes accessed | tf_op | source)
XLA Modules:
  0.0 16.8 jit_solution(6048222268979017903)
XLA Ops:
  0.6 1.4 %pack.1 = (bf16[112,128]{1,0:T(8,128)(2,1)S(1)}, bf16[112,128]{1,0:T(8,128)(2,1)S(1)}, s32[1,512]{1,0:T(1,128)S(1)}, s32[16,32]{1,0:T(8,128)S(1)}, bf16[1,1,32,6...) custom-call(s32[16,32]{1,0:T(8,128)} %bitcast.3, bf16[1,1,32,64]{3,2,1,0:T(8,128)(2,1)} %atom_hbm.1, ...), custom_call_target="tpu_custom_call" | custom-call | tf_op jit(solution)/shard_map/pack/pallas_call | solution.py:538
  2.0 3.0 %collective-permute-start = (bf16[112,128]{1,0:T(8,128)(2,1)S(1)}, bf16[112,128]{1,0:T(8,128)(2,1)S(1)}, u32[]{:S(2)}, u32[]{:S(2)}) collective-permute-start(bf16[112,128]{1,0:T(8,128)(2,1)S(1)} %get-tuple-element.34), channel_id=1, source_target_pairs={{0,1},{1,2},{2,3},{3,4},{4,5},{5,6},{6,7},{7,0},{8,9},{9,10},{10,1... | collective-permute-start | bytes 86024 | tf_op jit(solution)/shard_map/ppermute | solution.py:549
  5.0 3.1 %collective-permute-start.1 = (bf16[112,128]{1,0:T(8,128)(2,1)S(1)}, bf16[112,128]{1,0:T(8,128)(2,1)S(1)}, u32[]{:S(2)}, u32[]{:S(2)}) collective-permute-start(bf16[112,128]{1,0:T(8,128)(2,1)S(1)} %get-tuple-element.35), channel_id=1, source_target_pairs={{1,0},{2,1},{3,2},{4,3},{5,4},{6,5},{7,6},{0,7},{9,8},{10,9},{11,1... | collective-permute-start | bytes 86024 | tf_op jit(solution)/shard_map/ppermute | solution.py:550
  8.1 0.9 %prepare.1 = (bf16[112,128]{1,0:T(8,128)(2,1)S(1)}, bf16[512,432]{1,0:T(8,128)(2,1)S(1)}, f32[512,128]{1,0:T(8,128)S(1)}, bf16[512,128]{1,0:T(8,128)(2,1)S(1)}, ...) custom-call(s32[1,512]{1,0:T(1,128)S(1)} %get-tuple-element.29.spot_ref, ...), custom_call_target="tpu_custom_call" | custom-call | flops 67108864 | bytes 2097152 | tf_op jit(solution)/shard_map/prepare/pallas_call | solution.py:553
  9.0 0.9 %collective-permute-done.up_ref = bf16[112,128]{1,0:T(8,128)(2,1)S(1)} collective-permute-done((bf16[112,128]{1,0:T(8,128)(2,1)S(1)}, bf16[112,128]{1,0:T(8,128)(2,1)S(1)}, u32[]{:S(2)}, u32[]{:S(2)}) %collective-permute-start) | collective-permute-done | bytes 28704 | tf_op jit(solution)/shard_map/ppermute | solution.py:549
  9.9 0.0 collective-permute-done.1.down_ref
  10.0 0.2 %collective-permute-start.3 = (bf16[144,128]{1,0:T(8,128)(2,1)S(1)}, bf16[144,128]{1,0:T(8,128)(2,1)S(1)}, u32[]{:S(2)}, u32[]{:S(2)}) collective-permute-start(bf16[144,128]{1,0:T(8,128)(2,1)S(1)} %get-tuple-element.56), channel_id=1, source_target_pairs={{0,24},{8,16},{16,8},{24,0},{1,25},{9,17},{17,9},{25,1},{2,26},{10... | collective-permute-start | bytes 110600 | tf_op jit(solution)/shard_map/ppermute | solution.py:577
  10.2 1.6 %collective-permute-start.2 = (bf16[144,128]{1,0:T(8,128)(2,1)S(1)}, bf16[144,128]{1,0:T(8,128)(2,1)S(1)}, u32[]{:S(2)}, u32[]{:S(2)}) collective-permute-start(bf16[144,128]{1,0:T(8,128)(2,1)S(1)} %get-tuple-element.57), channel_id=1, source_target_pairs={{0,8},{8,0},{16,24},{24,16},{1,9},{9,1},{17,25},{25,17},{2,10},{10... | collective-permute-start | bytes 110600 | tf_op jit(solution)/shard_map/ppermute | solution.py:578
  11.8 1.7 %angular.1 = (f32[16,256,256]{2,1,0:T(8,128)S(1)}, bf16[256,256]{1,0:T(8,128)(2,1)S(1)}, bf16[128,128]{1,0:T(8,128)(2,1)S(1)}, bf16[512,512]{1,0:T(8,128)(2,1)S(...) custom-call(f32[2,1,1,512]{3,2,1,0:T(1,128)S(1)} %get-tuple-element., ...), custom_call_target="tpu_custom_call" | custom-call | flops 268435456 | bytes 4194304 | tf_op jit(solution)/shard_map/angular/pallas_call | solution.py:579
  13.5 0.1 collective-permute-done.3.one_ref
  13.6 0.0 collective-permute-done.2.two_ref
  13.6 3.2 %main.1 = (bf16[1,1,32,64]{3,2,1,0:T(8,128)(2,1)}, bf16[1,1,32,1024]{3,2,1,0:T(8,128)(2,1)}) custom-call(bf16[112,128]{1,0:T(8,128)(2,1)S(1)} %get-tuple-element.39.near_ref, bf16[112,128]{1,0:T(8,128)(2,1)S(1)} %collective-permute-done.up_ref, bf16[112,128]{1,0:T(8,128)(2,1)S(1)} %collective-permute-done.1.down_ref, ...), custom_call_target="tpu_custom_call" | custom-call | tf_op jit(solution)/shard_map/main/pallas_call | solution.py:602
  (6 shorter events, 0.0 us)
Async XLA Ops:
  2.0 7.9 %collective-permute-start = (bf16[112,128]{1,0:T(8,128)(2,1)S(1)}, bf16[112,128]{1,0:T(8,128)(2,1)S(1)}, u32[]{:S(2)}, u32[]{:S(2)}) collective-permute-start(bf16[112,128]{1,0:T(8,128)(2,1)S(1)} %get-tuple-element.34), channel_id=1, source_target_pairs={{0,1},{1,2},{2,3},{3,4},{4,5},{5,6},{6,7},{7,0},{8,9},{9,10},{10,1... | collective-permute-start | bytes 86024 | tf_op jit(solution)/shard_map/ppermute | solution.py:549
  5.0 4.9 %collective-permute-start.1 = (bf16[112,128]{1,0:T(8,128)(2,1)S(1)}, bf16[112,128]{1,0:T(8,128)(2,1)S(1)}, u32[]{:S(2)}, u32[]{:S(2)}) collective-permute-start(bf16[112,128]{1,0:T(8,128)(2,1)S(1)} %get-tuple-element.35), channel_id=1, source_target_pairs={{1,0},{2,1},{3,2},{4,3},{5,4},{6,5},{7,6},{0,7},{9,8},{10,9},{11,1... | collective-permute-start | bytes 86024 | tf_op jit(solution)/shard_map/ppermute | solution.py:550
  10.0 3.6 %collective-permute-start.3 = (bf16[144,128]{1,0:T(8,128)(2,1)S(1)}, bf16[144,128]{1,0:T(8,128)(2,1)S(1)}, u32[]{:S(2)}, u32[]{:S(2)}) collective-permute-start(bf16[144,128]{1,0:T(8,128)(2,1)S(1)} %get-tuple-element.56), channel_id=1, source_target_pairs={{0,24},{8,16},{16,8},{24,0},{1,25},{9,17},{17,9},{25,1},{2,26},{10... | collective-permute-start | bytes 110600 | tf_op jit(solution)/shard_map/ppermute | solution.py:577
  10.2 3.4 %collective-permute-start.2 = (bf16[144,128]{1,0:T(8,128)(2,1)S(1)}, bf16[144,128]{1,0:T(8,128)(2,1)S(1)}, u32[]{:S(2)}, u32[]{:S(2)}) collective-permute-start(bf16[144,128]{1,0:T(8,128)(2,1)S(1)} %get-tuple-element.57), channel_id=1, source_target_pairs={{0,8},{8,0},{16,24},{24,16},{1,9},{9,1},{17,25},{25,17},{2,10},{10... | collective-permute-start | bytes 110600 | tf_op jit(solution)/shard_map/ppermute | solution.py:578

commit v8 on v7

--- a/solution.py
+++ b/solution.py
@@ -437,19 +437,15 @@
     new = (old + mixed).astype(BF16).astype(F32)
     average = ((new + pltpu.roll(new, feature, 1)) * 0.5).astype(BF16).astype(F32)
     packed = jnp.where(left_lanes((pairs, width)), average[:pairs], average[pairs:])
-    group = 2
-
-    def first_gates(base):
-        for start in range(0, pairs, atoms):
-            here = first_ref[pl.ds(start, atoms)]
-            for diagonal in range(base, base + group):
-                there = (start + diagonal // 2 * atoms) % pairs
-                mixture = angular_ref[diagonal, pl.ds(start, atoms)] + (
-                    here + second_ref[diagonal % 2, pl.ds(there, atoms)]
-                )
-                pair_ref[pl.ds(diagonal * pairs + start, atoms)] = doubled_gate(mixture).astype(
-                    BF16
-                )
+    def first_gates(start):
+        here = first_ref[pl.ds(start, atoms)]
+        for diagonal in range(slots):
+            there = (start + diagonal // 2 * atoms) % pairs
+            mixture = angular_ref[diagonal, pl.ds(start, atoms)] + (
+                here + second_ref[diagonal % 2, pl.ds(there, atoms)]
+            )
+            row = start * slots + diagonal * atoms
+            pair_ref[pl.ds(row, atoms)] = doubled_gate(mixture).astype(BF16)
 
     def summed(rows):
         parts = [rows[k * atoms : (k + 1) * atoms] for k in range(slots // 2)]
@@ -463,30 +459,35 @@
         atom_in_weight_ref[...],
         preferred_element_type=F32,
     )
-    total = jnp.zeros((pairs, width), F32)
+    copies = []
+    sums = jnp.zeros((atoms, width), F32)
     first_gates(0)
-    for base in range(0, slots, group):
-        if base + group < slots:
-            first_gates(base + group)
+    for chunk, start in enumerate(range(0, pairs, atoms)):
+        if start + atoms < pairs:
+            first_gates(start + atoms)
         second = jnp.dot(
-            pair_ref[pl.ds(base * pairs, group * pairs)],
+            pair_ref[pl.ds(start * slots, atoms * slots)],
             hidden_weight_ref[...],
             preferred_element_type=F32,
         )
-        gates = doubled_gate(second)
-        for k in range(group):
-            total = total + gates[k * pairs : (k + 1) * pairs]
-    bond_out = packed + jnp.dot(
-        total.astype(BF16), out_weight_ref[...], preferred_element_type=F32
-    )
-    bond_out = bond_out.astype(BF16)
-    for k in range(slots // 2):
-        bond_result_ref[0, 0, :, k * width : (k + 1) * width] = bond_out[
-            k * atoms : (k + 1) * atoms
-        ]
-    copies = [pltpu.make_async_copy(bond_result_ref, bond_result_hbm, sems.at[0])]
-    copies[0].start()
-    sums = summed(total).astype(BF16)
+        total = jnp.zeros((atoms, width), F32)
+        for diagonal in range(slots):
+            total = total + doubled_gate(second[diagonal * atoms : (diagonal + 1) * atoms])
+        sums = sums + total
+        bond_out = packed[start : start + atoms] + jnp.dot(
+            total.astype(BF16), out_weight_ref[...], preferred_element_type=F32
+        )
+        columns = pl.ds(chunk * width, width)
+        bond_result_ref[0, 0, :, columns] = bond_out.astype(BF16)
+        copies.append(
+            pltpu.make_async_copy(
+                bond_result_ref.at[0, 0, :, columns],
+                bond_result_hbm.at[0, 0, :, columns],
+                sems.at[1 + chunk],
+            )
+        )
+        copies[-1].start()
+    sums = sums.astype(BF16)
     atom_incoming = atom_incoming + jnp.dot(
         jnp.concatenate([sums, sums], axis=1), sum_weight_ref[...], preferred_element_type=F32
     )
@@ -495,7 +496,7 @@
         atom_hidden, atom_out_weight_ref[...], preferred_element_type=F32
     )
     atom_result_ref[0, 0] = atom_new[:, :feature].astype(BF16)
-    copies.append(pltpu.make_async_copy(atom_result_ref, atom_result_hbm, sems.at[1]))
+    copies.append(pltpu.make_async_copy(atom_result_ref, atom_result_hbm, sems.at[0]))
     copies[-1].start()
     for copy in copies:
         copy.wait()
@@ -610,7 +611,7 @@
             pltpu.VMEM((pairs, 4 * feature), F32),
             pltpu.VMEM((2, pairs, 4 * feature), F32),
             pltpu.VMEM((slots * pairs, 2 * feature), BF16),
-            pltpu.SemaphoreType.DMA((2,)),
+            pltpu.SemaphoreType.DMA((1 + slots // 2,)),
         ],
         compiler_params=params,
         name="main",

time: 17.1 us -> 18.3 us (1.070)
  Pallas kernels: 7.07 us -> 8.31 us
    pallas_call x1, Pallas kernels: 3.16 us -> 4.4 us  [per_device(): pl.pallas_call(main_kernel, out_shape=(shaped(atom_feat.shape, BF16), sha...]
  transfers between devices with their start and end apart: 4 -> 4, of which waited for: 2 -> 2; matrix products, arithmetic and copies ran while one was open for 0% -> 0% of each run, Pallas kernels for 15% -> 14%
where the time goes in v8:
time: 18.3 us; the launch traced here: 18 us
  Pallas kernels  8.31 us (45%)
  starting transfers between devices  7.95 us (43%)
  waiting for transfers between devices  1.03 us (6%)
  between operations  0.67 us (4%)
    pallas_call x1, Pallas kernels, per_device(): pl.pallas_call(main_kernel, out_shape=(shaped(atom_feat.shape, BF16), sha...  4.4 us
    ppermute x1, starting transfers between devices, per_device(): down = lax.ppermute(down, 'gy', second)  3.1 us
    ppermute x1, starting transfers between devices, per_device(): up = lax.ppermute(up, 'gy', first)  3.02 us
    pallas_call x1, Pallas kernels, per_device(): pl.pallas_call(functools.partial(angular_kernel, atoms), out_shape=(shape...  1.68 us
    ppermute x1, starting transfers between devices, per_device(): two = lax.ppermute(forwarded(2), 'gx', second)  1.6 us
    pallas_call x1, Pallas kernels, per_device(): pl.pallas_call(functools.partial(pack_kernel, extents, paired), out_shape...  1.36 us
    ppermute x1, waiting for transfers between devices, per_device(): up = lax.ppermute(up, 'gy', first)  0.91 us
    pallas_call x1, Pallas kernels, per_device(): pl.pallas_call(functools.partial(prepare_kernel, extents, paired), out_sh...  0.87 us
  transfers between devices with their start and end apart: 4, of which 2 were waited for; matrix products, arithmetic and copies ran while one was open for 0% of the time, Pallas kernels for 14%

profile of v8, /device:TPU:0, one launch (start us, length us, event | category | flops | bytes accessed | tf_op | source)
XLA Modules:
  0.0 18.0 jit_solution(15707795815507105454)
XLA Ops:
  0.6 1.4 %pack.1 = (bf16[112,128]{1,0:T(8,128)(2,1)S(1)}, bf16[112,128]{1,0:T(8,128)(2,1)S(1)}, s32[1,512]{1,0:T(1,128)S(1)}, s32[16,32]{1,0:T(8,128)S(1)}, bf16[1,1,32,6...) custom-call(s32[16,32]{1,0:T(8,128)} %bitcast.3, bf16[1,1,32,64]{3,2,1,0:T(8,128)(2,1)} %atom_hbm.1, ...), custom_call_target="tpu_custom_call" | custom-call | tf_op jit(solution)/shard_map/pack/pallas_call | solution.py:539
  2.0 3.0 %collective-permute-start = (bf16[112,128]{1,0:T(8,128)(2,1)S(1)}, bf16[112,128]{1,0:T(8,128)(2,1)S(1)}, u32[]{:S(2)}, u32[]{:S(2)}) collective-permute-start(bf16[112,128]{1,0:T(8,128)(2,1)S(1)} %get-tuple-element.34), channel_id=1, source_target_pairs={{0,1},{1,2},{2,3},{3,4},{4,5},{5,6},{6,7},{7,0},{8,9},{9,10},{10,1... | collective-permute-start | bytes 86024 | tf_op jit(solution)/shard_map/ppermute | solution.py:550
  5.0 3.1 %collective-permute-start.1 = (bf16[112,128]{1,0:T(8,128)(2,1)S(1)}, bf16[112,128]{1,0:T(8,128)(2,1)S(1)}, u32[]{:S(2)}, u32[]{:S(2)}) collective-permute-start(bf16[112,128]{1,0:T(8,128)(2,1)S(1)} %get-tuple-element.35), channel_id=1, source_target_pairs={{1,0},{2,1},{3,2},{4,3},{5,4},{6,5},{7,6},{0,7},{9,8},{10,9},{11,1... | collective-permute-start | bytes 86024 | tf_op jit(solution)/shard_map/ppermute | solution.py:551
  8.1 0.9 %prepare.1 = (bf16[112,128]{1,0:T(8,128)(2,1)S(1)}, bf16[512,432]{1,0:T(8,128)(2,1)S(1)}, f32[512,128]{1,0:T(8,128)S(1)}, bf16[512,128]{1,0:T(8,128)(2,1)S(1)}, ...) custom-call(s32[1,512]{1,0:T(1,128)S(1)} %get-tuple-element.29.spot_ref, ...), custom_call_target="tpu_custom_call" | custom-call | flops 67108864 | bytes 2097152 | tf_op jit(solution)/shard_map/prepare/pallas_call | solution.py:554
  9.0 0.9 %collective-permute-done.up_ref = bf16[112,128]{1,0:T(8,128)(2,1)S(1)} collective-permute-done((bf16[112,128]{1,0:T(8,128)(2,1)S(1)}, bf16[112,128]{1,0:T(8,128)(2,1)S(1)}, u32[]{:S(2)}, u32[]{:S(2)}) %collective-permute-start) | collective-permute-done | bytes 28704 | tf_op jit(solution)/shard_map/ppermute | solution.py:550
  9.9 0.0 collective-permute-done.1.down_ref
  10.0 0.2 %collective-permute-start.3 = (bf16[144,128]{1,0:T(8,128)(2,1)S(1)}, bf16[144,128]{1,0:T(8,128)(2,1)S(1)}, u32[]{:S(2)}, u32[]{:S(2)}) collective-permute-start(bf16[144,128]{1,0:T(8,128)(2,1)S(1)} %get-tuple-element.56), channel_id=1, source_target_pairs={{0,24},{8,16},{16,8},{24,0},{1,25},{9,17},{17,9},{25,1},{2,26},{10... | collective-permute-start | bytes 110600 | tf_op jit(solution)/shard_map/ppermute | solution.py:578
  10.2 1.6 %collective-permute-start.2 = (bf16[144,128]{1,0:T(8,128)(2,1)S(1)}, bf16[144,128]{1,0:T(8,128)(2,1)S(1)}, u32[]{:S(2)}, u32[]{:S(2)}) collective-permute-start(bf16[144,128]{1,0:T(8,128)(2,1)S(1)} %get-tuple-element.57), channel_id=1, source_target_pairs={{0,8},{8,0},{16,24},{24,16},{1,9},{9,1},{17,25},{25,17},{2,10},{10... | collective-permute-start | bytes 110600 | tf_op jit(solution)/shard_map/ppermute | solution.py:579
  11.8 1.7 %angular.1 = (f32[16,256,256]{2,1,0:T(8,128)S(1)}, bf16[256,256]{1,0:T(8,128)(2,1)S(1)}, bf16[128,128]{1,0:T(8,128)(2,1)S(1)}, bf16[512,512]{1,0:T(8,128)(2,1)S(...) custom-call(f32[2,1,1,512]{3,2,1,0:T(1,128)S(1)} %get-tuple-element., ...), custom_call_target="tpu_custom_call" | custom-call | flops 268435456 | bytes 4194304 | tf_op jit(solution)/shard_map/angular/pallas_call | solution.py:580
  13.5 0.1 collective-permute-done.3.one_ref
  13.6 0.0 collective-permute-done.2.two_ref
  13.6 4.4 %main.1 = (bf16[1,1,32,64]{3,2,1,0:T(8,128)(2,1)}, bf16[1,1,32,1024]{3,2,1,0:T(8,128)(2,1)}) custom-call(bf16[112,128]{1,0:T(8,128)(2,1)S(1)} %get-tuple-element.39.near_ref, bf16[112,128]{1,0:T(8,128)(2,1)S(1)} %collective-permute-done.up_ref, bf16[112,128]{1,0:T(8,128)(2,1)S(1)} %collective-permute-done.1.down_ref, ...), custom_call_target="tpu_custom_call" | custom-call | tf_op jit(solution)/shard_map/main/pallas_call | solution.py:603
  (6 shorter events, 0.0 us)
Async XLA Ops:
  2.0 7.9 %collective-permute-start = (bf16[112,128]{1,0:T(8,128)(2,1)S(1)}, bf16[112,128]{1,0:T(8,128)(2,1)S(1)}, u32[]{:S(2)}, u32[]{:S(2)}) collective-permute-start(bf16[112,128]{1,0:T(8,128)(2,1)S(1)} %get-tuple-element.34), channel_id=1, source_target_pairs={{0,1},{1,2},{2,3},{3,4},{4,5},{5,6},{6,7},{7,0},{8,9},{9,10},{10,1... | collective-permute-start | bytes 86024 | tf_op jit(solution)/shard_map/ppermute | solution.py:550
  5.0 4.9 %collective-permute-start.1 = (bf16[112,128]{1,0:T(8,128)(2,1)S(1)}, bf16[112,128]{1,0:T(8,128)(2,1)S(1)}, u32[]{:S(2)}, u32[]{:S(2)}) collective-permute-start(bf16[112,128]{1,0:T(8,128)(2,1)S(1)} %get-tuple-element.35), channel_id=1, source_target_pairs={{1,0},{2,1},{3,2},{4,3},{5,4},{6,5},{7,6},{0,7},{9,8},{10,9},{11,1... | collective-permute-start | bytes 86024 | tf_op jit(solution)/shard_map/ppermute | solution.py:551
  10.0 3.6 %collective-permute-start.3 = (bf16[144,128]{1,0:T(8,128)(2,1)S(1)}, bf16[144,128]{1,0:T(8,128)(2,1)S(1)}, u32[]{:S(2)}, u32[]{:S(2)}) collective-permute-start(bf16[144,128]{1,0:T(8,128)(2,1)S(1)} %get-tuple-element.56), channel_id=1, source_target_pairs={{0,24},{8,16},{16,8},{24,0},{1,25},{9,17},{17,9},{25,1},{2,26},{10... | collective-permute-start | bytes 110600 | tf_op jit(solution)/shard_map/ppermute | solution.py:578
  10.2 3.4 %collective-permute-start.2 = (bf16[144,128]{1,0:T(8,128)(2,1)S(1)}, bf16[144,128]{1,0:T(8,128)(2,1)S(1)}, u32[]{:S(2)}, u32[]{:S(2)}) collective-permute-start(bf16[144,128]{1,0:T(8,128)(2,1)S(1)} %get-tuple-element.57), channel_id=1, source_target_pairs={{0,8},{8,0},{16,24},{24,16},{1,9},{9,1},{17,25},{25,17},{2,10},{10... | collective-permute-start | bytes 110600 | tf_op jit(solution)/shard_map/ppermute | solution.py:579

commit v9 on v7

--- a/solution.py
+++ b/solution.py
@@ -186,7 +186,7 @@
     slots, pairs, _ = angular_ref.shape
     bonds = 2 * pairs
     degrees = angle_ref.shape[0]
-    weight = (two_blocks(angle_ref[...].astype(F32)) * 0.5).astype(BF16)
+    weight = two_blocks(angle_ref[...].astype(F32)).astype(BF16)
     polar, azimuth = dirs_ref[0, 0], dirs_ref[1, 0]
     unit = jnp.concatenate(
         [
@@ -257,27 +257,27 @@
     blank = jnp.zeros_like(source)
     away = [crossed(bond_part, blank), crossed(source, other)]
     near = [crossed(other, source), crossed(blank, bond_part)]
-    bond_weight_ref[...] = (jnp.concatenate(away + near, axis=0) * 0.5).astype(BF16)
-    mix_weight_ref[...] = (diagonal_blocks(bond_mix_ref[...].astype(F32)) * 0.5).astype(BF16)
-    old = pair_ref[...].astype(F32) * 0.25
-    hidden = jnp.dot(bond_mix_ref[...], pair_ref[...], preferred_element_type=F32) * 0.125
+    bond_weight_ref[...] = jnp.concatenate(away + near, axis=0).astype(BF16)
+    mix_weight_ref[...] = diagonal_blocks(bond_mix_ref[...].astype(F32)).astype(BF16)
+    old = pair_ref[...].astype(F32) * 0.5
+    hidden = jnp.dot(bond_mix_ref[...], pair_ref[...], preferred_element_type=F32) * 0.5
     weight = jnp.concatenate([hidden, hidden, old, old], axis=0).astype(BF16)
     pair_weight_ref[...] = jnp.concatenate(
         [two_blocks(weight[:, : 2 * feature]), two_blocks(weight[:, 2 * feature :])], axis=1
     )
-    hidden_weight_ref[...] = (two_blocks(pair_hidden_ref[...].astype(F32)) * 0.25).astype(BF16)
-    out_weight_ref[...] = (diagonal_blocks(pair_out_ref[...].astype(F32)) * 0.5).astype(BF16)
-    weight = atom_in_ref[...].astype(F32) * 0.5
+    hidden_weight_ref[...] = two_blocks(pair_hidden_ref[...].astype(F32)).astype(BF16)
+    out_weight_ref[...] = diagonal_blocks(pair_out_ref[...].astype(F32)).astype(BF16)
+    weight = atom_in_ref[...].astype(F32)
     weight = crossed(weight, jnp.zeros_like(weight))
     mean = weight[feature:] * (1.0 / slots)
     atom_in_weight_ref[...] = jnp.concatenate([weight[:feature], mean, mean], axis=0).astype(BF16)
     folded = jnp.dot(
-        pair_out_ref[...], (mean * 0.5).astype(BF16), preferred_element_type=F32
+        pair_out_ref[...], mean.astype(BF16), preferred_element_type=F32
     )
     high = folded.astype(BF16)
     low = (folded - high.astype(F32)).astype(BF16)
     sum_weight_ref[...] = jnp.concatenate([high, high, low, low], axis=0)
-    weight = atom_out_ref[...].astype(F32) * 0.5
+    weight = atom_out_ref[...].astype(F32)
     blank = jnp.zeros_like(weight)
     weight = jnp.concatenate([weight, blank], axis=1)
     atom_out_weight_ref[...] = jnp.concatenate([weight, jnp.zeros_like(weight)], axis=0).astype(
@@ -355,10 +355,10 @@
         copy.wait()
 
 
-def doubled_gate(values):
+def gated(values):
     half = values.shape[1] // 2
     first, second = values[:, :half], values[:, half:]
-    return first * (1.0 + jnp.tanh(first)) * (1.0 + jnp.tanh(second))
+    return first * jax.nn.sigmoid(first) * jax.nn.sigmoid(second)
 
 
 def main_kernel(
@@ -418,7 +418,7 @@
         bond_weight_ref[...],
         preferred_element_type=F32,
     )
-    hidden = doubled_gate(incoming).astype(BF16)
+    hidden = gated(incoming).astype(BF16)
     old = jnp.where(left_lanes((bonds, width)), far, own.astype(F32))
     both = jnp.concatenate([hidden, old.astype(BF16)], axis=1)
     even, odd = both[:pairs], both[pairs:]
@@ -447,7 +447,7 @@
                 mixture = angular_ref[diagonal, pl.ds(start, atoms)] + (
                     here + second_ref[diagonal % 2, pl.ds(there, atoms)]
                 )
-                pair_ref[pl.ds(diagonal * pairs + start, atoms)] = doubled_gate(mixture).astype(
+                pair_ref[pl.ds(diagonal * pairs + start, atoms)] = gated(mixture).astype(
                     BF16
                 )
 
@@ -473,7 +473,7 @@
             hidden_weight_ref[...],
             preferred_element_type=F32,
         )
-        gates = doubled_gate(second)
+        gates = gated(second)
         for k in range(group):
             total = total + gates[k * pairs : (k + 1) * pairs]
     bond_out = packed + jnp.dot(
@@ -490,7 +490,7 @@
     atom_incoming = atom_incoming + jnp.dot(
         jnp.concatenate([sums, sums], axis=1), sum_weight_ref[...], preferred_element_type=F32
     )
-    atom_hidden = doubled_gate(atom_incoming).astype(BF16)
+    atom_hidden = gated(atom_incoming).astype(BF16)
     atom_new = atom.astype(F32) + jnp.dot(
         atom_hidden, atom_out_weight_ref[...], preferred_element_type=F32
     )

time: 17.1 us -> 17.1 us (level)
  no operation moved by 1% of the time
where the time goes in v9:
time: 17.1 us; the launch traced here: 16.8 us
  starting transfers between devices  7.95 us (46%)
  Pallas kernels  7.06 us (41%)
  waiting for transfers between devices  1.04 us (6%)
  between operations  0.67 us (4%)
    pallas_call x1, Pallas kernels, per_device(): pl.pallas_call(main_kernel, out_shape=(shaped(atom_feat.shape, BF16), sha...  3.16 us
    ppermute x1, starting transfers between devices, per_device(): down = lax.ppermute(down, 'gy', second)  3.1 us
    ppermute x1, starting transfers between devices, per_device(): up = lax.ppermute(up, 'gy', first)  3.02 us
    pallas_call x1, Pallas kernels, per_device(): pl.pallas_call(functools.partial(angular_kernel, atoms), out_shape=(shape...  1.67 us
    ppermute x1, starting transfers between devices, per_device(): two = lax.ppermute(forwarded(2), 'gx', second)  1.6 us
    pallas_call x1, Pallas kernels, per_device(): pl.pallas_call(functools.partial(pack_kernel, extents, paired), out_shape...  1.36 us
    ppermute x1, waiting for transfers between devices, per_device(): up = lax.ppermute(up, 'gy', first)  0.91 us
    pallas_call x1, Pallas kernels, per_device(): pl.pallas_call(functools.partial(prepare_kernel, extents, paired), out_sh...  0.87 us
  transfers between devices with their start and end apart: 4, of which 2 were waited for; matrix products, arithmetic and copies ran while one was open for 0% of the time, Pallas kernels for 15%

profile of v9, /device:TPU:0, one launch (start us, length us, event | category | flops | bytes accessed | tf_op | source)
XLA Modules:
  0.0 16.8 jit_solution(13849048847701139712)
XLA Ops:
  0.6 1.4 %pack.1 = (bf16[112,128]{1,0:T(8,128)(2,1)S(1)}, bf16[112,128]{1,0:T(8,128)(2,1)S(1)}, s32[1,512]{1,0:T(1,128)S(1)}, s32[16,32]{1,0:T(8,128)S(1)}, bf16[1,1,32,6...) custom-call(s32[16,32]{1,0:T(8,128)} %bitcast.3, bf16[1,1,32,64]{3,2,1,0:T(8,128)(2,1)} %atom_hbm.1, ...), custom_call_target="tpu_custom_call" | custom-call | tf_op jit(solution)/shard_map/pack/pallas_call | solution.py:538
  2.0 3.0 %collective-permute-start = (bf16[112,128]{1,0:T(8,128)(2,1)S(1)}, bf16[112,128]{1,0:T(8,128)(2,1)S(1)}, u32[]{:S(2)}, u32[]{:S(2)}) collective-permute-start(bf16[112,128]{1,0:T(8,128)(2,1)S(1)} %get-tuple-element.34), channel_id=1, source_target_pairs={{0,1},{1,2},{2,3},{3,4},{4,5},{5,6},{6,7},{7,0},{8,9},{9,10},{10,1... | collective-permute-start | bytes 86024 | tf_op jit(solution)/shard_map/ppermute | solution.py:549
  5.0 3.1 %collective-permute-start.1 = (bf16[112,128]{1,0:T(8,128)(2,1)S(1)}, bf16[112,128]{1,0:T(8,128)(2,1)S(1)}, u32[]{:S(2)}, u32[]{:S(2)}) collective-permute-start(bf16[112,128]{1,0:T(8,128)(2,1)S(1)} %get-tuple-element.35), channel_id=1, source_target_pairs={{1,0},{2,1},{3,2},{4,3},{5,4},{6,5},{7,6},{0,7},{9,8},{10,9},{11,1... | collective-permute-start | bytes 86024 | tf_op jit(solution)/shard_map/ppermute | solution.py:550
  8.1 0.9 %prepare.1 = (bf16[112,128]{1,0:T(8,128)(2,1)S(1)}, bf16[512,432]{1,0:T(8,128)(2,1)S(1)}, f32[512,128]{1,0:T(8,128)S(1)}, bf16[512,128]{1,0:T(8,128)(2,1)S(1)}, ...) custom-call(s32[1,512]{1,0:T(1,128)S(1)} %get-tuple-element.29.spot_ref, ...), custom_call_target="tpu_custom_call" | custom-call | flops 67108864 | bytes 2097152 | tf_op jit(solution)/shard_map/prepare/pallas_call | solution.py:553
  9.0 0.9 %collective-permute-done.up_ref = bf16[112,128]{1,0:T(8,128)(2,1)S(1)} collective-permute-done((bf16[112,128]{1,0:T(8,128)(2,1)S(1)}, bf16[112,128]{1,0:T(8,128)(2,1)S(1)}, u32[]{:S(2)}, u32[]{:S(2)}) %collective-permute-start) | collective-permute-done | bytes 28704 | tf_op jit(solution)/shard_map/ppermute | solution.py:549
  9.9 0.0 collective-permute-done.1.down_ref
  10.0 0.2 %collective-permute-start.3 = (bf16[144,128]{1,0:T(8,128)(2,1)S(1)}, bf16[144,128]{1,0:T(8,128)(2,1)S(1)}, u32[]{:S(2)}, u32[]{:S(2)}) collective-permute-start(bf16[144,128]{1,0:T(8,128)(2,1)S(1)} %get-tuple-element.56), channel_id=1, source_target_pairs={{0,24},{8,16},{16,8},{24,0},{1,25},{9,17},{17,9},{25,1},{2,26},{10... | collective-permute-start | bytes 110600 | tf_op jit(solution)/shard_map/ppermute | solution.py:577
  10.2 1.6 %collective-permute-start.2 = (bf16[144,128]{1,0:T(8,128)(2,1)S(1)}, bf16[144,128]{1,0:T(8,128)(2,1)S(1)}, u32[]{:S(2)}, u32[]{:S(2)}) collective-permute-start(bf16[144,128]{1,0:T(8,128)(2,1)S(1)} %get-tuple-element.57), channel_id=1, source_target_pairs={{0,8},{8,0},{16,24},{24,16},{1,9},{9,1},{17,25},{25,17},{2,10},{10... | collective-permute-start | bytes 110600 | tf_op jit(solution)/shard_map/ppermute | solution.py:578
  11.8 1.7 %angular.1 = (f32[16,256,256]{2,1,0:T(8,128)S(1)}, bf16[256,256]{1,0:T(8,128)(2,1)S(1)}, bf16[128,128]{1,0:T(8,128)(2,1)S(1)}, bf16[512,512]{1,0:T(8,128)(2,1)S(...) custom-call(f32[2,1,1,512]{3,2,1,0:T(1,128)S(1)} %get-tuple-element., ...), custom_call_target="tpu_custom_call" | custom-call | flops 268435456 | bytes 4194304 | tf_op jit(solution)/shard_map/angular/pallas_call | solution.py:579
  13.5 0.1 collective-permute-done.3.one_ref
  13.6 0.0 collective-permute-done.2.two_ref
  13.6 3.2 %main.1 = (bf16[1,1,32,64]{3,2,1,0:T(8,128)(2,1)}, bf16[1,1,32,1024]{3,2,1,0:T(8,128)(2,1)}) custom-call(bf16[112,128]{1,0:T(8,128)(2,1)S(1)} %get-tuple-element.39.near_ref, bf16[112,128]{1,0:T(8,128)(2,1)S(1)} %collective-permute-done.up_ref, bf16[112,128]{1,0:T(8,128)(2,1)S(1)} %collective-permute-done.1.down_ref, ...), custom_call_target="tpu_custom_call" | custom-call | tf_op jit(solution)/shard_map/main/pallas_call | solution.py:602
  (6 shorter events, 0.0 us)
Async XLA Ops:
  2.0 7.9 %collective-permute-start = (bf16[112,128]{1,0:T(8,128)(2,1)S(1)}, bf16[112,128]{1,0:T(8,128)(2,1)S(1)}, u32[]{:S(2)}, u32[]{:S(2)}) collective-permute-start(bf16[112,128]{1,0:T(8,128)(2,1)S(1)} %get-tuple-element.34), channel_id=1, source_target_pairs={{0,1},{1,2},{2,3},{3,4},{4,5},{5,6},{6,7},{7,0},{8,9},{9,10},{10,1... | collective-permute-start | bytes 86024 | tf_op jit(solution)/shard_map/ppermute | solution.py:549
  5.0 4.9 %collective-permute-start.1 = (bf16[112,128]{1,0:T(8,128)(2,1)S(1)}, bf16[112,128]{1,0:T(8,128)(2,1)S(1)}, u32[]{:S(2)}, u32[]{:S(2)}) collective-permute-start(bf16[112,128]{1,0:T(8,128)(2,1)S(1)} %get-tuple-element.35), channel_id=1, source_target_pairs={{1,0},{2,1},{3,2},{4,3},{5,4},{6,5},{7,6},{0,7},{9,8},{10,9},{11,1... | collective-permute-start | bytes 86024 | tf_op jit(solution)/shard_map/ppermute | solution.py:550
  10.0 3.6 %collective-permute-start.3 = (bf16[144,128]{1,0:T(8,128)(2,1)S(1)}, bf16[144,128]{1,0:T(8,128)(2,1)S(1)}, u32[]{:S(2)}, u32[]{:S(2)}) collective-permute-start(bf16[144,128]{1,0:T(8,128)(2,1)S(1)} %get-tuple-element.56), channel_id=1, source_target_pairs={{0,24},{8,16},{16,8},{24,0},{1,25},{9,17},{17,9},{25,1},{2,26},{10... | collective-permute-start | bytes 110600 | tf_op jit(solution)/shard_map/ppermute | solution.py:577
  10.2 3.4 %collective-permute-start.2 = (bf16[144,128]{1,0:T(8,128)(2,1)S(1)}, bf16[144,128]{1,0:T(8,128)(2,1)S(1)}, u32[]{:S(2)}, u32[]{:S(2)}) collective-permute-start(bf16[144,128]{1,0:T(8,128)(2,1)S(1)} %get-tuple-element.57), channel_id=1, source_target_pairs={{0,8},{8,0},{16,24},{24,16},{1,9},{9,1},{17,25},{25,17},{2,10},{10... | collective-permute-start | bytes 110600 | tf_op jit(solution)/shard_map/ppermute | solution.py:578

commit v10 on v9

--- a/solution.py
+++ b/solution.py
@@ -265,7 +265,7 @@
     pair_weight_ref[...] = jnp.concatenate(
         [two_blocks(weight[:, : 2 * feature]), two_blocks(weight[:, 2 * feature :])], axis=1
     )
-    hidden_weight_ref[...] = two_blocks(pair_hidden_ref[...].astype(F32)).astype(BF16)
+    hidden_weight_ref[...] = two_blocks(two_blocks(pair_hidden_ref[...].astype(F32))).astype(BF16)
     out_weight_ref[...] = diagonal_blocks(pair_out_ref[...].astype(F32)).astype(BF16)
     weight = atom_in_ref[...].astype(F32)
     weight = crossed(weight, jnp.zeros_like(weight))
@@ -468,14 +468,12 @@
     for base in range(0, slots, group):
         if base + group < slots:
             first_gates(base + group)
+        beside = [pair_ref[pl.ds((base + k) * pairs, pairs)] for k in range(group)]
         second = jnp.dot(
-            pair_ref[pl.ds(base * pairs, group * pairs)],
-            hidden_weight_ref[...],
-            preferred_element_type=F32,
+            jnp.concatenate(beside, axis=1), hidden_weight_ref[...], preferred_element_type=F32
         )
         gates = gated(second)
-        for k in range(group):
-            total = total + gates[k * pairs : (k + 1) * pairs]
+        total = total + (gates[:, :width] + gates[:, width:])
     bond_out = packed + jnp.dot(
         total.astype(BF16), out_weight_ref[...], preferred_element_type=F32
     )
@@ -583,7 +581,7 @@
             shaped((4 * feature, 4 * feature), BF16),
             shaped((2 * feature, 2 * feature), BF16),
             shaped((8 * feature, 8 * feature), BF16),
-            shaped((2 * feature, 4 * feature), BF16),
+            shaped((4 * feature, 8 * feature), BF16),
             shaped((2 * feature, 2 * feature), BF16),
             shaped((3 * feature, 4 * feature), BF16),
             shaped((4 * feature, 4 * feature), BF16),

time: 17.1 us -> 17.3 us (1.012)
  no operation moved by 1% of the time
where the time goes in v10:
time: 17.3 us; the launch traced here: 16.9 us
  starting transfers between devices  7.95 us (46%)
  Pallas kernels  7.22 us (42%)
  waiting for transfers between devices  1.04 us (6%)
  between operations  0.67 us (4%)
    pallas_call x1, Pallas kernels, per_device(): pl.pallas_call(main_kernel, out_shape=(shaped(atom_feat.shape, BF16), sha...  3.33 us
    ppermute x1, starting transfers between devices, per_device(): down = lax.ppermute(down, 'gy', second)  3.1 us
    ppermute x1, starting transfers between devices, per_device(): up = lax.ppermute(up, 'gy', first)  3.02 us
    pallas_call x1, Pallas kernels, per_device(): pl.pallas_call(functools.partial(angular_kernel, atoms), out_shape=(shape...  1.67 us
    ppermute x1, starting transfers between devices, per_device(): two = lax.ppermute(forwarded(2), 'gx', second)  1.6 us
    pallas_call x1, Pallas kernels, per_device(): pl.pallas_call(functools.partial(pack_kernel, extents, paired), out_shape...  1.36 us
    ppermute x1, waiting for transfers between devices, per_device(): up = lax.ppermute(up, 'gy', first)  0.91 us
    pallas_call x1, Pallas kernels, per_device(): pl.pallas_call(functools.partial(prepare_kernel, extents, paired), out_sh...  0.87 us
  transfers between devices with their start and end apart: 4, of which 2 were waited for; matrix products, arithmetic and copies ran while one was open for 0% of the time, Pallas kernels for 15%

profile of v10, /device:TPU:0, one launch (start us, length us, event | category | flops | bytes accessed | tf_op | source)
XLA Modules:
  0.0 16.9 jit_solution(12993881416932681222)
XLA Ops:
  0.6 1.4 %pack.1 = (bf16[112,128]{1,0:T(8,128)(2,1)S(1)}, bf16[112,128]{1,0:T(8,128)(2,1)S(1)}, s32[1,512]{1,0:T(1,128)S(1)}, s32[16,32]{1,0:T(8,128)S(1)}, bf16[1,1,32,6...) custom-call(s32[16,32]{1,0:T(8,128)} %bitcast.3, bf16[1,1,32,64]{3,2,1,0:T(8,128)(2,1)} %atom_hbm.1, ...), custom_call_target="tpu_custom_call" | custom-call | tf_op jit(solution)/shard_map/pack/pallas_call | solution.py:536
  2.0 3.0 %collective-permute-start = (bf16[112,128]{1,0:T(8,128)(2,1)S(1)}, bf16[112,128]{1,0:T(8,128)(2,1)S(1)}, u32[]{:S(2)}, u32[]{:S(2)}) collective-permute-start(bf16[112,128]{1,0:T(8,128)(2,1)S(1)} %get-tuple-element.34), channel_id=1, source_target_pairs={{0,1},{1,2},{2,3},{3,4},{4,5},{5,6},{6,7},{7,0},{8,9},{9,10},{10,1... | collective-permute-start | bytes 86024 | tf_op jit(solution)/shard_map/ppermute | solution.py:547
  5.0 3.1 %collective-permute-start.1 = (bf16[112,128]{1,0:T(8,128)(2,1)S(1)}, bf16[112,128]{1,0:T(8,128)(2,1)S(1)}, u32[]{:S(2)}, u32[]{:S(2)}) collective-permute-start(bf16[112,128]{1,0:T(8,128)(2,1)S(1)} %get-tuple-element.35), channel_id=1, source_target_pairs={{1,0},{2,1},{3,2},{4,3},{5,4},{6,5},{7,6},{0,7},{9,8},{10,9},{11,1... | collective-permute-start | bytes 86024 | tf_op jit(solution)/shard_map/ppermute | solution.py:548
  8.1 0.9 %prepare.1 = (bf16[112,128]{1,0:T(8,128)(2,1)S(1)}, bf16[512,432]{1,0:T(8,128)(2,1)S(1)}, f32[512,128]{1,0:T(8,128)S(1)}, bf16[512,128]{1,0:T(8,128)(2,1)S(1)}, ...) custom-call(s32[1,512]{1,0:T(1,128)S(1)} %get-tuple-element.29.spot_ref, ...), custom_call_target="tpu_custom_call" | custom-call | flops 67108864 | bytes 2097152 | tf_op jit(solution)/shard_map/prepare/pallas_call | solution.py:551
  9.0 0.9 %collective-permute-done.up_ref = bf16[112,128]{1,0:T(8,128)(2,1)S(1)} collective-permute-done((bf16[112,128]{1,0:T(8,128)(2,1)S(1)}, bf16[112,128]{1,0:T(8,128)(2,1)S(1)}, u32[]{:S(2)}, u32[]{:S(2)}) %collective-permute-start) | collective-permute-done | bytes 28704 | tf_op jit(solution)/shard_map/ppermute | solution.py:547
  9.9 0.0 collective-permute-done.1.down_ref
  10.0 0.2 %collective-permute-start.3 = (bf16[144,128]{1,0:T(8,128)(2,1)S(1)}, bf16[144,128]{1,0:T(8,128)(2,1)S(1)}, u32[]{:S(2)}, u32[]{:S(2)}) collective-permute-start(bf16[144,128]{1,0:T(8,128)(2,1)S(1)} %get-tuple-element.56), channel_id=1, source_target_pairs={{0,24},{8,16},{16,8},{24,0},{1,25},{9,17},{17,9},{25,1},{2,26},{10... | collective-permute-start | bytes 110600 | tf_op jit(solution)/shard_map/ppermute | solution.py:575
  10.2 1.6 %collective-permute-start.2 = (bf16[144,128]{1,0:T(8,128)(2,1)S(1)}, bf16[144,128]{1,0:T(8,128)(2,1)S(1)}, u32[]{:S(2)}, u32[]{:S(2)}) collective-permute-start(bf16[144,128]{1,0:T(8,128)(2,1)S(1)} %get-tuple-element.57), channel_id=1, source_target_pairs={{0,8},{8,0},{16,24},{24,16},{1,9},{9,1},{17,25},{25,17},{2,10},{10... | collective-permute-start | bytes 110600 | tf_op jit(solution)/shard_map/ppermute | solution.py:576
  11.8 1.7 %angular.1 = (f32[16,256,256]{2,1,0:T(8,128)S(1)}, bf16[256,256]{1,0:T(8,128)(2,1)S(1)}, bf16[128,128]{1,0:T(8,128)(2,1)S(1)}, bf16[512,512]{1,0:T(8,128)(2,1)S(...) custom-call(f32[2,1,1,512]{3,2,1,0:T(1,128)S(1)} %get-tuple-element., ...), custom_call_target="tpu_custom_call" | custom-call | flops 268435456 | bytes 4194304 | tf_op jit(solution)/shard_map/angular/pallas_call | solution.py:577
  13.5 0.1 collective-permute-done.3.one_ref
  13.6 0.0 collective-permute-done.2.two_ref
  13.6 3.3 %main.1 = (bf16[1,1,32,64]{3,2,1,0:T(8,128)(2,1)}, bf16[1,1,32,1024]{3,2,1,0:T(8,128)(2,1)}) custom-call(bf16[112,128]{1,0:T(8,128)(2,1)S(1)} %get-tuple-element.39.near_ref, bf16[112,128]{1,0:T(8,128)(2,1)S(1)} %collective-permute-done.up_ref, bf16[112,128]{1,0:T(8,128)(2,1)S(1)} %collective-permute-done.1.down_ref, ...), custom_call_target="tpu_custom_call" | custom-call | tf_op jit(solution)/shard_map/main/pallas_call | solution.py:600
  (6 shorter events, 0.0 us)
Async XLA Ops:
  2.0 7.9 %collective-permute-start = (bf16[112,128]{1,0:T(8,128)(2,1)S(1)}, bf16[112,128]{1,0:T(8,128)(2,1)S(1)}, u32[]{:S(2)}, u32[]{:S(2)}) collective-permute-start(bf16[112,128]{1,0:T(8,128)(2,1)S(1)} %get-tuple-element.34), channel_id=1, source_target_pairs={{0,1},{1,2},{2,3},{3,4},{4,5},{5,6},{6,7},{7,0},{8,9},{9,10},{10,1... | collective-permute-start | bytes 86024 | tf_op jit(solution)/shard_map/ppermute | solution.py:547
  5.0 4.9 %collective-permute-start.1 = (bf16[112,128]{1,0:T(8,128)(2,1)S(1)}, bf16[112,128]{1,0:T(8,128)(2,1)S(1)}, u32[]{:S(2)}, u32[]{:S(2)}) collective-permute-start(bf16[112,128]{1,0:T(8,128)(2,1)S(1)} %get-tuple-element.35), channel_id=1, source_target_pairs={{1,0},{2,1},{3,2},{4,3},{5,4},{6,5},{7,6},{0,7},{9,8},{10,9},{11,1... | collective-permute-start | bytes 86024 | tf_op jit(solution)/shard_map/ppermute | solution.py:548
  10.0 3.6 %collective-permute-start.3 = (bf16[144,128]{1,0:T(8,128)(2,1)S(1)}, bf16[144,128]{1,0:T(8,128)(2,1)S(1)}, u32[]{:S(2)}, u32[]{:S(2)}) collective-permute-start(bf16[144,128]{1,0:T(8,128)(2,1)S(1)} %get-tuple-element.56), channel_id=1, source_target_pairs={{0,24},{8,16},{16,8},{24,0},{1,25},{9,17},{17,9},{25,1},{2,26},{10... | collective-permute-start | bytes 110600 | tf_op jit(solution)/shard_map/ppermute | solution.py:575
  10.2 3.4 %collective-permute-start.2 = (bf16[144,128]{1,0:T(8,128)(2,1)S(1)}, bf16[144,128]{1,0:T(8,128)(2,1)S(1)}, u32[]{:S(2)}, u32[]{:S(2)}) collective-permute-start(bf16[144,128]{1,0:T(8,128)(2,1)S(1)} %get-tuple-element.57), channel_id=1, source_target_pairs={{0,8},{8,0},{16,24},{24,16},{1,9},{9,1},{17,25},{25,17},{2,10},{10... | collective-permute-start | bytes 110600 | tf_op jit(solution)/shard_map/ppermute | solution.py:576

commit v11 on v9

--- a/solution.py
+++ b/solution.py
@@ -261,10 +261,7 @@
     mix_weight_ref[...] = diagonal_blocks(bond_mix_ref[...].astype(F32)).astype(BF16)
     old = pair_ref[...].astype(F32) * 0.5
     hidden = jnp.dot(bond_mix_ref[...], pair_ref[...], preferred_element_type=F32) * 0.5
-    weight = jnp.concatenate([hidden, hidden, old, old], axis=0).astype(BF16)
-    pair_weight_ref[...] = jnp.concatenate(
-        [two_blocks(weight[:, : 2 * feature]), two_blocks(weight[:, 2 * feature :])], axis=1
-    )
+    pair_weight_ref[...] = jnp.concatenate([hidden, hidden, old, old], axis=0).astype(BF16)
     hidden_weight_ref[...] = two_blocks(pair_hidden_ref[...].astype(F32)).astype(BF16)
     out_weight_ref[...] = diagonal_blocks(pair_out_ref[...].astype(F32)).astype(BF16)
     weight = atom_in_ref[...].astype(F32)
@@ -421,23 +418,29 @@
     hidden = gated(incoming).astype(BF16)
     old = jnp.where(left_lanes((bonds, width)), far, own.astype(F32))
     both = jnp.concatenate([hidden, old.astype(BF16)], axis=1)
-    even, odd = both[:pairs], both[pairs:]
-    projected = jnp.dot(
-        jnp.concatenate([even, odd], axis=1), pair_weight_ref[...], preferred_element_type=F32
-    )
-    first_ref[...] = projected[:, : 2 * width]
-    second_ref[0] = projected[:, 2 * width :]
-    shifted = jnp.concatenate([even[atoms:], even[:atoms]], axis=0)
-    second_ref[1] = jnp.dot(
-        jnp.concatenate([odd, shifted], axis=1),
-        pair_weight_ref[:, 2 * width :],
-        preferred_element_type=F32,
-    )
+    projected = jnp.dot(both, pair_weight_ref[...], preferred_element_type=F32)
+    left = left_lanes((pairs, width))
+
+    def beside(one, other, one_turned, other_turned):
+        silu = jnp.where(left, one, other_turned)
+        return jnp.concatenate([silu, jnp.where(left, one_turned, other)], axis=1)
+
+    def parities(columns):
+        turned = pltpu.roll(columns, feature, 1)
+        return columns[:pairs], columns[pairs:], turned[:pairs], turned[pairs:]
+
+    first_ref[...] = beside(*parities(projected[:, :width]))
+    even, odd, even_turned, odd_turned = parities(projected[:, width:])
+    second_ref[0] = beside(even, odd, even_turned, odd_turned)
+    even, even_turned = (
+        jnp.concatenate([x[atoms:], x[:atoms]], axis=0) for x in (even, even_turned)
+    )
+    second_ref[1] = beside(odd, even, odd_turned, even_turned)
     mixed = jnp.dot(hidden, mix_weight_ref[...], preferred_element_type=F32)
     new = (old + mixed).astype(BF16).astype(F32)
     average = ((new + pltpu.roll(new, feature, 1)) * 0.5).astype(BF16).astype(F32)
-    packed = jnp.where(left_lanes((pairs, width)), average[:pairs], average[pairs:])
-    group = 2
+    packed = jnp.where(left, average[:pairs], average[pairs:])
+    group = 4
 
     def first_gates(base):
         for start in range(0, pairs, atoms):
@@ -582,7 +585,7 @@
             shaped((slots, pairs, 4 * feature), F32),
             shaped((4 * feature, 4 * feature), BF16),
             shaped((2 * feature, 2 * feature), BF16),
-            shaped((8 * feature, 8 * feature), BF16),
+            shaped((4 * feature, 4 * feature), BF16),
             shaped((2 * feature, 4 * feature), BF16),
             shaped((2 * feature, 2 * feature), BF16),
             shaped((3 * feature, 4 * feature), BF16),

time: 17.1 us -> 17.1 us (level)
  no operation moved by 1% of the time
where the time goes in v11:
time: 17.1 us; the launch traced here: 16.8 us
  starting transfers between devices  7.95 us (46%)
  Pallas kernels  7.07 us (41%)
  waiting for transfers between devices  1.05 us (6%)
  between operations  0.67 us (4%)
    pallas_call x1, Pallas kernels, per_device(): pl.pallas_call(main_kernel, out_shape=(shaped(atom_feat.shape, BF16), sha...  3.18 us
    ppermute x1, starting transfers between devices, per_device(): down = lax.ppermute(down, 'gy', second)  3.1 us
    ppermute x1, starting transfers between devices, per_device(): up = lax.ppermute(up, 'gy', first)  3.02 us
    pallas_call x1, Pallas kernels, per_device(): pl.pallas_call(functools.partial(angular_kernel, atoms), out_shape=(shape...  1.66 us
    ppermute x1, starting transfers between devices, per_device(): two = lax.ppermute(forwarded(2), 'gx', second)  1.6 us
    pallas_call x1, Pallas kernels, per_device(): pl.pallas_call(functools.partial(pack_kernel, extents, paired), out_shape...  1.36 us
    ppermute x1, waiting for transfers between devices, per_device(): up = lax.ppermute(up, 'gy', first)  0.91 us
    pallas_call x1, Pallas kernels, per_device(): pl.pallas_call(functools.partial(prepare_kernel, extents, paired), out_sh...  0.87 us
  transfers between devices with their start and end apart: 4, of which 2 were waited for; matrix products, arithmetic and copies ran while one was open for 0% of the time, Pallas kernels for 15%

profile of v11, /device:TPU:0, one launch (start us, length us, event | category | flops | bytes accessed | tf_op | source)
XLA Modules:
  0.0 16.8 jit_solution(14333838209824901004)
XLA Ops:
  0.6 1.4 %pack.1 = (bf16[112,128]{1,0:T(8,128)(2,1)S(1)}, bf16[112,128]{1,0:T(8,128)(2,1)S(1)}, s32[1,512]{1,0:T(1,128)S(1)}, s32[16,32]{1,0:T(8,128)S(1)}, bf16[1,1,32,6...) custom-call(s32[16,32]{1,0:T(8,128)} %bitcast.3, bf16[1,1,32,64]{3,2,1,0:T(8,128)(2,1)} %atom_hbm.1, ...), custom_call_target="tpu_custom_call" | custom-call | tf_op jit(solution)/shard_map/pack/pallas_call | solution.py:541
  2.0 3.0 %collective-permute-start = (bf16[112,128]{1,0:T(8,128)(2,1)S(1)}, bf16[112,128]{1,0:T(8,128)(2,1)S(1)}, u32[]{:S(2)}, u32[]{:S(2)}) collective-permute-start(bf16[112,128]{1,0:T(8,128)(2,1)S(1)} %get-tuple-element.34), channel_id=1, source_target_pairs={{0,1},{1,2},{2,3},{3,4},{4,5},{5,6},{6,7},{7,0},{8,9},{9,10},{10,1... | collective-permute-start | bytes 86024 | tf_op jit(solution)/shard_map/ppermute | solution.py:552
  5.0 3.1 %collective-permute-start.1 = (bf16[112,128]{1,0:T(8,128)(2,1)S(1)}, bf16[112,128]{1,0:T(8,128)(2,1)S(1)}, u32[]{:S(2)}, u32[]{:S(2)}) collective-permute-start(bf16[112,128]{1,0:T(8,128)(2,1)S(1)} %get-tuple-element.35), channel_id=1, source_target_pairs={{1,0},{2,1},{3,2},{4,3},{5,4},{6,5},{7,6},{0,7},{9,8},{10,9},{11,1... | collective-permute-start | bytes 86024 | tf_op jit(solution)/shard_map/ppermute | solution.py:553
  8.1 0.9 %prepare.1 = (bf16[112,128]{1,0:T(8,128)(2,1)S(1)}, bf16[512,432]{1,0:T(8,128)(2,1)S(1)}, f32[512,128]{1,0:T(8,128)S(1)}, bf16[512,128]{1,0:T(8,128)(2,1)S(1)}, ...) custom-call(s32[1,512]{1,0:T(1,128)S(1)} %get-tuple-element.29.spot_ref, ...), custom_call_target="tpu_custom_call" | custom-call | flops 67108864 | bytes 2097152 | tf_op jit(solution)/shard_map/prepare/pallas_call | solution.py:556
  9.0 0.9 %collective-permute-done.up_ref = bf16[112,128]{1,0:T(8,128)(2,1)S(1)} collective-permute-done((bf16[112,128]{1,0:T(8,128)(2,1)S(1)}, bf16[112,128]{1,0:T(8,128)(2,1)S(1)}, u32[]{:S(2)}, u32[]{:S(2)}) %collective-permute-start) | collective-permute-done | bytes 28704 | tf_op jit(solution)/shard_map/ppermute | solution.py:552
  9.9 0.0 collective-permute-done.1.down_ref
  10.0 0.2 %collective-permute-start.3 = (bf16[144,128]{1,0:T(8,128)(2,1)S(1)}, bf16[144,128]{1,0:T(8,128)(2,1)S(1)}, u32[]{:S(2)}, u32[]{:S(2)}) collective-permute-start(bf16[144,128]{1,0:T(8,128)(2,1)S(1)} %get-tuple-element.56), channel_id=1, source_target_pairs={{0,24},{8,16},{16,8},{24,0},{1,25},{9,17},{17,9},{25,1},{2,26},{10... | collective-permute-start | bytes 110600 | tf_op jit(solution)/shard_map/ppermute | solution.py:580
  10.2 1.6 %collective-permute-start.2 = (bf16[144,128]{1,0:T(8,128)(2,1)S(1)}, bf16[144,128]{1,0:T(8,128)(2,1)S(1)}, u32[]{:S(2)}, u32[]{:S(2)}) collective-permute-start(bf16[144,128]{1,0:T(8,128)(2,1)S(1)} %get-tuple-element.57), channel_id=1, source_target_pairs={{0,8},{8,0},{16,24},{24,16},{1,9},{9,1},{17,25},{25,17},{2,10},{10... | collective-permute-start | bytes 110600 | tf_op jit(solution)/shard_map/ppermute | solution.py:581
  11.8 1.7 %angular.1 = (f32[16,256,256]{2,1,0:T(8,128)S(1)}, bf16[256,256]{1,0:T(8,128)(2,1)S(1)}, bf16[128,128]{1,0:T(8,128)(2,1)S(1)}, bf16[256,256]{1,0:T(8,128)(2,1)S(...) custom-call(f32[2,1,1,512]{3,2,1,0:T(1,128)S(1)} %get-tuple-element., ...), custom_call_target="tpu_custom_call" | custom-call | flops 268435456 | bytes 4194304 | tf_op jit(solution)/shard_map/angular/pallas_call | solution.py:582
  13.5 0.1 collective-permute-done.3.one_ref
  13.6 0.0 collective-permute-done.2.two_ref
  13.6 3.2 %main.1 = (bf16[1,1,32,64]{3,2,1,0:T(8,128)(2,1)}, bf16[1,1,32,1024]{3,2,1,0:T(8,128)(2,1)}) custom-call(bf16[112,128]{1,0:T(8,128)(2,1)S(1)} %get-tuple-element.39.near_ref, bf16[112,128]{1,0:T(8,128)(2,1)S(1)} %collective-permute-done.up_ref, bf16[112,128]{1,0:T(8,128)(2,1)S(1)} %collective-permute-done.1.down_ref, ...), custom_call_target="tpu_custom_call" | custom-call | tf_op jit(solution)/shard_map/main/pallas_call | solution.py:605
  (6 shorter events, 0.0 us)
Async XLA Ops:
  2.0 7.9 %collective-permute-start = (bf16[112,128]{1,0:T(8,128)(2,1)S(1)}, bf16[112,128]{1,0:T(8,128)(2,1)S(1)}, u32[]{:S(2)}, u32[]{:S(2)}) collective-permute-start(bf16[112,128]{1,0:T(8,128)(2,1)S(1)} %get-tuple-element.34), channel_id=1, source_target_pairs={{0,1},{1,2},{2,3},{3,4},{4,5},{5,6},{6,7},{7,0},{8,9},{9,10},{10,1... | collective-permute-start | bytes 86024 | tf_op jit(solution)/shard_map/ppermute | solution.py:552
  5.0 4.9 %collective-permute-start.1 = (bf16[112,128]{1,0:T(8,128)(2,1)S(1)}, bf16[112,128]{1,0:T(8,128)(2,1)S(1)}, u32[]{:S(2)}, u32[]{:S(2)}) collective-permute-start(bf16[112,128]{1,0:T(8,128)(2,1)S(1)} %get-tuple-element.35), channel_id=1, source_target_pairs={{1,0},{2,1},{3,2},{4,3},{5,4},{6,5},{7,6},{0,7},{9,8},{10,9},{11,1... | collective-permute-start | bytes 86024 | tf_op jit(solution)/shard_map/ppermute | solution.py:553
  10.0 3.6 %collective-permute-start.3 = (bf16[144,128]{1,0:T(8,128)(2,1)S(1)}, bf16[144,128]{1,0:T(8,128)(2,1)S(1)}, u32[]{:S(2)}, u32[]{:S(2)}) collective-permute-start(bf16[144,128]{1,0:T(8,128)(2,1)S(1)} %get-tuple-element.56), channel_id=1, source_target_pairs={{0,24},{8,16},{16,8},{24,0},{1,25},{9,17},{17,9},{25,1},{2,26},{10... | collective-permute-start | bytes 110600 | tf_op jit(solution)/shard_map/ppermute | solution.py:580
  10.2 3.4 %collective-permute-start.2 = (bf16[144,128]{1,0:T(8,128)(2,1)S(1)}, bf16[144,128]{1,0:T(8,128)(2,1)S(1)}, u32[]{:S(2)}, u32[]{:S(2)}) collective-permute-start(bf16[144,128]{1,0:T(8,128)(2,1)S(1)} %get-tuple-element.57), channel_id=1, source_target_pairs={{0,8},{8,0},{16,24},{24,16},{1,9},{9,1},{17,25},{25,17},{2,10},{10... | collective-permute-start | bytes 110600 | tf_op jit(solution)/shard_map/ppermute | solution.py:581

commit v12 on v11

--- a/solution.py
+++ b/solution.py
@@ -440,7 +440,7 @@
     new = (old + mixed).astype(BF16).astype(F32)
     average = ((new + pltpu.roll(new, feature, 1)) * 0.5).astype(BF16).astype(F32)
     packed = jnp.where(left, average[:pairs], average[pairs:])
-    group = 4
+    group = 2
 
     def first_gates(base):
         for start in range(0, pairs, atoms):

time: 17.1 us -> 17.2 us (level)
  no operation moved by 1% of the time
where the time goes in v12:
time: 17.2 us; the launch traced here: 16.8 us
  starting transfers between devices  7.95 us (46%)
  Pallas kernels  7.1 us (41%)
  waiting for transfers between devices  1.05 us (6%)
  between operations  0.67 us (4%)
    pallas_call x1, Pallas kernels, per_device(): pl.pallas_call(main_kernel, out_shape=(shaped(atom_feat.shape, BF16), sha...  3.22 us
    ppermute x1, starting transfers between devices, per_device(): down = lax.ppermute(down, 'gy', second)  3.1 us
    ppermute x1, starting transfers between devices, per_device(): up = lax.ppermute(up, 'gy', first)  3.02 us
    pallas_call x1, Pallas kernels, per_device(): pl.pallas_call(functools.partial(angular_kernel, atoms), out_shape=(shape...  1.66 us
    ppermute x1, starting transfers between devices, per_device(): two = lax.ppermute(forwarded(2), 'gx', second)  1.6 us
    pallas_call x1, Pallas kernels, per_device(): pl.pallas_call(functools.partial(pack_kernel, extents, paired), out_shape...  1.36 us
    ppermute x1, waiting for transfers between devices, per_device(): up = lax.ppermute(up, 'gy', first)  0.91 us
    pallas_call x1, Pallas kernels, per_device(): pl.pallas_call(functools.partial(prepare_kernel, extents, paired), out_sh...  0.87 us
  transfers between devices with their start and end apart: 4, of which 2 were waited for; matrix products, arithmetic and copies ran while one was open for 0% of the time, Pallas kernels for 15%

profile of v12, /device:TPU:0, one launch (start us, length us, event | category | flops | bytes accessed | tf_op | source)
XLA Modules:
  0.0 16.8 jit_solution(2165208515529597082)
XLA Ops:
  0.6 1.4 %pack.1 = (bf16[112,128]{1,0:T(8,128)(2,1)S(1)}, bf16[112,128]{1,0:T(8,128)(2,1)S(1)}, s32[1,512]{1,0:T(1,128)S(1)}, s32[16,32]{1,0:T(8,128)S(1)}, bf16[1,1,32,6...) custom-call(s32[16,32]{1,0:T(8,128)} %bitcast.3, bf16[1,1,32,64]{3,2,1,0:T(8,128)(2,1)} %atom_hbm.1, ...), custom_call_target="tpu_custom_call" | custom-call | tf_op jit(solution)/shard_map/pack/pallas_call | solution.py:541
  2.0 3.0 %collective-permute-start = (bf16[112,128]{1,0:T(8,128)(2,1)S(1)}, bf16[112,128]{1,0:T(8,128)(2,1)S(1)}, u32[]{:S(2)}, u32[]{:S(2)}) collective-permute-start(bf16[112,128]{1,0:T(8,128)(2,1)S(1)} %get-tuple-element.34), channel_id=1, source_target_pairs={{0,1},{1,2},{2,3},{3,4},{4,5},{5,6},{6,7},{7,0},{8,9},{9,10},{10,1... | collective-permute-start | bytes 86024 | tf_op jit(solution)/shard_map/ppermute | solution.py:552
  5.0 3.1 %collective-permute-start.1 = (bf16[112,128]{1,0:T(8,128)(2,1)S(1)}, bf16[112,128]{1,0:T(8,128)(2,1)S(1)}, u32[]{:S(2)}, u32[]{:S(2)}) collective-permute-start(bf16[112,128]{1,0:T(8,128)(2,1)S(1)} %get-tuple-element.35), channel_id=1, source_target_pairs={{1,0},{2,1},{3,2},{4,3},{5,4},{6,5},{7,6},{0,7},{9,8},{10,9},{11,1... | collective-permute-start | bytes 86024 | tf_op jit(solution)/shard_map/ppermute | solution.py:553
  8.1 0.9 %prepare.1 = (bf16[112,128]{1,0:T(8,128)(2,1)S(1)}, bf16[512,432]{1,0:T(8,128)(2,1)S(1)}, f32[512,128]{1,0:T(8,128)S(1)}, bf16[512,128]{1,0:T(8,128)(2,1)S(1)}, ...) custom-call(s32[1,512]{1,0:T(1,128)S(1)} %get-tuple-element.29.spot_ref, ...), custom_call_target="tpu_custom_call" | custom-call | flops 67108864 | bytes 2097152 | tf_op jit(solution)/shard_map/prepare/pallas_call | solution.py:556
  9.0 0.9 %collective-permute-done.up_ref = bf16[112,128]{1,0:T(8,128)(2,1)S(1)} collective-permute-done((bf16[112,128]{1,0:T(8,128)(2,1)S(1)}, bf16[112,128]{1,0:T(8,128)(2,1)S(1)}, u32[]{:S(2)}, u32[]{:S(2)}) %collective-permute-start) | collective-permute-done | bytes 28704 | tf_op jit(solution)/shard_map/ppermute | solution.py:552
  9.9 0.0 collective-permute-done.1.down_ref
  10.0 0.2 %collective-permute-start.3 = (bf16[144,128]{1,0:T(8,128)(2,1)S(1)}, bf16[144,128]{1,0:T(8,128)(2,1)S(1)}, u32[]{:S(2)}, u32[]{:S(2)}) collective-permute-start(bf16[144,128]{1,0:T(8,128)(2,1)S(1)} %get-tuple-element.56), channel_id=1, source_target_pairs={{0,24},{8,16},{16,8},{24,0},{1,25},{9,17},{17,9},{25,1},{2,26},{10... | collective-permute-start | bytes 110600 | tf_op jit(solution)/shard_map/ppermute | solution.py:580
  10.2 1.6 %collective-permute-start.2 = (bf16[144,128]{1,0:T(8,128)(2,1)S(1)}, bf16[144,128]{1,0:T(8,128)(2,1)S(1)}, u32[]{:S(2)}, u32[]{:S(2)}) collective-permute-start(bf16[144,128]{1,0:T(8,128)(2,1)S(1)} %get-tuple-element.57), channel_id=1, source_target_pairs={{0,8},{8,0},{16,24},{24,16},{1,9},{9,1},{17,25},{25,17},{2,10},{10... | collective-permute-start | bytes 110600 | tf_op jit(solution)/shard_map/ppermute | solution.py:581
  11.8 1.7 %angular.1 = (f32[16,256,256]{2,1,0:T(8,128)S(1)}, bf16[256,256]{1,0:T(8,128)(2,1)S(1)}, bf16[128,128]{1,0:T(8,128)(2,1)S(1)}, bf16[256,256]{1,0:T(8,128)(2,1)S(...) custom-call(f32[2,1,1,512]{3,2,1,0:T(1,128)S(1)} %get-tuple-element., ...), custom_call_target="tpu_custom_call" | custom-call | flops 268435456 | bytes 4194304 | tf_op jit(solution)/shard_map/angular/pallas_call | solution.py:582
  13.5 0.1 collective-permute-done.3.one_ref
  13.6 0.0 collective-permute-done.2.two_ref
  13.6 3.2 %main.1 = (bf16[1,1,32,64]{3,2,1,0:T(8,128)(2,1)}, bf16[1,1,32,1024]{3,2,1,0:T(8,128)(2,1)}) custom-call(bf16[112,128]{1,0:T(8,128)(2,1)S(1)} %get-tuple-element.39.near_ref, bf16[112,128]{1,0:T(8,128)(2,1)S(1)} %collective-permute-done.up_ref, bf16[112,128]{1,0:T(8,128)(2,1)S(1)} %collective-permute-done.1.down_ref, ...), custom_call_target="tpu_custom_call" | custom-call | tf_op jit(solution)/shard_map/main/pallas_call | solution.py:605
  (6 shorter events, 0.0 us)
Async XLA Ops:
  2.0 7.9 %collective-permute-start = (bf16[112,128]{1,0:T(8,128)(2,1)S(1)}, bf16[112,128]{1,0:T(8,128)(2,1)S(1)}, u32[]{:S(2)}, u32[]{:S(2)}) collective-permute-start(bf16[112,128]{1,0:T(8,128)(2,1)S(1)} %get-tuple-element.34), channel_id=1, source_target_pairs={{0,1},{1,2},{2,3},{3,4},{4,5},{5,6},{6,7},{7,0},{8,9},{9,10},{10,1... | collective-permute-start | bytes 86024 | tf_op jit(solution)/shard_map/ppermute | solution.py:552
  5.0 4.9 %collective-permute-start.1 = (bf16[112,128]{1,0:T(8,128)(2,1)S(1)}, bf16[112,128]{1,0:T(8,128)(2,1)S(1)}, u32[]{:S(2)}, u32[]{:S(2)}) collective-permute-start(bf16[112,128]{1,0:T(8,128)(2,1)S(1)} %get-tuple-element.35), channel_id=1, source_target_pairs={{1,0},{2,1},{3,2},{4,3},{5,4},{6,5},{7,6},{0,7},{9,8},{10,9},{11,1... | collective-permute-start | bytes 86024 | tf_op jit(solution)/shard_map/ppermute | solution.py:553
  10.0 3.6 %collective-permute-start.3 = (bf16[144,128]{1,0:T(8,128)(2,1)S(1)}, bf16[144,128]{1,0:T(8,128)(2,1)S(1)}, u32[]{:S(2)}, u32[]{:S(2)}) collective-permute-start(bf16[144,128]{1,0:T(8,128)(2,1)S(1)} %get-tuple-element.56), channel_id=1, source_target_pairs={{0,24},{8,16},{16,8},{24,0},{1,25},{9,17},{17,9},{25,1},{2,26},{10... | collective-permute-start | bytes 110600 | tf_op jit(solution)/shard_map/ppermute | solution.py:580
  10.2 3.4 %collective-permute-start.2 = (bf16[144,128]{1,0:T(8,128)(2,1)S(1)}, bf16[144,128]{1,0:T(8,128)(2,1)S(1)}, u32[]{:S(2)}, u32[]{:S(2)}) collective-permute-start(bf16[144,128]{1,0:T(8,128)(2,1)S(1)} %get-tuple-element.57), channel_id=1, source_target_pairs={{0,8},{8,0},{16,24},{24,16},{1,9},{9,1},{17,25},{25,17},{2,10},{10... | collective-permute-start | bytes 110600 | tf_op jit(solution)/shard_map/ppermute | solution.py:581

commit v13 on v9

--- a/solution.py
+++ b/solution.py
@@ -145,9 +145,11 @@
     chosen = jnp.where(spot == wanted, 1.0, 0.0).astype(BF16)
     blocks = blocks_of(bond_ref, slots // 2)
     feature = blocks[0].shape[1] // 2
-    values = [x[:, :feature] for x in blocks] + [x[:, feature:] for x in blocks]
+    values = [jnp.concatenate([x[:, :feature]] * 2, axis=1) for x in blocks]
+    values += [jnp.concatenate([x[:, feature:]] * 2, axis=1) for x in blocks]
     packed = jnp.dot(chosen, jnp.concatenate(values, axis=0), preferred_element_type=F32)
-    return jnp.concatenate([packed[:count], packed[count:]], axis=1).astype(BF16)
+    left = left_lanes((count, 2 * feature))
+    return jnp.where(left, packed[:count], packed[count:]).astype(BF16)
 
 
 def atom_rows(atom_ref):
@@ -433,10 +435,6 @@
         pair_weight_ref[:, 2 * width :],
         preferred_element_type=F32,
     )
-    mixed = jnp.dot(hidden, mix_weight_ref[...], preferred_element_type=F32)
-    new = (old + mixed).astype(BF16).astype(F32)
-    average = ((new + pltpu.roll(new, feature, 1)) * 0.5).astype(BF16).astype(F32)
-    packed = jnp.where(left_lanes((pairs, width)), average[:pairs], average[pairs:])
     group = 2
 
     def first_gates(base):
@@ -457,12 +455,6 @@
             parts = [x + y for x, y in zip(parts[::2], parts[1::2])]
         return parts[0]
 
-    atom = own[0:atoms]
-    atom_incoming = jnp.dot(
-        jnp.concatenate([atom[:, :feature], summed(packed).astype(BF16)], axis=1),
-        atom_in_weight_ref[...],
-        preferred_element_type=F32,
-    )
     total = jnp.zeros((pairs, width), F32)
     first_gates(0)
     for base in range(0, slots, group):
@@ -476,6 +468,17 @@
         gates = gated(second)
         for k in range(group):
             total = total + gates[k * pairs : (k + 1) * pairs]
+        if base == slots // 2:
+            mixed = jnp.dot(hidden, mix_weight_ref[...], preferred_element_type=F32)
+            new = (old + mixed).astype(BF16).astype(F32)
+            average = ((new + pltpu.roll(new, feature, 1)) * 0.5).astype(BF16).astype(F32)
+            packed = jnp.where(left_lanes((pairs, width)), average[:pairs], average[pairs:])
+            atom = own[0:atoms]
+            atom_incoming = jnp.dot(
+                jnp.concatenate([atom[:, :feature], summed(packed).astype(BF16)], axis=1),
+                atom_in_weight_ref[...],
+                preferred_element_type=F32,
+            )
     bond_out = packed + jnp.dot(
         total.astype(BF16), out_weight_ref[...], preferred_element_type=F32
     )

time: 17.1 us -> 17 us (level)
  no operation moved by 1% of the time
where the time goes in v13:
time: 17 us; the launch traced here: 16.8 us
  starting transfers between devices  7.96 us (47%)
  Pallas kernels  7.01 us (41%)
  waiting for transfers between devices  1.06 us (6%)
  between operations  0.67 us (4%)
    pallas_call x1, Pallas kernels, per_device(): pl.pallas_call(main_kernel, out_shape=(shaped(atom_feat.shape, BF16), sha...  3.19 us
    ppermute x1, starting transfers between devices, per_device(): down = lax.ppermute(down, 'gy', second)  3.1 us
    ppermute x1, starting transfers between devices, per_device(): up = lax.ppermute(up, 'gy', first)  3.02 us
    pallas_call x1, Pallas kernels, per_device(): pl.pallas_call(functools.partial(angular_kernel, atoms), out_shape=(shape...  1.67 us
    ppermute x1, starting transfers between devices, per_device(): two = lax.ppermute(forwarded(2), 'gx', second)  1.6 us
    pallas_call x1, Pallas kernels, per_device(): pl.pallas_call(functools.partial(pack_kernel, extents, paired), out_shape...  1.32 us
    ppermute x1, waiting for transfers between devices, per_device(): up = lax.ppermute(up, 'gy', first)  0.95 us
    pallas_call x1, Pallas kernels, per_device(): pl.pallas_call(functools.partial(prepare_kernel, extents, paired), out_sh...  0.83 us
  transfers between devices with their start and end apart: 4, of which 2 were waited for; matrix products, arithmetic and copies ran while one was open for 0% of the time, Pallas kernels for 15%

profile of v13, /device:TPU:0, one launch (start us, length us, event | category | flops | bytes accessed | tf_op | source)
XLA Modules:
  0.0 16.8 jit_solution(7404227326529793049)
XLA Ops:
  0.6 1.3 %pack.1 = (bf16[112,128]{1,0:T(8,128)(2,1)S(1)}, bf16[112,128]{1,0:T(8,128)(2,1)S(1)}, s32[1,512]{1,0:T(1,128)S(1)}, s32[16,32]{1,0:T(8,128)S(1)}, bf16[1,1,32,6...) custom-call(s32[16,32]{1,0:T(8,128)} %bitcast.3, bf16[1,1,32,64]{3,2,1,0:T(8,128)(2,1)} %atom_hbm.1, ...), custom_call_target="tpu_custom_call" | custom-call | tf_op jit(solution)/shard_map/pack/pallas_call | solution.py:541
  2.0 3.0 %collective-permute-start = (bf16[112,128]{1,0:T(8,128)(2,1)S(1)}, bf16[112,128]{1,0:T(8,128)(2,1)S(1)}, u32[]{:S(2)}, u32[]{:S(2)}) collective-permute-start(bf16[112,128]{1,0:T(8,128)(2,1)S(1)} %get-tuple-element.34), channel_id=1, source_target_pairs={{0,1},{1,2},{2,3},{3,4},{4,5},{5,6},{6,7},{7,0},{8,9},{9,10},{10,1... | collective-permute-start | bytes 86024 | tf_op jit(solution)/shard_map/ppermute | solution.py:552
  5.0 3.1 %collective-permute-start.1 = (bf16[112,128]{1,0:T(8,128)(2,1)S(1)}, bf16[112,128]{1,0:T(8,128)(2,1)S(1)}, u32[]{:S(2)}, u32[]{:S(2)}) collective-permute-start(bf16[112,128]{1,0:T(8,128)(2,1)S(1)} %get-tuple-element.35), channel_id=1, source_target_pairs={{1,0},{2,1},{3,2},{4,3},{5,4},{6,5},{7,6},{0,7},{9,8},{10,9},{11,1... | collective-permute-start | bytes 86024 | tf_op jit(solution)/shard_map/ppermute | solution.py:553
  8.1 0.8 %prepare.1 = (bf16[112,128]{1,0:T(8,128)(2,1)S(1)}, bf16[512,432]{1,0:T(8,128)(2,1)S(1)}, f32[512,128]{1,0:T(8,128)S(1)}, bf16[512,128]{1,0:T(8,128)(2,1)S(1)}, ...) custom-call(s32[1,512]{1,0:T(1,128)S(1)} %get-tuple-element.29.spot_ref, ...), custom_call_target="tpu_custom_call" | custom-call | flops 67108864 | bytes 2097152 | tf_op jit(solution)/shard_map/prepare/pallas_call | solution.py:556
  8.9 0.9 %collective-permute-done.up_ref = bf16[112,128]{1,0:T(8,128)(2,1)S(1)} collective-permute-done((bf16[112,128]{1,0:T(8,128)(2,1)S(1)}, bf16[112,128]{1,0:T(8,128)(2,1)S(1)}, u32[]{:S(2)}, u32[]{:S(2)}) %collective-permute-start) | collective-permute-done | bytes 28704 | tf_op jit(solution)/shard_map/ppermute | solution.py:552
  9.9 0.0 collective-permute-done.1.down_ref
  9.9 0.2 %collective-permute-start.3 = (bf16[144,128]{1,0:T(8,128)(2,1)S(1)}, bf16[144,128]{1,0:T(8,128)(2,1)S(1)}, u32[]{:S(2)}, u32[]{:S(2)}) collective-permute-start(bf16[144,128]{1,0:T(8,128)(2,1)S(1)} %get-tuple-element.56), channel_id=1, source_target_pairs={{0,24},{8,16},{16,8},{24,0},{1,25},{9,17},{17,9},{25,1},{2,26},{10... | collective-permute-start | bytes 110600 | tf_op jit(solution)/shard_map/ppermute | solution.py:580
  10.2 1.6 %collective-permute-start.2 = (bf16[144,128]{1,0:T(8,128)(2,1)S(1)}, bf16[144,128]{1,0:T(8,128)(2,1)S(1)}, u32[]{:S(2)}, u32[]{:S(2)}) collective-permute-start(bf16[144,128]{1,0:T(8,128)(2,1)S(1)} %get-tuple-element.57), channel_id=1, source_target_pairs={{0,8},{8,0},{16,24},{24,16},{1,9},{9,1},{17,25},{25,17},{2,10},{10... | collective-permute-start | bytes 110600 | tf_op jit(solution)/shard_map/ppermute | solution.py:581
  11.8 1.7 %angular.1 = (f32[16,256,256]{2,1,0:T(8,128)S(1)}, bf16[256,256]{1,0:T(8,128)(2,1)S(1)}, bf16[128,128]{1,0:T(8,128)(2,1)S(1)}, bf16[512,512]{1,0:T(8,128)(2,1)S(...) custom-call(f32[2,1,1,512]{3,2,1,0:T(1,128)S(1)} %get-tuple-element., ...), custom_call_target="tpu_custom_call" | custom-call | flops 268435456 | bytes 4194304 | tf_op jit(solution)/shard_map/angular/pallas_call | solution.py:582
  13.5 0.1 collective-permute-done.3.one_ref
  13.6 0.0 collective-permute-done.2.two_ref
  13.6 3.2 %main.1 = (bf16[1,1,32,64]{3,2,1,0:T(8,128)(2,1)}, bf16[1,1,32,1024]{3,2,1,0:T(8,128)(2,1)}) custom-call(bf16[112,128]{1,0:T(8,128)(2,1)S(1)} %get-tuple-element.39.near_ref, bf16[112,128]{1,0:T(8,128)(2,1)S(1)} %collective-permute-done.up_ref, bf16[112,128]{1,0:T(8,128)(2,1)S(1)} %collective-permute-done.1.down_ref, ...), custom_call_target="tpu_custom_call" | custom-call | tf_op jit(solution)/shard_map/main/pallas_call | solution.py:605
  (6 shorter events, 0.0 us)
Async XLA Ops:
  2.0 7.9 %collective-permute-start = (bf16[112,128]{1,0:T(8,128)(2,1)S(1)}, bf16[112,128]{1,0:T(8,128)(2,1)S(1)}, u32[]{:S(2)}, u32[]{:S(2)}) collective-permute-start(bf16[112,128]{1,0:T(8,128)(2,1)S(1)} %get-tuple-element.34), channel_id=1, source_target_pairs={{0,1},{1,2},{2,3},{3,4},{4,5},{5,6},{6,7},{7,0},{8,9},{9,10},{10,1... | collective-permute-start | bytes 86024 | tf_op jit(solution)/shard_map/ppermute | solution.py:552
  5.0 4.9 %collective-permute-start.1 = (bf16[112,128]{1,0:T(8,128)(2,1)S(1)}, bf16[112,128]{1,0:T(8,128)(2,1)S(1)}, u32[]{:S(2)}, u32[]{:S(2)}) collective-permute-start(bf16[112,128]{1,0:T(8,128)(2,1)S(1)} %get-tuple-element.35), channel_id=1, source_target_pairs={{1,0},{2,1},{3,2},{4,3},{5,4},{6,5},{7,6},{0,7},{9,8},{10,9},{11,1... | collective-permute-start | bytes 86024 | tf_op jit(solution)/shard_map/ppermute | solution.py:553
  9.9 3.6 %collective-permute-start.3 = (bf16[144,128]{1,0:T(8,128)(2,1)S(1)}, bf16[144,128]{1,0:T(8,128)(2,1)S(1)}, u32[]{:S(2)}, u32[]{:S(2)}) collective-permute-start(bf16[144,128]{1,0:T(8,128)(2,1)S(1)} %get-tuple-element.56), channel_id=1, source_target_pairs={{0,24},{8,16},{16,8},{24,0},{1,25},{9,17},{17,9},{25,1},{2,26},{10... | collective-permute-start | bytes 110600 | tf_op jit(solution)/shard_map/ppermute | solution.py:580
  10.2 3.4 %collective-permute-start.2 = (bf16[144,128]{1,0:T(8,128)(2,1)S(1)}, bf16[144,128]{1,0:T(8,128)(2,1)S(1)}, u32[]{:S(2)}, u32[]{:S(2)}) collective-permute-start(bf16[144,128]{1,0:T(8,128)(2,1)S(1)} %get-tuple-element.57), channel_id=1, source_target_pairs={{0,8},{8,0},{16,24},{24,16},{1,9},{9,1},{17,25},{25,17},{2,10},{10... | collective-permute-start | bytes 110600 | tf_op jit(solution)/shard_map/ppermute | solution.py:581

commit v14 on v9

--- a/solution.py
+++ b/solution.py
@@ -145,9 +145,11 @@
     chosen = jnp.where(spot == wanted, 1.0, 0.0).astype(BF16)
     blocks = blocks_of(bond_ref, slots // 2)
     feature = blocks[0].shape[1] // 2
-    values = [x[:, :feature] for x in blocks] + [x[:, feature:] for x in blocks]
+    values = [jnp.concatenate([x[:, :feature]] * 2, axis=1) for x in blocks]
+    values += [jnp.concatenate([x[:, feature:]] * 2, axis=1) for x in blocks]
     packed = jnp.dot(chosen, jnp.concatenate(values, axis=0), preferred_element_type=F32)
-    return jnp.concatenate([packed[:count], packed[count:]], axis=1).astype(BF16)
+    left = left_lanes((count, 2 * feature))
+    return jnp.where(left, packed[:count], packed[count:]).astype(BF16)
 
 
 def atom_rows(atom_ref):

time: 17.1 us -> 17 us (level)
  no operation moved by 1% of the time
where the time goes in v14:
time: 17 us; the launch traced here: 16.7 us
  starting transfers between devices  7.96 us (47%)
  Pallas kernels  6.99 us (41%)
  waiting for transfers between devices  1.06 us (6%)
  between operations  0.67 us (4%)
    pallas_call x1, Pallas kernels, per_device(): pl.pallas_call(main_kernel, out_shape=(shaped(atom_feat.shape, BF16), sha...  3.16 us
    ppermute x1, starting transfers between devices, per_device(): down = lax.ppermute(down, 'gy', second)  3.1 us
    ppermute x1, starting transfers between devices, per_device(): up = lax.ppermute(up, 'gy', first)  3.02 us
    pallas_call x1, Pallas kernels, per_device(): pl.pallas_call(functools.partial(angular_kernel, atoms), out_shape=(shape...  1.67 us
    ppermute x1, starting transfers between devices, per_device(): two = lax.ppermute(forwarded(2), 'gx', second)  1.6 us
    pallas_call x1, Pallas kernels, per_device(): pl.pallas_call(functools.partial(pack_kernel, extents, paired), out_shape...  1.32 us
    ppermute x1, waiting for transfers between devices, per_device(): up = lax.ppermute(up, 'gy', first)  0.95 us
    pallas_call x1, Pallas kernels, per_device(): pl.pallas_call(functools.partial(prepare_kernel, extents, paired), out_sh...  0.83 us
  transfers between devices with their start and end apart: 4, of which 2 were waited for; matrix products, arithmetic and copies ran while one was open for 0% of the time, Pallas kernels for 15%

profile of v14, /device:TPU:0, one launch (start us, length us, event | category | flops | bytes accessed | tf_op | source)
XLA Modules:
  0.0 16.7 jit_solution(6101287462749402434)
XLA Ops:
  0.6 1.3 %pack.1 = (bf16[112,128]{1,0:T(8,128)(2,1)S(1)}, bf16[112,128]{1,0:T(8,128)(2,1)S(1)}, s32[1,512]{1,0:T(1,128)S(1)}, s32[16,32]{1,0:T(8,128)S(1)}, bf16[1,1,32,6...) custom-call(s32[16,32]{1,0:T(8,128)} %bitcast.3, bf16[1,1,32,64]{3,2,1,0:T(8,128)(2,1)} %atom_hbm.1, ...), custom_call_target="tpu_custom_call" | custom-call | tf_op jit(solution)/shard_map/pack/pallas_call | solution.py:540
  2.0 3.0 %collective-permute-start = (bf16[112,128]{1,0:T(8,128)(2,1)S(1)}, bf16[112,128]{1,0:T(8,128)(2,1)S(1)}, u32[]{:S(2)}, u32[]{:S(2)}) collective-permute-start(bf16[112,128]{1,0:T(8,128)(2,1)S(1)} %get-tuple-element.34), channel_id=1, source_target_pairs={{0,1},{1,2},{2,3},{3,4},{4,5},{5,6},{6,7},{7,0},{8,9},{9,10},{10,1... | collective-permute-start | bytes 86024 | tf_op jit(solution)/shard_map/ppermute | solution.py:551
  5.0 3.1 %collective-permute-start.1 = (bf16[112,128]{1,0:T(8,128)(2,1)S(1)}, bf16[112,128]{1,0:T(8,128)(2,1)S(1)}, u32[]{:S(2)}, u32[]{:S(2)}) collective-permute-start(bf16[112,128]{1,0:T(8,128)(2,1)S(1)} %get-tuple-element.35), channel_id=1, source_target_pairs={{1,0},{2,1},{3,2},{4,3},{5,4},{6,5},{7,6},{0,7},{9,8},{10,9},{11,1... | collective-permute-start | bytes 86024 | tf_op jit(solution)/shard_map/ppermute | solution.py:552
  8.1 0.8 %prepare.1 = (bf16[112,128]{1,0:T(8,128)(2,1)S(1)}, bf16[512,432]{1,0:T(8,128)(2,1)S(1)}, f32[512,128]{1,0:T(8,128)S(1)}, bf16[512,128]{1,0:T(8,128)(2,1)S(1)}, ...) custom-call(s32[1,512]{1,0:T(1,128)S(1)} %get-tuple-element.29.spot_ref, ...), custom_call_target="tpu_custom_call" | custom-call | flops 67108864 | bytes 2097152 | tf_op jit(solution)/shard_map/prepare/pallas_call | solution.py:555
  8.9 0.9 %collective-permute-done.up_ref = bf16[112,128]{1,0:T(8,128)(2,1)S(1)} collective-permute-done((bf16[112,128]{1,0:T(8,128)(2,1)S(1)}, bf16[112,128]{1,0:T(8,128)(2,1)S(1)}, u32[]{:S(2)}, u32[]{:S(2)}) %collective-permute-start) | collective-permute-done | bytes 28704 | tf_op jit(solution)/shard_map/ppermute | solution.py:551
  9.9 0.0 collective-permute-done.1.down_ref
  9.9 0.2 %collective-permute-start.3 = (bf16[144,128]{1,0:T(8,128)(2,1)S(1)}, bf16[144,128]{1,0:T(8,128)(2,1)S(1)}, u32[]{:S(2)}, u32[]{:S(2)}) collective-permute-start(bf16[144,128]{1,0:T(8,128)(2,1)S(1)} %get-tuple-element.56), channel_id=1, source_target_pairs={{0,24},{8,16},{16,8},{24,0},{1,25},{9,17},{17,9},{25,1},{2,26},{10... | collective-permute-start | bytes 110600 | tf_op jit(solution)/shard_map/ppermute | solution.py:579
  10.2 1.6 %collective-permute-start.2 = (bf16[144,128]{1,0:T(8,128)(2,1)S(1)}, bf16[144,128]{1,0:T(8,128)(2,1)S(1)}, u32[]{:S(2)}, u32[]{:S(2)}) collective-permute-start(bf16[144,128]{1,0:T(8,128)(2,1)S(1)} %get-tuple-element.57), channel_id=1, source_target_pairs={{0,8},{8,0},{16,24},{24,16},{1,9},{9,1},{17,25},{25,17},{2,10},{10... | collective-permute-start | bytes 110600 | tf_op jit(solution)/shard_map/ppermute | solution.py:580
  11.8 1.7 %angular.1 = (f32[16,256,256]{2,1,0:T(8,128)S(1)}, bf16[256,256]{1,0:T(8,128)(2,1)S(1)}, bf16[128,128]{1,0:T(8,128)(2,1)S(1)}, bf16[512,512]{1,0:T(8,128)(2,1)S(...) custom-call(f32[2,1,1,512]{3,2,1,0:T(1,128)S(1)} %get-tuple-element., ...), custom_call_target="tpu_custom_call" | custom-call | flops 268435456 | bytes 4194304 | tf_op jit(solution)/shard_map/angular/pallas_call | solution.py:581
  13.5 0.1 collective-permute-done.3.one_ref
  13.6 0.0 collective-permute-done.2.two_ref
  13.6 3.2 %main.1 = (bf16[1,1,32,64]{3,2,1,0:T(8,128)(2,1)}, bf16[1,1,32,1024]{3,2,1,0:T(8,128)(2,1)}) custom-call(bf16[112,128]{1,0:T(8,128)(2,1)S(1)} %get-tuple-element.39.near_ref, bf16[112,128]{1,0:T(8,128)(2,1)S(1)} %collective-permute-done.up_ref, bf16[112,128]{1,0:T(8,128)(2,1)S(1)} %collective-permute-done.1.down_ref, ...), custom_call_target="tpu_custom_call" | custom-call | tf_op jit(solution)/shard_map/main/pallas_call | solution.py:604
  (6 shorter events, 0.0 us)
Async XLA Ops:
  2.0 7.9 %collective-permute-start = (bf16[112,128]{1,0:T(8,128)(2,1)S(1)}, bf16[112,128]{1,0:T(8,128)(2,1)S(1)}, u32[]{:S(2)}, u32[]{:S(2)}) collective-permute-start(bf16[112,128]{1,0:T(8,128)(2,1)S(1)} %get-tuple-element.34), channel_id=1, source_target_pairs={{0,1},{1,2},{2,3},{3,4},{4,5},{5,6},{6,7},{7,0},{8,9},{9,10},{10,1... | collective-permute-start | bytes 86024 | tf_op jit(solution)/shard_map/ppermute | solution.py:551
  5.0 4.9 %collective-permute-start.1 = (bf16[112,128]{1,0:T(8,128)(2,1)S(1)}, bf16[112,128]{1,0:T(8,128)(2,1)S(1)}, u32[]{:S(2)}, u32[]{:S(2)}) collective-permute-start(bf16[112,128]{1,0:T(8,128)(2,1)S(1)} %get-tuple-element.35), channel_id=1, source_target_pairs={{1,0},{2,1},{3,2},{4,3},{5,4},{6,5},{7,6},{0,7},{9,8},{10,9},{11,1... | collective-permute-start | bytes 86024 | tf_op jit(solution)/shard_map/ppermute | solution.py:552
  9.9 3.6 %collective-permute-start.3 = (bf16[144,128]{1,0:T(8,128)(2,1)S(1)}, bf16[144,128]{1,0:T(8,128)(2,1)S(1)}, u32[]{:S(2)}, u32[]{:S(2)}) collective-permute-start(bf16[144,128]{1,0:T(8,128)(2,1)S(1)} %get-tuple-element.56), channel_id=1, source_target_pairs={{0,24},{8,16},{16,8},{24,0},{1,25},{9,17},{17,9},{25,1},{2,26},{10... | collective-permute-start | bytes 110600 | tf_op jit(solution)/shard_map/ppermute | solution.py:579
  10.2 3.4 %collective-permute-start.2 = (bf16[144,128]{1,0:T(8,128)(2,1)S(1)}, bf16[144,128]{1,0:T(8,128)(2,1)S(1)}, u32[]{:S(2)}, u32[]{:S(2)}) collective-permute-start(bf16[144,128]{1,0:T(8,128)(2,1)S(1)} %get-tuple-element.57), channel_id=1, source_target_pairs={{0,8},{8,0},{16,24},{24,16},{1,9},{9,1},{17,25},{25,17},{2,10},{10... | collective-permute-start | bytes 110600 | tf_op jit(solution)/shard_map/ppermute | solution.py:580

commit v15 on v14

--- a/solution.py
+++ b/solution.py
@@ -468,13 +468,13 @@
     total = jnp.zeros((pairs, width), F32)
     first_gates(0)
     for base in range(0, slots, group):
-        if base + group < slots:
-            first_gates(base + group)
         second = jnp.dot(
             pair_ref[pl.ds(base * pairs, group * pairs)],
             hidden_weight_ref[...],
             preferred_element_type=F32,
         )
+        if base + group < slots:
+            first_gates(base + group)
         gates = gated(second)
         for k in range(group):
             total = total + gates[k * pairs : (k + 1) * pairs]

time: 17 us -> 17 us (level)
  no operation moved by 1% of the time
where the time goes in v15:
time: 17 us; the launch traced here: 16.7 us
  starting transfers between devices  7.96 us (47%)
  Pallas kernels  6.99 us (41%)
  waiting for transfers between devices  1.06 us (6%)
  between operations  0.67 us (4%)
    pallas_call x1, Pallas kernels, per_device(): pl.pallas_call(main_kernel, out_shape=(shaped(atom_feat.shape, BF16), sha...  3.16 us
    ppermute x1, starting transfers between devices, per_device(): down = lax.ppermute(down, 'gy', second)  3.1 us
    ppermute x1, starting transfers between devices, per_device(): up = lax.ppermute(up, 'gy', first)  3.02 us
    pallas_call x1, Pallas kernels, per_device(): pl.pallas_call(functools.partial(angular_kernel, atoms), out_shape=(shape...  1.67 us
    ppermute x1, starting transfers between devices, per_device(): two = lax.ppermute(forwarded(2), 'gx', second)  1.6 us
    pallas_call x1, Pallas kernels, per_device(): pl.pallas_call(functools.partial(pack_kernel, extents, paired), out_shape...  1.32 us
    ppermute x1, waiting for transfers between devices, per_device(): up = lax.ppermute(up, 'gy', first)  0.95 us
    pallas_call x1, Pallas kernels, per_device(): pl.pallas_call(functools.partial(prepare_kernel, extents, paired), out_sh...  0.83 us
  transfers between devices with their start and end apart: 4, of which 2 were waited for; matrix products, arithmetic and copies ran while one was open for 0% of the time, Pallas kernels for 15%

profile of v15, /device:TPU:0, one launch (start us, length us, event | category | flops | bytes accessed | tf_op | source)
XLA Modules:
  0.0 16.7 jit_solution(6101287462749402434)
XLA Ops:
  0.6 1.3 %pack.1 = (bf16[112,128]{1,0:T(8,128)(2,1)S(1)}, bf16[112,128]{1,0:T(8,128)(2,1)S(1)}, s32[1,512]{1,0:T(1,128)S(1)}, s32[16,32]{1,0:T(8,128)S(1)}, bf16[1,1,32,6...) custom-call(s32[16,32]{1,0:T(8,128)} %bitcast.3, bf16[1,1,32,64]{3,2,1,0:T(8,128)(2,1)} %atom_hbm.1, ...), custom_call_target="tpu_custom_call" | custom-call | tf_op jit(solution)/shard_map/pack/pallas_call | solution.py:540
  2.0 3.0 %collective-permute-start = (bf16[112,128]{1,0:T(8,128)(2,1)S(1)}, bf16[112,128]{1,0:T(8,128)(2,1)S(1)}, u32[]{:S(2)}, u32[]{:S(2)}) collective-permute-start(bf16[112,128]{1,0:T(8,128)(2,1)S(1)} %get-tuple-element.34), channel_id=1, source_target_pairs={{0,1},{1,2},{2,3},{3,4},{4,5},{5,6},{6,7},{7,0},{8,9},{9,10},{10,1... | collective-permute-start | bytes 86024 | tf_op jit(solution)/shard_map/ppermute | solution.py:551
  5.0 3.1 %collective-permute-start.1 = (bf16[112,128]{1,0:T(8,128)(2,1)S(1)}, bf16[112,128]{1,0:T(8,128)(2,1)S(1)}, u32[]{:S(2)}, u32[]{:S(2)}) collective-permute-start(bf16[112,128]{1,0:T(8,128)(2,1)S(1)} %get-tuple-element.35), channel_id=1, source_target_pairs={{1,0},{2,1},{3,2},{4,3},{5,4},{6,5},{7,6},{0,7},{9,8},{10,9},{11,1... | collective-permute-start | bytes 86024 | tf_op jit(solution)/shard_map/ppermute | solution.py:552
  8.1 0.8 %prepare.1 = (bf16[112,128]{1,0:T(8,128)(2,1)S(1)}, bf16[512,432]{1,0:T(8,128)(2,1)S(1)}, f32[512,128]{1,0:T(8,128)S(1)}, bf16[512,128]{1,0:T(8,128)(2,1)S(1)}, ...) custom-call(s32[1,512]{1,0:T(1,128)S(1)} %get-tuple-element.29.spot_ref, ...), custom_call_target="tpu_custom_call" | custom-call | flops 67108864 | bytes 2097152 | tf_op jit(solution)/shard_map/prepare/pallas_call | solution.py:555
  8.9 0.9 %collective-permute-done.up_ref = bf16[112,128]{1,0:T(8,128)(2,1)S(1)} collective-permute-done((bf16[112,128]{1,0:T(8,128)(2,1)S(1)}, bf16[112,128]{1,0:T(8,128)(2,1)S(1)}, u32[]{:S(2)}, u32[]{:S(2)}) %collective-permute-start) | collective-permute-done | bytes 28704 | tf_op jit(solution)/shard_map/ppermute | solution.py:551
  9.9 0.0 collective-permute-done.1.down_ref
  9.9 0.2 %collective-permute-start.3 = (bf16[144,128]{1,0:T(8,128)(2,1)S(1)}, bf16[144,128]{1,0:T(8,128)(2,1)S(1)}, u32[]{:S(2)}, u32[]{:S(2)}) collective-permute-start(bf16[144,128]{1,0:T(8,128)(2,1)S(1)} %get-tuple-element.56), channel_id=1, source_target_pairs={{0,24},{8,16},{16,8},{24,0},{1,25},{9,17},{17,9},{25,1},{2,26},{10... | collective-permute-start | bytes 110600 | tf_op jit(solution)/shard_map/ppermute | solution.py:579
  10.2 1.6 %collective-permute-start.2 = (bf16[144,128]{1,0:T(8,128)(2,1)S(1)}, bf16[144,128]{1,0:T(8,128)(2,1)S(1)}, u32[]{:S(2)}, u32[]{:S(2)}) collective-permute-start(bf16[144,128]{1,0:T(8,128)(2,1)S(1)} %get-tuple-element.57), channel_id=1, source_target_pairs={{0,8},{8,0},{16,24},{24,16},{1,9},{9,1},{17,25},{25,17},{2,10},{10... | collective-permute-start | bytes 110600 | tf_op jit(solution)/shard_map/ppermute | solution.py:580
  11.8 1.7 %angular.1 = (f32[16,256,256]{2,1,0:T(8,128)S(1)}, bf16[256,256]{1,0:T(8,128)(2,1)S(1)}, bf16[128,128]{1,0:T(8,128)(2,1)S(1)}, bf16[512,512]{1,0:T(8,128)(2,1)S(...) custom-call(f32[2,1,1,512]{3,2,1,0:T(1,128)S(1)} %get-tuple-element., ...), custom_call_target="tpu_custom_call" | custom-call | flops 268435456 | bytes 4194304 | tf_op jit(solution)/shard_map/angular/pallas_call | solution.py:581
  13.5 0.1 collective-permute-done.3.one_ref
  13.6 0.0 collective-permute-done.2.two_ref
  13.6 3.2 %main.1 = (bf16[1,1,32,64]{3,2,1,0:T(8,128)(2,1)}, bf16[1,1,32,1024]{3,2,1,0:T(8,128)(2,1)}) custom-call(bf16[112,128]{1,0:T(8,128)(2,1)S(1)} %get-tuple-element.39.near_ref, bf16[112,128]{1,0:T(8,128)(2,1)S(1)} %collective-permute-done.up_ref, bf16[112,128]{1,0:T(8,128)(2,1)S(1)} %collective-permute-done.1.down_ref, ...), custom_call_target="tpu_custom_call" | custom-call | tf_op jit(solution)/shard_map/main/pallas_call | solution.py:604
  (6 shorter events, 0.0 us)
Async XLA Ops:
  2.0 7.9 %collective-permute-start = (bf16[112,128]{1,0:T(8,128)(2,1)S(1)}, bf16[112,128]{1,0:T(8,128)(2,1)S(1)}, u32[]{:S(2)}, u32[]{:S(2)}) collective-permute-start(bf16[112,128]{1,0:T(8,128)(2,1)S(1)} %get-tuple-element.34), channel_id=1, source_target_pairs={{0,1},{1,2},{2,3},{3,4},{4,5},{5,6},{6,7},{7,0},{8,9},{9,10},{10,1... | collective-permute-start | bytes 86024 | tf_op jit(solution)/shard_map/ppermute | solution.py:551
  5.0 4.9 %collective-permute-start.1 = (bf16[112,128]{1,0:T(8,128)(2,1)S(1)}, bf16[112,128]{1,0:T(8,128)(2,1)S(1)}, u32[]{:S(2)}, u32[]{:S(2)}) collective-permute-start(bf16[112,128]{1,0:T(8,128)(2,1)S(1)} %get-tuple-element.35), channel_id=1, source_target_pairs={{1,0},{2,1},{3,2},{4,3},{5,4},{6,5},{7,6},{0,7},{9,8},{10,9},{11,1... | collective-permute-start | bytes 86024 | tf_op jit(solution)/shard_map/ppermute | solution.py:552
  9.9 3.6 %collective-permute-start.3 = (bf16[144,128]{1,0:T(8,128)(2,1)S(1)}, bf16[144,128]{1,0:T(8,128)(2,1)S(1)}, u32[]{:S(2)}, u32[]{:S(2)}) collective-permute-start(bf16[144,128]{1,0:T(8,128)(2,1)S(1)} %get-tuple-element.56), channel_id=1, source_target_pairs={{0,24},{8,16},{16,8},{24,0},{1,25},{9,17},{17,9},{25,1},{2,26},{10... | collective-permute-start | bytes 110600 | tf_op jit(solution)/shard_map/ppermute | solution.py:579
  10.2 3.4 %collective-permute-start.2 = (bf16[144,128]{1,0:T(8,128)(2,1)S(1)}, bf16[144,128]{1,0:T(8,128)(2,1)S(1)}, u32[]{:S(2)}, u32[]{:S(2)}) collective-permute-start(bf16[144,128]{1,0:T(8,128)(2,1)S(1)} %get-tuple-element.57), channel_id=1, source_target_pairs={{0,8},{8,0},{16,24},{24,16},{1,9},{9,1},{17,25},{25,17},{2,10},{10... | collective-permute-start | bytes 110600 | tf_op jit(solution)/shard_map/ppermute | solution.py:580

commit v16 on v14

--- a/solution.py
+++ b/solution.py
@@ -478,6 +478,18 @@
         gates = gated(second)
         for k in range(group):
             total = total + gates[k * pairs : (k + 1) * pairs]
+    sums = summed(total).astype(BF16)
+    atom_incoming = atom_incoming + jnp.dot(
+        jnp.concatenate([sums, sums], axis=1), sum_weight_ref[...], preferred_element_type=F32
+    )
+    atom_hidden = gated(atom_incoming).astype(BF16)
+    atom_new = atom.astype(F32) + jnp.dot(
+        atom_hidden, atom_out_weight_ref[...], preferred_element_type=F32
+    )
+    atom_result_ref[0, 0] = atom_new[:, :feature].astype(BF16)
+    copies = []
+    copies.append(pltpu.make_async_copy(atom_result_ref, atom_result_hbm, sems.at[1]))
+    copies[-1].start()
     bond_out = packed + jnp.dot(
         total.astype(BF16), out_weight_ref[...], preferred_element_type=F32
     )
@@ -486,18 +498,7 @@
         bond_result_ref[0, 0, :, k * width : (k + 1) * width] = bond_out[
             k * atoms : (k + 1) * atoms
         ]
-    copies = [pltpu.make_async_copy(bond_result_ref, bond_result_hbm, sems.at[0])]
-    copies[0].start()
-    sums = summed(total).astype(BF16)
-    atom_incoming = atom_incoming + jnp.dot(
-        jnp.concatenate([sums, sums], axis=1), sum_weight_ref[...], preferred_element_type=F32
-    )
-    atom_hidden = gated(atom_incoming).astype(BF16)
-    atom_new = atom.astype(F32) + jnp.dot(
-        atom_hidden, atom_out_weight_ref[...], preferred_element_type=F32
-    )
-    atom_result_ref[0, 0] = atom_new[:, :feature].astype(BF16)
-    copies.append(pltpu.make_async_copy(atom_result_ref, atom_result_hbm, sems.at[1]))
+    copies.append(pltpu.make_async_copy(bond_result_ref, bond_result_hbm, sems.at[0]))
     copies[-1].start()
     for copy in copies:
         copy.wait()

time: 17 us -> 17 us (level)
  no operation moved by 1% of the time
where the time goes in v16:
time: 17 us; the launch traced here: 16.8 us
  starting transfers between devices  7.96 us (47%)
  Pallas kernels  7.04 us (41%)
  waiting for transfers between devices  1.06 us (6%)
  between operations  0.67 us (4%)
    pallas_call x1, Pallas kernels, per_device(): pl.pallas_call(main_kernel, out_shape=(shaped(atom_feat.shape, BF16), sha...  3.21 us
    ppermute x1, starting transfers between devices, per_device(): down = lax.ppermute(down, 'gy', second)  3.1 us
    ppermute x1, starting transfers between devices, per_device(): up = lax.ppermute(up, 'gy', first)  3.02 us
    pallas_call x1, Pallas kernels, per_device(): pl.pallas_call(functools.partial(angular_kernel, atoms), out_shape=(shape...  1.67 us
    ppermute x1, starting transfers between devices, per_device(): two = lax.ppermute(forwarded(2), 'gx', second)  1.6 us
    pallas_call x1, Pallas kernels, per_device(): pl.pallas_call(functools.partial(pack_kernel, extents, paired), out_shape...  1.32 us
    ppermute x1, waiting for transfers between devices, per_device(): up = lax.ppermute(up, 'gy', first)  0.95 us
    pallas_call x1, Pallas kernels, per_device(): pl.pallas_call(functools.partial(prepare_kernel, extents, paired), out_sh...  0.83 us
  transfers between devices with their start and end apart: 4, of which 2 were waited for; matrix products, arithmetic and copies ran while one was open for 0% of the time, Pallas kernels for 15%

profile of v16, /device:TPU:0, one launch (start us, length us, event | category | flops | bytes accessed | tf_op | source)
XLA Modules:
  0.0 16.8 jit_solution(1187564631408275284)
XLA Ops:
  0.6 1.3 %pack.1 = (bf16[112,128]{1,0:T(8,128)(2,1)S(1)}, bf16[112,128]{1,0:T(8,128)(2,1)S(1)}, s32[1,512]{1,0:T(1,128)S(1)}, s32[16,32]{1,0:T(8,128)S(1)}, bf16[1,1,32,6...) custom-call(s32[16,32]{1,0:T(8,128)} %bitcast.3, bf16[1,1,32,64]{3,2,1,0:T(8,128)(2,1)} %atom_hbm.1, ...), custom_call_target="tpu_custom_call" | custom-call | tf_op jit(solution)/shard_map/pack/pallas_call | solution.py:541
  2.0 3.0 %collective-permute-start = (bf16[112,128]{1,0:T(8,128)(2,1)S(1)}, bf16[112,128]{1,0:T(8,128)(2,1)S(1)}, u32[]{:S(2)}, u32[]{:S(2)}) collective-permute-start(bf16[112,128]{1,0:T(8,128)(2,1)S(1)} %get-tuple-element.34), channel_id=1, source_target_pairs={{0,1},{1,2},{2,3},{3,4},{4,5},{5,6},{6,7},{7,0},{8,9},{9,10},{10,1... | collective-permute-start | bytes 86024 | tf_op jit(solution)/shard_map/ppermute | solution.py:552
  5.0 3.1 %collective-permute-start.1 = (bf16[112,128]{1,0:T(8,128)(2,1)S(1)}, bf16[112,128]{1,0:T(8,128)(2,1)S(1)}, u32[]{:S(2)}, u32[]{:S(2)}) collective-permute-start(bf16[112,128]{1,0:T(8,128)(2,1)S(1)} %get-tuple-element.35), channel_id=1, source_target_pairs={{1,0},{2,1},{3,2},{4,3},{5,4},{6,5},{7,6},{0,7},{9,8},{10,9},{11,1... | collective-permute-start | bytes 86024 | tf_op jit(solution)/shard_map/ppermute | solution.py:553
  8.1 0.8 %prepare.1 = (bf16[112,128]{1,0:T(8,128)(2,1)S(1)}, bf16[512,432]{1,0:T(8,128)(2,1)S(1)}, f32[512,128]{1,0:T(8,128)S(1)}, bf16[512,128]{1,0:T(8,128)(2,1)S(1)}, ...) custom-call(s32[1,512]{1,0:T(1,128)S(1)} %get-tuple-element.29.spot_ref, ...), custom_call_target="tpu_custom_call" | custom-call | flops 67108864 | bytes 2097152 | tf_op jit(solution)/shard_map/prepare/pallas_call | solution.py:556
  8.9 0.9 %collective-permute-done.up_ref = bf16[112,128]{1,0:T(8,128)(2,1)S(1)} collective-permute-done((bf16[112,128]{1,0:T(8,128)(2,1)S(1)}, bf16[112,128]{1,0:T(8,128)(2,1)S(1)}, u32[]{:S(2)}, u32[]{:S(2)}) %collective-permute-start) | collective-permute-done | bytes 28704 | tf_op jit(solution)/shard_map/ppermute | solution.py:552
  9.9 0.0 collective-permute-done.1.down_ref
  9.9 0.2 %collective-permute-start.3 = (bf16[144,128]{1,0:T(8,128)(2,1)S(1)}, bf16[144,128]{1,0:T(8,128)(2,1)S(1)}, u32[]{:S(2)}, u32[]{:S(2)}) collective-permute-start(bf16[144,128]{1,0:T(8,128)(2,1)S(1)} %get-tuple-element.56), channel_id=1, source_target_pairs={{0,24},{8,16},{16,8},{24,0},{1,25},{9,17},{17,9},{25,1},{2,26},{10... | collective-permute-start | bytes 110600 | tf_op jit(solution)/shard_map/ppermute | solution.py:580
  10.2 1.6 %collective-permute-start.2 = (bf16[144,128]{1,0:T(8,128)(2,1)S(1)}, bf16[144,128]{1,0:T(8,128)(2,1)S(1)}, u32[]{:S(2)}, u32[]{:S(2)}) collective-permute-start(bf16[144,128]{1,0:T(8,128)(2,1)S(1)} %get-tuple-element.57), channel_id=1, source_target_pairs={{0,8},{8,0},{16,24},{24,16},{1,9},{9,1},{17,25},{25,17},{2,10},{10... | collective-permute-start | bytes 110600 | tf_op jit(solution)/shard_map/ppermute | solution.py:581
  11.8 1.7 %angular.1 = (f32[16,256,256]{2,1,0:T(8,128)S(1)}, bf16[256,256]{1,0:T(8,128)(2,1)S(1)}, bf16[128,128]{1,0:T(8,128)(2,1)S(1)}, bf16[512,512]{1,0:T(8,128)(2,1)S(...) custom-call(f32[2,1,1,512]{3,2,1,0:T(1,128)S(1)} %get-tuple-element., ...), custom_call_target="tpu_custom_call" | custom-call | flops 268435456 | bytes 4194304 | tf_op jit(solution)/shard_map/angular/pallas_call | solution.py:582
  13.5 0.1 collective-permute-done.3.one_ref
  13.6 0.0 collective-permute-done.2.two_ref
  13.6 3.2 %main.1 = (bf16[1,1,32,64]{3,2,1,0:T(8,128)(2,1)}, bf16[1,1,32,1024]{3,2,1,0:T(8,128)(2,1)}) custom-call(bf16[112,128]{1,0:T(8,128)(2,1)S(1)} %get-tuple-element.39.near_ref, bf16[112,128]{1,0:T(8,128)(2,1)S(1)} %collective-permute-done.up_ref, bf16[112,128]{1,0:T(8,128)(2,1)S(1)} %collective-permute-done.1.down_ref, ...), custom_call_target="tpu_custom_call" | custom-call | tf_op jit(solution)/shard_map/main/pallas_call | solution.py:605
  (6 shorter events, 0.0 us)
Async XLA Ops:
  2.0 7.9 %collective-permute-start = (bf16[112,128]{1,0:T(8,128)(2,1)S(1)}, bf16[112,128]{1,0:T(8,128)(2,1)S(1)}, u32[]{:S(2)}, u32[]{:S(2)}) collective-permute-start(bf16[112,128]{1,0:T(8,128)(2,1)S(1)} %get-tuple-element.34), channel_id=1, source_target_pairs={{0,1},{1,2},{2,3},{3,4},{4,5},{5,6},{6,7},{7,0},{8,9},{9,10},{10,1... | collective-permute-start | bytes 86024 | tf_op jit(solution)/shard_map/ppermute | solution.py:552
  5.0 4.9 %collective-permute-start.1 = (bf16[112,128]{1,0:T(8,128)(2,1)S(1)}, bf16[112,128]{1,0:T(8,128)(2,1)S(1)}, u32[]{:S(2)}, u32[]{:S(2)}) collective-permute-start(bf16[112,128]{1,0:T(8,128)(2,1)S(1)} %get-tuple-element.35), channel_id=1, source_target_pairs={{1,0},{2,1},{3,2},{4,3},{5,4},{6,5},{7,6},{0,7},{9,8},{10,9},{11,1... | collective-permute-start | bytes 86024 | tf_op jit(solution)/shard_map/ppermute | solution.py:553
  9.9 3.6 %collective-permute-start.3 = (bf16[144,128]{1,0:T(8,128)(2,1)S(1)}, bf16[144,128]{1,0:T(8,128)(2,1)S(1)}, u32[]{:S(2)}, u32[]{:S(2)}) collective-permute-start(bf16[144,128]{1,0:T(8,128)(2,1)S(1)} %get-tuple-element.56), channel_id=1, source_target_pairs={{0,24},{8,16},{16,8},{24,0},{1,25},{9,17},{17,9},{25,1},{2,26},{10... | collective-permute-start | bytes 110600 | tf_op jit(solution)/shard_map/ppermute | solution.py:580
  10.2 3.4 %collective-permute-start.2 = (bf16[144,128]{1,0:T(8,128)(2,1)S(1)}, bf16[144,128]{1,0:T(8,128)(2,1)S(1)}, u32[]{:S(2)}, u32[]{:S(2)}) collective-permute-start(bf16[144,128]{1,0:T(8,128)(2,1)S(1)} %get-tuple-element.57), channel_id=1, source_target_pairs={{0,8},{8,0},{16,24},{24,16},{1,9},{9,1},{17,25},{25,17},{2,10},{10... | collective-permute-start | bytes 110600 | tf_op jit(solution)/shard_map/ppermute | solution.py:581

commit v17 on v16

--- a/solution.py
+++ b/solution.py
@@ -490,16 +490,22 @@
     copies = []
     copies.append(pltpu.make_async_copy(atom_result_ref, atom_result_hbm, sems.at[1]))
     copies[-1].start()
-    bond_out = packed + jnp.dot(
-        total.astype(BF16), out_weight_ref[...], preferred_element_type=F32
-    )
-    bond_out = bond_out.astype(BF16)
-    for k in range(slots // 2):
-        bond_result_ref[0, 0, :, k * width : (k + 1) * width] = bond_out[
-            k * atoms : (k + 1) * atoms
-        ]
-    copies.append(pltpu.make_async_copy(bond_result_ref, bond_result_hbm, sems.at[0]))
-    copies[-1].start()
+    height = pairs // 2
+    for part in range(2):
+        rows = slice(part * height, (part + 1) * height)
+        bond_out = packed[rows] + jnp.dot(
+            total[rows].astype(BF16), out_weight_ref[...], preferred_element_type=F32
+        )
+        bond_out = bond_out.astype(BF16)
+        first = part * height // atoms
+        count = height // atoms
+        for k in range(count):
+            place = (first + k) * width
+            bond_result_ref[0, 0, :, place : place + width] = bond_out[k * atoms : (k + 1) * atoms]
+        columns = pl.ds(first * width, count * width)
+        source, target = (x.at[0, 0, :, columns] for x in (bond_result_ref, bond_result_hbm))
+        copies.append(pltpu.make_async_copy(source, target, sems.at[2 * part]))
+        copies[-1].start()
     for copy in copies:
         copy.wait()
 
@@ -613,7 +619,7 @@
             pltpu.VMEM((pairs, 4 * feature), F32),
             pltpu.VMEM((2, pairs, 4 * feature), F32),
             pltpu.VMEM((slots * pairs, 2 * feature), BF16),
-            pltpu.SemaphoreType.DMA((2,)),
+            pltpu.SemaphoreType.DMA((3,)),
         ],
         compiler_params=params,
         name="main",

time: 17 us -> 17 us (level)
  no operation moved by 1% of the time
where the time goes in v17:
time: 17 us; the launch traced here: 16.8 us
  starting transfers between devices  7.96 us (47%)
  Pallas kernels  7.05 us (41%)
  waiting for transfers between devices  1.06 us (6%)
  between operations  0.67 us (4%)
    pallas_call x1, Pallas kernels, per_device(): pl.pallas_call(main_kernel, out_shape=(shaped(atom_feat.shape, BF16), sha...  3.22 us
    ppermute x1, starting transfers between devices, per_device(): down = lax.ppermute(down, 'gy', second)  3.1 us
    ppermute x1, starting transfers between devices, per_device(): up = lax.ppermute(up, 'gy', first)  3.02 us
    pallas_call x1, Pallas kernels, per_device(): pl.pallas_call(functools.partial(angular_kernel, atoms), out_shape=(shape...  1.67 us
    ppermute x1, starting transfers between devices, per_device(): two = lax.ppermute(forwarded(2), 'gx', second)  1.6 us
    pallas_call x1, Pallas kernels, per_device(): pl.pallas_call(functools.partial(pack_kernel, extents, paired), out_shape...  1.32 us
    ppermute x1, waiting for transfers between devices, per_device(): up = lax.ppermute(up, 'gy', first)  0.95 us
    pallas_call x1, Pallas kernels, per_device(): pl.pallas_call(functools.partial(prepare_kernel, extents, paired), out_sh...  0.83 us
  transfers between devices with their start and end apart: 4, of which 2 were waited for; matrix products, arithmetic and copies ran while one was open for 0% of the time, Pallas kernels for 15%

profile of v17, /device:TPU:0, one launch (start us, length us, event | category | flops | bytes accessed | tf_op | source)
XLA Modules:
  0.0 16.8 jit_solution(9646737275789927632)
XLA Ops:
  0.6 1.3 %pack.1 = (bf16[112,128]{1,0:T(8,128)(2,1)S(1)}, bf16[112,128]{1,0:T(8,128)(2,1)S(1)}, s32[1,512]{1,0:T(1,128)S(1)}, s32[16,32]{1,0:T(8,128)S(1)}, bf16[1,1,32,6...) custom-call(s32[16,32]{1,0:T(8,128)} %bitcast.3, bf16[1,1,32,64]{3,2,1,0:T(8,128)(2,1)} %atom_hbm.1, ...), custom_call_target="tpu_custom_call" | custom-call | tf_op jit(solution)/shard_map/pack/pallas_call | solution.py:547
  2.0 3.0 %collective-permute-start = (bf16[112,128]{1,0:T(8,128)(2,1)S(1)}, bf16[112,128]{1,0:T(8,128)(2,1)S(1)}, u32[]{:S(2)}, u32[]{:S(2)}) collective-permute-start(bf16[112,128]{1,0:T(8,128)(2,1)S(1)} %get-tuple-element.34), channel_id=1, source_target_pairs={{0,1},{1,2},{2,3},{3,4},{4,5},{5,6},{6,7},{7,0},{8,9},{9,10},{10,1... | collective-permute-start | bytes 86024 | tf_op jit(solution)/shard_map/ppermute | solution.py:558
  5.0 3.1 %collective-permute-start.1 = (bf16[112,128]{1,0:T(8,128)(2,1)S(1)}, bf16[112,128]{1,0:T(8,128)(2,1)S(1)}, u32[]{:S(2)}, u32[]{:S(2)}) collective-permute-start(bf16[112,128]{1,0:T(8,128)(2,1)S(1)} %get-tuple-element.35), channel_id=1, source_target_pairs={{1,0},{2,1},{3,2},{4,3},{5,4},{6,5},{7,6},{0,7},{9,8},{10,9},{11,1... | collective-permute-start | bytes 86024 | tf_op jit(solution)/shard_map/ppermute | solution.py:559
  8.1 0.8 %prepare.1 = (bf16[112,128]{1,0:T(8,128)(2,1)S(1)}, bf16[512,432]{1,0:T(8,128)(2,1)S(1)}, f32[512,128]{1,0:T(8,128)S(1)}, bf16[512,128]{1,0:T(8,128)(2,1)S(1)}, ...) custom-call(s32[1,512]{1,0:T(1,128)S(1)} %get-tuple-element.29.spot_ref, ...), custom_call_target="tpu_custom_call" | custom-call | flops 67108864 | bytes 2097152 | tf_op jit(solution)/shard_map/prepare/pallas_call | solution.py:562
  8.9 0.9 %collective-permute-done.up_ref = bf16[112,128]{1,0:T(8,128)(2,1)S(1)} collective-permute-done((bf16[112,128]{1,0:T(8,128)(2,1)S(1)}, bf16[112,128]{1,0:T(8,128)(2,1)S(1)}, u32[]{:S(2)}, u32[]{:S(2)}) %collective-permute-start) | collective-permute-done | bytes 28704 | tf_op jit(solution)/shard_map/ppermute | solution.py:558
  9.9 0.0 collective-permute-done.1.down_ref
  9.9 0.2 %collective-permute-start.3 = (bf16[144,128]{1,0:T(8,128)(2,1)S(1)}, bf16[144,128]{1,0:T(8,128)(2,1)S(1)}, u32[]{:S(2)}, u32[]{:S(2)}) collective-permute-start(bf16[144,128]{1,0:T(8,128)(2,1)S(1)} %get-tuple-element.56), channel_id=1, source_target_pairs={{0,24},{8,16},{16,8},{24,0},{1,25},{9,17},{17,9},{25,1},{2,26},{10... | collective-permute-start | bytes 110600 | tf_op jit(solution)/shard_map/ppermute | solution.py:586
  10.2 1.6 %collective-permute-start.2 = (bf16[144,128]{1,0:T(8,128)(2,1)S(1)}, bf16[144,128]{1,0:T(8,128)(2,1)S(1)}, u32[]{:S(2)}, u32[]{:S(2)}) collective-permute-start(bf16[144,128]{1,0:T(8,128)(2,1)S(1)} %get-tuple-element.57), channel_id=1, source_target_pairs={{0,8},{8,0},{16,24},{24,16},{1,9},{9,1},{17,25},{25,17},{2,10},{10... | collective-permute-start | bytes 110600 | tf_op jit(solution)/shard_map/ppermute | solution.py:587
  11.8 1.7 %angular.1 = (f32[16,256,256]{2,1,0:T(8,128)S(1)}, bf16[256,256]{1,0:T(8,128)(2,1)S(1)}, bf16[128,128]{1,0:T(8,128)(2,1)S(1)}, bf16[512,512]{1,0:T(8,128)(2,1)S(...) custom-call(f32[2,1,1,512]{3,2,1,0:T(1,128)S(1)} %get-tuple-element., ...), custom_call_target="tpu_custom_call" | custom-call | flops 268435456 | bytes 4194304 | tf_op jit(solution)/shard_map/angular/pallas_call | solution.py:588
  13.5 0.1 collective-permute-done.3.one_ref
  13.6 0.0 collective-permute-done.2.two_ref
  13.6 3.2 %main.1 = (bf16[1,1,32,64]{3,2,1,0:T(8,128)(2,1)}, bf16[1,1,32,1024]{3,2,1,0:T(8,128)(2,1)}) custom-call(bf16[112,128]{1,0:T(8,128)(2,1)S(1)} %get-tuple-element.39.near_ref, bf16[112,128]{1,0:T(8,128)(2,1)S(1)} %collective-permute-done.up_ref, bf16[112,128]{1,0:T(8,128)(2,1)S(1)} %collective-permute-done.1.down_ref, ...), custom_call_target="tpu_custom_call" | custom-call | tf_op jit(solution)/shard_map/main/pallas_call | solution.py:611
  (6 shorter events, 0.0 us)
Async XLA Ops:
  2.0 7.9 %collective-permute-start = (bf16[112,128]{1,0:T(8,128)(2,1)S(1)}, bf16[112,128]{1,0:T(8,128)(2,1)S(1)}, u32[]{:S(2)}, u32[]{:S(2)}) collective-permute-start(bf16[112,128]{1,0:T(8,128)(2,1)S(1)} %get-tuple-element.34), channel_id=1, source_target_pairs={{0,1},{1,2},{2,3},{3,4},{4,5},{5,6},{6,7},{7,0},{8,9},{9,10},{10,1... | collective-permute-start | bytes 86024 | tf_op jit(solution)/shard_map/ppermute | solution.py:558
  5.0 4.9 %collective-permute-start.1 = (bf16[112,128]{1,0:T(8,128)(2,1)S(1)}, bf16[112,128]{1,0:T(8,128)(2,1)S(1)}, u32[]{:S(2)}, u32[]{:S(2)}) collective-permute-start(bf16[112,128]{1,0:T(8,128)(2,1)S(1)} %get-tuple-element.35), channel_id=1, source_target_pairs={{1,0},{2,1},{3,2},{4,3},{5,4},{6,5},{7,6},{0,7},{9,8},{10,9},{11,1... | collective-permute-start | bytes 86024 | tf_op jit(solution)/shard_map/ppermute | solution.py:559
  9.9 3.6 %collective-permute-start.3 = (bf16[144,128]{1,0:T(8,128)(2,1)S(1)}, bf16[144,128]{1,0:T(8,128)(2,1)S(1)}, u32[]{:S(2)}, u32[]{:S(2)}) collective-permute-start(bf16[144,128]{1,0:T(8,128)(2,1)S(1)} %get-tuple-element.56), channel_id=1, source_target_pairs={{0,24},{8,16},{16,8},{24,0},{1,25},{9,17},{17,9},{25,1},{2,26},{10... | collective-permute-start | bytes 110600 | tf_op jit(solution)/shard_map/ppermute | solution.py:586
  10.2 3.4 %collective-permute-start.2 = (bf16[144,128]{1,0:T(8,128)(2,1)S(1)}, bf16[144,128]{1,0:T(8,128)(2,1)S(1)}, u32[]{:S(2)}, u32[]{:S(2)}) collective-permute-start(bf16[144,128]{1,0:T(8,128)(2,1)S(1)} %get-tuple-element.57), channel_id=1, source_target_pairs={{0,8},{8,0},{16,24},{24,16},{1,9},{9,1},{17,25},{25,17},{2,10},{10... | collective-permute-start | bytes 110600 | tf_op jit(solution)/shard_map/ppermute | solution.py:587
